TPU v7x, 32 devices: a whole 2x2x4 slice. The times are simulated.
32 devices in a mesh: space: 8 (over z, y), fsdp: 4 (over x, core).
Axes of the slice: x: 2, y: 2, z: 4, core: 2. Of those that a mesh axis runs over, the one named last changes fastest.
Arguments:
- fields: bfloat16 [16, 64, 64, 200], P('space', 'fsdp'), may hold values from -6 to 6
- weight: bfloat16 [5, 5, 40, 200], P(None, None, None, 'fsdp'), may hold values from -0.1875 to 0.1875
- bias: bfloat16 [200], P('fsdp'), may hold values from -3 to 3
- cotangent: bfloat16 [16, 64, 64, 200], P('space', 'fsdp'), may hold values from -9 to 9
- neighbours: int32 [16, 8], P('space'), may hold values from -1 to 15, as said below
Outputs:
- activations: bfloat16 [16, 64, 64, 200], P('space', 'fsdp')
- weight_step: float32 [5, 5, 40, 200], P(None, None, None, 'fsdp')
- bias_step: float32 [200], P('fsdp')
Inputs may be any that keep to these rules, and one draw needn't show every extreme that they name: The tiles are the ocean tiles of a region 4 tiles tall, numbered column by column from west to east and north to south within a column, land tiles skipped; neighbours[t, k] is the tile beside t in direction k, or -1 where that place is land or outside the region; every neighbour differs from t by at most 5.
All inputs are finite; a program needn't handle non-finite values.
Results may differ from a plain program's by a relative error of at most 0.0034.
Values may be sent and summed in bfloat16 or wider, within the bound.
No kernel may reach another device: no remote copies, remote signals or barrier semaphores. Data moves between devices by JAX's collectives and lax.ppermute only.
A program may use at most 64 MiB of HBM per device.

v0:
```python
import functools

import jax
import jax.numpy as jnp
from jax import lax
from jax.experimental import pallas as pl
from jax.experimental.pallas import tpu as pltpu
from jax.sharding import PartitionSpec as P

GROUP = 40
KS = 5
RIM = 2
LANES = 256
HALF = 64
HALF_TAPS = 13
PIECE_ROWS = 528
SUM_LANES = 1024
XROWS = 208
VMEM = pl.BlockSpec(memory_space=pltpu.VMEM)
SMEM = pl.BlockSpec(memory_space=pltpu.SMEM)
F32 = jnp.float32
BF16 = jnp.bfloat16


def swapped(value, axis, partner):
    count = lax.axis_size(axis)
    pairs = [(i, partner(i)) for i in range(count)]
    return lax.ppermute(value, axis, [p for p in pairs if 0 <= p[1] < count])


def hop_pairs(value, distance, parity):
    def partner(i):
        return i + distance if (i // distance) % 2 == parity else i - distance

    return swapped(value, "space", partner)


def main_kernel(
    piece_count, near, fields, cot, above, below, far0, far1, close0, close1, edge0, edge1, *rest
):
    pieces = rest[:piece_count]
    act, keep, send = rest[piece_count : piece_count + 3]
    pool_l, pool_r, xf, xs, xst, wc, wd, g, gd, shares = rest[piece_count + 3 :]
    tiles, rows, side, chans = fields.shape
    tall = rows + 2 * RIM
    cells = tiles * side
    fsdp_count = lax.axis_size("fsdp")
    fsdp = lax.axis_index("fsdp")
    space = lax.axis_index("space")
    far_odd = lax.rem(lax.div(space, 2), 2) == 1
    close_odd = lax.rem(space, 2) == 1
    share = chans // fsdp_count

    zero_side = jnp.zeros((tall, RIM, LANES), F32)
    zero_slot = 4 * tiles
    pool_l[zero_slot] = zero_side
    pool_r[zero_slot] = zero_side
    for t in range(tiles):
        lo, hi = far0[t].astype(F32), far1[t].astype(F32)
        pool_l[tiles + t, :, :, :chans] = jnp.where(far_odd, lo, hi)
        pool_r[2 * tiles + t, :, :, :chans] = jnp.where(far_odd, hi, lo)
        lo = close0[t * tall : (t + 1) * tall].astype(F32)
        hi = close1[t * tall : (t + 1) * tall].astype(F32)
        pool_l[2 * tiles + t, :, :, :chans] = jnp.where(close_odd, lo, hi)
        pool_r[tiles + t, :, :, :chans] = jnp.where(close_odd, hi, lo)
    lo = close0[tiles * tall :].astype(F32)
    hi = close1[tiles * tall :].astype(F32)
    pool_l[tiles - 1, :RIM, :, :chans] = jnp.where(close_odd, lo, hi)
    pool_r[3 * tiles, rows + RIM :, :, :chans] = jnp.where(close_odd, hi, lo)
    lo, hi = edge0[...].astype(F32), edge1[...].astype(F32)
    edge_north = jnp.where(close_odd, lo, hi)
    edge_south = jnp.where(close_odd, hi, lo)

    lane = lax.broadcasted_iota(jnp.int32, (tiles, side + 16, 128), 2)
    one_behind = jnp.where(lane == chans - 128, 1.0, 0.0).astype(F32)
    for r in range(tall):
        xf[r, :, :, 128:] = one_behind
    for t in range(tiles):
        top, bottom = above[t].astype(F32), below[t].astype(F32)
        centre = fields[t].astype(F32)
        for part, first in ((top, 0), (centre, RIM), (bottom, RIM + rows)):
            length = part.shape[0]
            pool_l[3 * tiles + t, first : first + length, :, :chans] = part[:, side - RIM :]
            pool_r[t, first : first + length, :, :chans] = part[:, :RIM]
        xf[RIM : RIM + rows, t, 8 : 8 + side, :chans] = centre
        north = edge_north if t == 0 else above[t - 1].astype(F32)
        south = edge_south if t == tiles - 1 else below[t + 1].astype(F32)
        north = jnp.where(near[t, 0] >= 0, north, 0.0)
        south = jnp.where(near[t, 1] >= 0, south, 0.0)
        xf[:RIM, t, 8 : 8 + side, :chans] = jnp.where(fsdp == 0, north, top)
        xf[RIM + rows :, t, 8 : 8 + side, :chans] = jnp.where(fsdp == fsdp_count - 1, south, bottom)

    def slot(tile_id, first):
        return jnp.where(tile_id < 0, zero_slot, jnp.clip(tile_id - first * tiles, 0, zero_slot))

    for t in range(tiles):
        for pool, column, first, beside, up, down in (
            (pool_l, 6, space - 3, near[t, 2], near[t, 4], near[t, 6]),
            (pool_r, 8 + side, space, near[t, 3], near[t, 5], near[t, 7]),
        ):
            mid = slot(beside, first)
            top = jnp.where(fsdp == 0, slot(up, first), mid)
            bottom = jnp.where(fsdp == fsdp_count - 1, slot(down, first), mid)
            into = pl.ds(column, RIM)
            xf[RIM : RIM + rows, t, into, :chans] = pool[mid, RIM : RIM + rows, :, :chans]
            xf[:RIM, t, into, :chans] = pool[top, :RIM, :, :chans]
            xf[RIM + rows :, t, into, :chans] = pool[bottom, RIM + rows :, :, :chans]

    lined = jnp.concatenate([p[...] for p in pieces], axis=1)
    owner = []
    for i in range(piece_count):
        if piece_count == fsdp_count and fsdp_count != 4:
            owner.append(i)
        else:
            owner.append((fsdp, 3 - fsdp, fsdp ^ 1, 3 - (fsdp ^ 1))[i])
    from_lane = lax.broadcasted_iota(jnp.int32, (128, LANES), 0)
    to_lane = lax.broadcasted_iota(jnp.int32, (128, LANES), 1)
    for half in range(2):
        picks = []
        for i in range(piece_count):
            inside = from_lane - half * HALF
            valid = (inside >= 0) & (inside < share) & (to_lane == owner[i] * share + inside)
            picks.append(jnp.where(valid, 1.0, 0.0).astype(BF16))
        full = jnp.dot(lined, jnp.concatenate(picks, axis=0), preferred_element_type=F32)
        wc[half * HALF_TAPS * GROUP : (half + 1) * HALF_TAPS * GROUP, :] = full[: HALF_TAPS * GROUP]
    group_count = chans // GROUP
    group_of = lax.broadcasted_iota(jnp.int32, (GROUP, LANES), 1) // GROUP
    taps = KS * KS
    for tap in range(taps):
        one = wc[tap * GROUP : (tap + 1) * GROUP]
        blocks = [jnp.where(group_of == k, one, 0.0) for k in range(group_count)]
        if tap == taps // 2:
            blocks.append(wc[taps * GROUP : taps * GROUP + 8])
        else:
            blocks.append(jnp.zeros((8, LANES), F32))
        blocks.append(jnp.zeros((LANES - chans - 8, LANES), F32))
        wd[tap * LANES : (tap + 1) * LANES] = jnp.concatenate(blocks, axis=0).astype(BF16)

    @pl.loop(0, tall)
    def _(r):
        for b in range(KS):
            piece = xf[r, :, 6 + b : 6 + b + side, :].astype(BF16).reshape(cells, LANES)
            xs[r, :, b * LANES : (b + 1) * LANES] = piece
            xst[r, b * XROWS : (b + 1) * XROWS, :] = piece.T[:XROWS]

    step = min(8, rows)
    for r0 in range(0, rows, step):
        total = None
        for a in range(KS):
            left = xs[r0 + a : r0 + a + step].reshape(step * cells, KS * LANES)
            right = wd[a * KS * LANES : (a + 1) * KS * LANES]
            part = jnp.dot(left, right, preferred_element_type=F32)
            total = part if total is None else total + part
        total = total.reshape(step, tiles, side, LANES)
        for t in range(tiles):
            pre = total[:, t, :, :chans]
            logistic = 1.0 / (1.0 + jnp.exp(-pre))
            act[t, r0 : r0 + step] = (pre * logistic).astype(BF16)
            up = cot[t, r0 : r0 + step].astype(F32)
            g[r0 : r0 + step, t * side : (t + 1) * side, :chans] = (
                up * logistic * (1.0 + pre * (1.0 - logistic))
            ).astype(BF16)

    right = g[...].reshape(rows * cells, LANES)
    for a in range(KS):
        left = jnp.concatenate([xst[r + a] for r in range(rows)], axis=1)
        part = jnp.dot(left, right, preferred_element_type=F32)
        for b in range(KS):
            fold = jnp.zeros((GROUP, LANES), F32)
            for k in range(group_count):
                first = b * XROWS + k * GROUP
                fold = jnp.where(group_of == k, part[first : first + GROUP], fold)
            first = (a * KS + b) * GROUP
            gd[first : first + GROUP] = fold
        if a == 0:
            gd[taps * GROUP : taps * GROUP + 8] = part[chans : chans + 8]
            gd[taps * GROUP + 8 :] = jnp.zeros((SUM_LANES - taps * GROUP - 8, LANES), F32)
    turned = gd[...].T
    for i in range(fsdp_count):
        shares[i] = turned[i * share : (i + 1) * share]
    for i in range(fsdp_count // 2):
        keep[i] = shares[fsdp ^ (2 * i)]
        send[i] = shares[fsdp ^ (2 * i + 1)]


def finish_kernel(entries, own, first, second, third, weight_out, bias_out, squares_out):
    del entries
    total = (own[...].astype(F32) + first[...].astype(F32)) + (
        second[...].astype(F32) + third[...].astype(F32)
    )
    count = KS * KS * GROUP
    lane = lax.broadcasted_iota(jnp.int32, total.shape, 1)
    exact = total[:, count : count + 1] + total[:, count + 1 : count + 2]
    total = jnp.where(lane < count, total, jnp.where(lane == count, exact, 0.0))
    squares_out[...] = jnp.full((8, 128), jnp.sum(total * total), F32)
    share = total.shape[0]
    padded = jnp.concatenate([total, jnp.zeros((128 - share, total.shape[1]), F32)], axis=0)
    turned = padded.T
    weight_out[...] = turned[:count, :share].reshape(weight_out.shape)
    bias_out[...] = turned[count : count + 1, :share]


def per_device(fields, weight, bias, cotangent, neighbours):
    tiles, rows, side, chans = fields.shape
    fsdp_count = lax.axis_size("fsdp")
    space_count = lax.axis_size("space")
    fsdp = lax.axis_index("fsdp")
    space = lax.axis_index("space")
    share = chans // fsdp_count
    taps = KS * KS
    tall = rows + 2 * RIM

    flat = weight.reshape(taps * GROUP, share)
    low = flat[: HALF_TAPS * GROUP]
    high = jnp.concatenate([flat[HALF_TAPS * GROUP :], bias[None, :]], axis=0)
    low = jnp.pad(low, ((0, PIECE_ROWS - low.shape[0]), (0, HALF - share)))
    high = jnp.pad(high, ((0, PIECE_ROWS - high.shape[0]), (0, HALF - share)))
    packed = jnp.concatenate([low, high], axis=1)

    even = fsdp % 2 == 0
    first_rows, last_rows = fields[:, :RIM], fields[:, rows - RIM :]

    def outward(i):
        return (i + 1) % fsdp_count if i % 2 else (i - 1) % fsdp_count

    from_outward = swapped(jnp.where(even, first_rows, last_rows), "fsdp", outward)
    from_core = swapped(jnp.where(even, last_rows, first_rows), "fsdp", lambda i: i ^ 1)
    above = jnp.where(even, from_outward, from_core)
    below = jnp.where(even, from_core, from_outward)
    if fsdp_count == 4:
        packed_out = swapped(packed, "fsdp", outward)
        pieces = [
            packed,
            packed_out,
            swapped(packed, "fsdp", lambda i: i ^ 1),
            swapped(packed_out, "fsdp", lambda i: i ^ 1),
        ]
    else:
        gathered = lax.all_gather(packed, "fsdp")
        pieces = [gathered[i] for i in range(fsdp_count)]

    tall_rows = jnp.concatenate([above, fields, below], 1)
    west, east = tall_rows[:, :, :RIM], tall_rows[:, :, side - RIM :]
    far_odd = (space // 2) % 2 == 1
    close_odd = space % 2 == 1
    far0 = hop_pairs(jnp.where(far_odd, west, east), 2, 0)
    far1 = hop_pairs(jnp.where(far_odd, east, west), 2, 1)
    east_far = jnp.where(far_odd, far0, far1)[tiles - 1, :RIM]
    west_far = jnp.where(far_odd, far1, far0)[0, rows + RIM :]
    flat_side = (tiles * tall, RIM, chans)
    to_east = jnp.concatenate([east.reshape(flat_side), east_far], 0)
    to_west = jnp.concatenate([west.reshape(flat_side), west_far], 0)
    close0 = hop_pairs(jnp.where(close_odd, to_west, to_east), 1, 0)
    close1 = hop_pairs(jnp.where(close_odd, to_east, to_west), 1, 1)
    edge0 = hop_pairs(jnp.where(close_odd, below[0], above[tiles - 1]), 1, 0)
    edge1 = hop_pairs(jnp.where(close_odd, above[tiles - 1], below[0]), 1, 1)

    cells = tiles * side
    part = jax.ShapeDtypeStruct((fsdp_count // 2, share, SUM_LANES), F32)
    activations, keep, send = pl.pallas_call(
        functools.partial(main_kernel, len(pieces)),
        out_shape=(jax.ShapeDtypeStruct(fields.shape, BF16), part, part),
        in_specs=[SMEM] + [VMEM] * (10 + len(pieces)),
        out_specs=(VMEM, VMEM, VMEM),
        scratch_shapes=[
            pltpu.VMEM((4 * tiles + 1, tall, RIM, LANES), F32),
            pltpu.VMEM((4 * tiles + 1, tall, RIM, LANES), F32),
            pltpu.VMEM((tall, tiles, side + 16, LANES), F32),
            pltpu.VMEM((tall, cells, KS * LANES), BF16),
            pltpu.VMEM((tall, KS * XROWS, cells), BF16),
            pltpu.VMEM((2 * HALF_TAPS * GROUP, LANES), F32),
            pltpu.VMEM((taps * LANES, LANES), BF16),
            pltpu.VMEM((rows, cells, LANES), BF16),
            pltpu.VMEM((SUM_LANES, LANES), F32),
            pltpu.VMEM((fsdp_count, share, SUM_LANES), F32),
        ],
        compiler_params=pltpu.CompilerParams(vmem_limit_bytes=52 * 1024 * 1024),
        name="section",
    )(
        neighbours, fields, cotangent, above, below,
        far0, far1, close0, close1, edge0, edge1, *pieces,
    )

    held = keep + swapped(send, "fsdp", lambda i: i ^ 1)
    distance = 2
    while held.shape[0] > 1:
        pairs = held.reshape(held.shape[0] // 2, 2, share, SUM_LANES)
        held = pairs[:, 0] + swapped(pairs[:, 1], "fsdp", lambda i: i ^ distance)
        distance *= 2
    held = held[0]
    distance = 1
    while distance * 4 < space_count:
        held = held + swapped(held, "space", lambda i: i ^ distance)
        distance *= 2
    count = taps * GROUP
    lane = lax.broadcasted_iota(jnp.int32, held.shape, 1)
    bias_sum = held[:, count : count + 1]
    bias_low = bias_sum - lax.reduce_precision(bias_sum, 8, 7)
    rounded = jnp.where(lane == count + 1, bias_low, held).astype(BF16)
    others = [swapped(rounded, "space", lambda i, k=k: i ^ (distance * k)) for k in (1, 2, 3)]
    entries = count * chans + chans
    weight_sum, bias_sum, squares = pl.pallas_call(
        functools.partial(finish_kernel, entries),
        out_shape=(
            jax.ShapeDtypeStruct((KS, KS, GROUP, share), F32),
            jax.ShapeDtypeStruct((1, share), F32),
            jax.ShapeDtypeStruct((8, 128), F32),
        ),
        in_specs=[VMEM] * 4,
        out_specs=(VMEM, VMEM, VMEM),
        name="finish",
    )(rounded, *others)
    distance = 1
    while distance < fsdp_count:
        squares = squares + swapped(squares, "fsdp", lambda i: i ^ distance)
        distance *= 2
    scaling = lax.rsqrt(squares[0, 0] / entries + 1e-06)
    return (activations, weight_sum * scaling, bias_sum[0] * scaling)


def solution(mesh):
    return jax.shard_map(
        per_device,
        mesh=mesh,
        in_specs=(
            P("space", "fsdp", None, None),
            P(None, None, None, "fsdp"),
            P("fsdp"),
            P("space", "fsdp", None, None),
            P("space", None),
        ),
        out_specs=(P("space", "fsdp", None, None), P(None, None, None, "fsdp"), P("fsdp")),
        check_vma=False,
    )
```

profile of v0, /device:TPU:0, one launch (start us, length us, event | category | flops | bytes accessed | tf_op | source)
XLA Modules:
  0.0 87.3 jit_solution(11987182260458535726)
XLA Ops:
  0.7 1.1 %broadcast_select_fusion.2 = (bf16[2,2,64,200]{3,2,1,0:T(8,128)(2,1)S(1)}, bf16[2,2,64,200]{3,2,1,0:T(8,128)(2,1)S(1)}) fusion(pred[]{:T(512)S(6)} %eq.20, bf16[2,16,64,200]{3,2,1,0:T(8,128)(2,1)} %fields.1), kind=kLoop, calls=%fused_computation.20 | loop fusion | flops 102400 | bytes 409601 | tf_op jit(solution)/shard_map/jit(_where)/select_n | solution.py:227
  1.8 2.4 %collective-permute-start = (bf16[2,2,64,200]{3,2,1,0:T(8,128)(2,1)S(1)}, bf16[2,2,64,200]{3,2,1,0:T(8,128)(2,1)S(1)}, u32[]{:S(2)}, u32[]{:S(2)}) collective-permute-start(bf16[2,2,64,200]{3,2,1,0:T(8,128)(2,1)S(1)} %get-tuple-element.19), channel_id=1, source_target_pairs={{0,3},{1,2},{2,1},{3,0},{4,7},{5,6},{6,5},{7,4},{8,11},{9,10},{10,... | collective-permute-start | bytes 307208 | tf_op jit(solution)/shard_map/ppermute | solution.py:28
  4.2 0.7 collective-permute-start.1
  5.3 2.8 %collective-permute-done = bf16[2,2,64,200]{3,2,1,0:T(8,128)(2,1)S(1)} collective-permute-done((bf16[2,2,64,200]{3,2,1,0:T(8,128)(2,1)S(1)}, bf16[2,2,64,200]{3,2,1,0:T(8,128)(2,1)S(1)}, u32[]{:S(2)}, u32[]{:S(2)}) %collective-permute-start) | collective-permute-done | bytes 102432 | tf_op jit(solution)/shard_map/ppermute | solution.py:28
  8.3 2.6 %collective-permute-start.2 = (bf16[2,20,2,200]{3,2,1,0:T(2,128)(2,1)S(1)}, bf16[2,20,2,200]{3,2,1,0:T(2,128)(2,1)S(1)}, u32[]{:S(2)}, u32[]{:S(2)}) collective-permute-start(bf16[2,20,2,200]{3,2,1,0:T(2,128)(2,1)S(1)} %bitcast.36), channel_id=1, source_target_pairs={{0,8},{4,12},{8,0},{12,4},{16,24},{20,28},{24,16},{28,20},{1,9},{5... | collective-permute-start | bytes 96008 | tf_op jit(solution)/shard_map/ppermute | solution.py:28
  11.5 1.6 %collective-permute-start.6 = (bf16[2,64,200]{2,1,0:T(8,128)(2,1)S(1)}, bf16[2,64,200]{2,1,0:T(8,128)(2,1)S(1)}, u32[]{:S(2)}, u32[]{:S(2)}) collective-permute-start(bf16[2,64,200]{2,1,0:T(8,128)(2,1)S(1)} %get-tuple-element.21), channel_id=1, source_target_pairs={{0,4},{4,0},{8,12},{12,8},{16,20},{20,16},{24,28},{28,24},{1,5},{5... | collective-permute-start | bytes 153608 | tf_op jit(solution)/shard_map/ppermute | solution.py:28
  14.1 7.2 %collective-permute-start.4 = (bf16[42,2,200]{2,1,0:T(2,128)(2,1)S(1)}, bf16[42,2,200]{2,1,0:T(2,128)(2,1)S(1)}, u32[]{:S(2)}, u32[]{:S(2)}) collective-permute-start(bf16[42,2,200]{2,1,0:T(2,128)(2,1)S(1)} %get-tuple-element.25), channel_id=1, source_target_pairs={{0,4},{4,0},{8,12},{12,8},{16,20},{20,16},{24,28},{28,24},{1,5},{5... | collective-permute-start | bytes 100808 | tf_op jit(solution)/shard_map/ppermute | solution.py:28
  21.9 1.6 %collective-permute-done.4.close0 = bf16[42,2,200]{2,1,0:T(2,128)(2,1)S(1)} collective-permute-done((bf16[42,2,200]{2,1,0:T(2,128)(2,1)S(1)}, bf16[42,2,200]{2,1,0:T(2,128)(2,1)S(1)}, u32[]{:S(2)}, u32[]{:S(2)}) %collective-permute-start.4) | collective-permute-done | bytes 33632 | tf_op jit(solution)/shard_map/ppermute | solution.py:28
  23.5 18.6 %section.1 = (bf16[2,16,64,200]{3,2,1,0:T(8,128)(2,1)}, f32[2,50,1024]{2,1,0:T(8,128)S(1)}, f32[2,50,1024]{2,1,0:T(8,128)S(1)}) custom-call(s32[2,8]{1,0:T(2,128)S(1)} %copy-done, bf16[2,16,64,200]{3,2,1,0:T(8,128)(2,1)} %fields.1, bf16[2,16,64,200]{3,2,1,0:T(8,128)(2,1)} %cot.1, bf16[2,2,64,200]{3,2,1,0:T(8,128)(2,1)S(1)} %get-tuple-element.23.above, ...), custom_call_target="tpu_custom_call" | custom-call | tf_op jit(solution)/shard_map/section/pallas_call | solution.py:260
  42.2 1.8 %collective-permute-done.11 = f32[2,50,1024]{2,1,0:T(8,128)S(1)} collective-permute-done((f32[2,50,1024]{2,1,0:T(8,128)S(1)}, f32[2,50,1024]{2,1,0:T(8,128)S(1)}, u32[]{:S(2)}, u32[]{:S(2)}) %collective-permute-start.11) | collective-permute-done | bytes 409632 | tf_op jit(solution)/shard_map/ppermute | solution.py:28
  44.1 1.6 %collective-permute-start.12 = (f32[1,50,1024]{2,1,0:T(8,128)S(1)}, f32[1,50,1024]{2,1,0:T(8,128)S(1)}, u32[]{:S(2)}, u32[]{:S(2)}) collective-permute-start(f32[1,50,1024]{2,1,0:T(8,128)S(1)} %slice_bitcast_fusion), channel_id=1, source_target_pairs={{0,2},{1,3},{2,0},{3,1},{4,6},{5,7},{6,4},{7,5},{8,10},{9,11},{10,... | collective-permute-start | bytes 614408 | tf_op jit(solution)/shard_map/ppermute | solution.py:28
  45.7 6.1 %collective-permute-done.12 = f32[1,50,1024]{2,1,0:T(8,128)S(1)} collective-permute-done((f32[1,50,1024]{2,1,0:T(8,128)S(1)}, f32[1,50,1024]{2,1,0:T(8,128)S(1)}, u32[]{:S(2)}, u32[]{:S(2)}) %collective-permute-start.12) | collective-permute-done | bytes 204832 | tf_op jit(solution)/shard_map/ppermute | solution.py:28
  51.8 4.6 %collective-permute-start.13 = (f32[50,1024]{1,0:T(8,128)S(1)}, f32[50,1024]{1,0:T(8,128)S(1)}, u32[]{:S(2)}, u32[]{:S(2)}) collective-permute-start(f32[50,1024]{1,0:T(8,128)S(1)} %fusion.5), channel_id=1, source_target_pairs={{0,4},{4,0},{8,12},{12,8},{16,20},{20,16},{24,28},{28,24},{1,5},{5... | collective-permute-start | bytes 614408 | tf_op jit(solution)/shard_map/ppermute | solution.py:28
  56.4 5.1 %collective-permute-done.13 = f32[50,1024]{1,0:T(8,128)S(1)} collective-permute-done((f32[50,1024]{1,0:T(8,128)S(1)}, f32[50,1024]{1,0:T(8,128)S(1)}, u32[]{:S(2)}, u32[]{:S(2)}) %collective-permute-start.13) | collective-permute-done | bytes 204832 | tf_op jit(solution)/shard_map/ppermute | solution.py:28
  61.8 1.8 %collective-permute-start.14 = (bf16[50,1024]{1,0:T(8,128)(2,1)S(1)}, bf16[50,1024]{1,0:T(8,128)(2,1)S(1)}, u32[]{:S(2)}, u32[]{:S(2)}) collective-permute-start(bf16[50,1024]{1,0:T(8,128)(2,1)S(1)} %select_convert_fusion.own), channel_id=1, source_target_pairs={{0,8},{4,12},{8,0},{12,4},{16,24},{20,28},{24,16},{28,20},{1,9},{5... | collective-permute-start | bytes 307208 | tf_op jit(solution)/shard_map/ppermute | solution.py:28
  64.1 2.2 %collective-permute-start.16 = (bf16[50,1024]{1,0:T(8,128)(2,1)S(1)}, bf16[50,1024]{1,0:T(8,128)(2,1)S(1)}, u32[]{:S(2)}, u32[]{:S(2)}) collective-permute-start(bf16[50,1024]{1,0:T(8,128)(2,1)S(1)} %select_convert_fusion.own), channel_id=1, source_target_pairs={{0,24},{4,28},{8,16},{12,20},{16,8},{20,12},{24,0},{28,4},{1,25},{... | collective-permute-start | bytes 307208 | tf_op jit(solution)/shard_map/ppermute | solution.py:28
  66.3 0.8 collective-permute-done.14.first
  67.1 6.7 %collective-permute-done.15.second = bf16[50,1024]{1,0:T(8,128)(2,1)S(1)} collective-permute-done((bf16[50,1024]{1,0:T(8,128)(2,1)S(1)}, bf16[50,1024]{1,0:T(8,128)(2,1)S(1)}, u32[]{:S(2)}, u32[]{:S(2)}) %collective-permute-start.15) | collective-permute-done | bytes 102432 | tf_op jit(solution)/shard_map/ppermute | solution.py:28
  75.1 2.2 %finish.1 = (f32[5,5,40,50]{3,2,1,0:T(8,128)}, f32[1,50]{1,0:T(1,128)}, f32[8,128]{1,0:T(8,128)}) custom-call(bf16[50,1024]{1,0:T(8,128)(2,1)} %copy-done.2, bf16[50,1024]{1,0:T(8,128)(2,1)} %copy-done.4, bf16[50,1024]{1,0:T(8,128)(2,1)} %copy-done.5, bf16[50,1024]{1,0:T(8,128)(2,1)} %copy-done.6), custom_call_target="tpu_custom_call" | custom-call | tf_op jit(solution)/shard_map/finish/pallas_call | solution.py:302
  77.3 1.4 %collective-permute-done.17 = f32[8,128]{1,0:T(8,128)S(1)} collective-permute-done((f32[8,128]{1,0:T(8,128)}, f32[8,128]{1,0:T(8,128)S(1)}, u32[]{:S(2)}, u32[]{:S(2)}) %collective-permute-start.17) | collective-permute-done | bytes 4128 | tf_op jit(solution)/shard_map/ppermute | solution.py:28
  78.7 0.7 add.40
  79.4 1.5 %collective-permute-start.18 = (f32[8,128]{1,0:T(8,128)S(1)}, f32[8,128]{1,0:T(8,128)S(1)}, u32[]{:S(2)}, u32[]{:S(2)}) collective-permute-start(f32[8,128]{1,0:T(8,128)S(1)} %add.40), channel_id=1, source_target_pairs={{0,2},{1,3},{2,0},{3,1},{4,6},{5,7},{6,4},{7,5},{8,10},{9,11},{10,... | collective-permute-start | bytes 12296 | tf_op jit(solution)/shard_map/ppermute | solution.py:28
  80.9 2.1 %collective-permute-done.18 = f32[8,128]{1,0:T(8,128)S(1)} collective-permute-done((f32[8,128]{1,0:T(8,128)S(1)}, f32[8,128]{1,0:T(8,128)S(1)}, u32[]{:S(2)}, u32[]{:S(2)}) %collective-permute-start.18) | collective-permute-done | bytes 4128 | tf_op jit(solution)/shard_map/ppermute | solution.py:28
  85.4 1.9 %broadcast_multiply_fusion = f32[5,5,40,50]{3,2,1,0:T(8,128)} fusion(f32[5,5,40,50]{3,2,1,0:T(8,128)} %get-tuple-element.12, f32[]{:T(128)} %bitcast.12), kind=kLoop, calls=%fused_computation.8 | loop fusion | flops 50000 | bytes 400004 | tf_op jit(solution)/shard_map/mul | solution.py:318
  (57 shorter events, 6.7 us)
Async XLA Ops:
  0.6 4.3 %copy-start.7 = (bf16[50]{0:T(256)(128)(2,1)S(1)}, bf16[50]{0:T(256)(128)(2,1)}, u32[]{:S(2)}) copy-start(bf16[50]{0:T(256)(128)(2,1)} %param.7) | copy-start | bytes 304
  0.7 7.5 %copy-start.1 = (bf16[2,16,64,200]{3,2,1,0:T(8,128)(2,1)S(1)}, bf16[2,16,64,200]{3,2,1,0:T(8,128)(2,1)}, u32[]{:S(2)}) copy-start(bf16[2,16,64,200]{3,2,1,0:T(8,128)(2,1)} %fields.1) | copy-start | bytes 2457604
  1.8 6.3 %collective-permute-start = (bf16[2,2,64,200]{3,2,1,0:T(8,128)(2,1)S(1)}, bf16[2,2,64,200]{3,2,1,0:T(8,128)(2,1)S(1)}, u32[]{:S(2)}, u32[]{:S(2)}) collective-permute-start(bf16[2,2,64,200]{3,2,1,0:T(8,128)(2,1)S(1)} %get-tuple-element.19), channel_id=1, source_target_pairs={{0,3},{1,2},{2,1},{3,0},{4,7},{5,6},{6,5},{7,4},{8,11},{9,10},{10,... | collective-permute-start | bytes 307208 | tf_op jit(solution)/shard_map/ppermute | solution.py:28
  4.2 3.9 %collective-permute-start.1 = (bf16[2,2,64,200]{3,2,1,0:T(8,128)(2,1)S(1)}, bf16[2,2,64,200]{3,2,1,0:T(8,128)(2,1)S(1)}, u32[]{:S(2)}, u32[]{:S(2)}) collective-permute-start(bf16[2,2,64,200]{3,2,1,0:T(8,128)(2,1)S(1)} %get-tuple-element.18), channel_id=1, source_target_pairs={{0,1},{1,0},{2,3},{3,2},{4,5},{5,4},{6,7},{7,6},{8,9},{9,8},{10,11... | collective-permute-start | bytes 307208 | tf_op jit(solution)/shard_map/ppermute | solution.py:28
  5.1 8.7 %collective-permute-start.8 = (bf16[528,128]{1,0:T(8,128)(2,1)S(1)}, bf16[528,128]{1,0:T(8,128)(2,1)S(1)}, u32[]{:S(2)}, u32[]{:S(2)}) collective-permute-start(bf16[528,128]{1,0:T(8,128)(2,1)S(1)} %fusion.9.rest_0_), channel_id=1, source_target_pairs={{0,3},{1,2},{2,1},{3,0},{4,7},{5,6},{6,5},{7,4},{8,11},{9,10},{10,... | collective-permute-start | bytes 405512 | tf_op jit(solution)/shard_map/ppermute | solution.py:28
  5.3 16.0 %collective-permute-start.9 = (bf16[528,128]{1,0:T(8,128)(2,1)S(1)}, bf16[528,128]{1,0:T(8,128)(2,1)S(1)}, u32[]{:S(2)}, u32[]{:S(2)}) collective-permute-start(bf16[528,128]{1,0:T(8,128)(2,1)S(1)} %fusion.9.rest_0_), channel_id=1, source_target_pairs={{0,1},{1,0},{2,3},{3,2},{4,5},{5,4},{6,7},{7,6},{8,9},{9,8},{10,11... | collective-permute-start | bytes 405512 | tf_op jit(solution)/shard_map/ppermute | solution.py:28
  8.3 4.8 %collective-permute-start.2 = (bf16[2,20,2,200]{3,2,1,0:T(2,128)(2,1)S(1)}, bf16[2,20,2,200]{3,2,1,0:T(2,128)(2,1)S(1)}, u32[]{:S(2)}, u32[]{:S(2)}) collective-permute-start(bf16[2,20,2,200]{3,2,1,0:T(2,128)(2,1)S(1)} %bitcast.36), channel_id=1, source_target_pairs={{0,8},{4,12},{8,0},{12,4},{16,24},{20,28},{24,16},{28,20},{1,9},{5... | collective-permute-start | bytes 96008 | tf_op jit(solution)/shard_map/ppermute | solution.py:28
  10.8 2.9 %collective-permute-start.3 = (bf16[2,20,2,200]{3,2,1,0:T(2,128)(2,1)S(1)}, bf16[2,20,2,200]{3,2,1,0:T(2,128)(2,1)S(1)}, u32[]{:S(2)}, u32[]{:S(2)}) collective-permute-start(bf16[2,20,2,200]{3,2,1,0:T(2,128)(2,1)S(1)} %get-tuple-element.15), channel_id=1, source_target_pairs={{8,16},{12,20},{16,8},{20,12},{9,17},{13,21},{17,9},{21,13},{10,18... | collective-permute-start | bytes 96008 | tf_op jit(solution)/shard_map/ppermute | solution.py:28
  11.5 10.4 %collective-permute-start.6 = (bf16[2,64,200]{2,1,0:T(8,128)(2,1)S(1)}, bf16[2,64,200]{2,1,0:T(8,128)(2,1)S(1)}, u32[]{:S(2)}, u32[]{:S(2)}) collective-permute-start(bf16[2,64,200]{2,1,0:T(8,128)(2,1)S(1)} %get-tuple-element.21), channel_id=1, source_target_pairs={{0,4},{4,0},{8,12},{12,8},{16,20},{20,16},{24,28},{28,24},{1,5},{5... | collective-permute-start | bytes 153608 | tf_op jit(solution)/shard_map/ppermute | solution.py:28
  13.1 8.8 %collective-permute-start.7 = (bf16[2,64,200]{2,1,0:T(8,128)(2,1)S(1)}, bf16[2,64,200]{2,1,0:T(8,128)(2,1)S(1)}, u32[]{:S(2)}, u32[]{:S(2)}) collective-permute-start(bf16[2,64,200]{2,1,0:T(8,128)(2,1)S(1)} %get-tuple-element.20), channel_id=1, source_target_pairs={{4,8},{8,4},{12,16},{16,12},{20,24},{24,20},{5,9},{9,5},{13,17},{1... | collective-permute-start | bytes 153608 | tf_op jit(solution)/shard_map/ppermute | solution.py:28
  13.8 9.7 %collective-permute-start.10 = (bf16[528,128]{1,0:T(8,128)(2,1)S(1)}, bf16[528,128]{1,0:T(8,128)(2,1)S(1)}, u32[]{:S(2)}, u32[]{:S(2)}) collective-permute-start(bf16[528,128]{1,0:T(8,128)(2,1)S(1)} %collective-permute-done.8.rest_1_), channel_id=1, source_target_pairs={{0,1},{1,0},{2,3},{3,2},{4,5},{5,4},{6,7},{7,6},{8,9},{9,8},{10,11... | collective-permute-start | bytes 405512 | tf_op jit(solution)/shard_map/ppermute | solution.py:28
  14.0 9.5 %copy-start = (s32[2,8]{1,0:T(2,128)S(1)}, s32[2,8]{1,0:T(2,128)}, u32[]{:S(2)}) copy-start(s32[2,8]{1,0:T(2,128)} %near.1) | copy-start | bytes 196
  14.1 9.4 %collective-permute-start.4 = (bf16[42,2,200]{2,1,0:T(2,128)(2,1)S(1)}, bf16[42,2,200]{2,1,0:T(2,128)(2,1)S(1)}, u32[]{:S(2)}, u32[]{:S(2)}) collective-permute-start(bf16[42,2,200]{2,1,0:T(2,128)(2,1)S(1)} %get-tuple-element.25), channel_id=1, source_target_pairs={{0,4},{4,0},{8,12},{12,8},{16,20},{20,16},{24,28},{28,24},{1,5},{5... | collective-permute-start | bytes 100808 | tf_op jit(solution)/shard_map/ppermute | solution.py:28
  21.2 2.3 %collective-permute-start.5 = (bf16[42,2,200]{2,1,0:T(2,128)(2,1)S(1)}, bf16[42,2,200]{2,1,0:T(2,128)(2,1)S(1)}, u32[]{:S(2)}, u32[]{:S(2)}) collective-permute-start(bf16[42,2,200]{2,1,0:T(2,128)(2,1)S(1)} %get-tuple-element.24), channel_id=1, source_target_pairs={{4,8},{8,4},{12,16},{16,12},{20,24},{24,20},{5,9},{9,5},{13,17},{1... | collective-permute-start | bytes 100808 | tf_op jit(solution)/shard_map/ppermute | solution.py:28
  42.1 1.9 %collective-permute-start.11 = (f32[2,50,1024]{2,1,0:T(8,128)S(1)}, f32[2,50,1024]{2,1,0:T(8,128)S(1)}, u32[]{:S(2)}, u32[]{:S(2)}) collective-permute-start(f32[2,50,1024]{2,1,0:T(8,128)S(1)} %get-tuple-element.11), channel_id=1, source_target_pairs={{0,1},{1,0},{2,3},{3,2},{4,5},{5,4},{6,7},{7,6},{8,9},{9,8},{10,11... | collective-permute-start | bytes 1228808 | tf_op jit(solution)/shard_map/ppermute | solution.py:28
  44.1 7.7 %collective-permute-start.12 = (f32[1,50,1024]{2,1,0:T(8,128)S(1)}, f32[1,50,1024]{2,1,0:T(8,128)S(1)}, u32[]{:S(2)}, u32[]{:S(2)}) collective-permute-start(f32[1,50,1024]{2,1,0:T(8,128)S(1)} %slice_bitcast_fusion), channel_id=1, source_target_pairs={{0,2},{1,3},{2,0},{3,1},{4,6},{5,7},{6,4},{7,5},{8,10},{9,11},{10,... | collective-permute-start | bytes 614408 | tf_op jit(solution)/shard_map/ppermute | solution.py:28
  51.8 9.7 %collective-permute-start.13 = (f32[50,1024]{1,0:T(8,128)S(1)}, f32[50,1024]{1,0:T(8,128)S(1)}, u32[]{:S(2)}, u32[]{:S(2)}) collective-permute-start(f32[50,1024]{1,0:T(8,128)S(1)} %fusion.5), channel_id=1, source_target_pairs={{0,4},{4,0},{8,12},{12,8},{16,20},{20,16},{24,28},{28,24},{1,5},{5... | collective-permute-start | bytes 614408 | tf_op jit(solution)/shard_map/ppermute | solution.py:28
  61.8 12.0 %copy-start.2 = (bf16[50,1024]{1,0:T(8,128)(2,1)}, bf16[50,1024]{1,0:T(8,128)(2,1)S(1)}, u32[]{:S(2)}) copy-start(bf16[50,1024]{1,0:T(8,128)(2,1)S(1)} %select_convert_fusion.own) | copy-start | bytes 307204
  61.8 5.3 %collective-permute-start.14 = (bf16[50,1024]{1,0:T(8,128)(2,1)S(1)}, bf16[50,1024]{1,0:T(8,128)(2,1)S(1)}, u32[]{:S(2)}, u32[]{:S(2)}) collective-permute-start(bf16[50,1024]{1,0:T(8,128)(2,1)S(1)} %select_convert_fusion.own), channel_id=1, source_target_pairs={{0,8},{4,12},{8,0},{12,4},{16,24},{20,28},{24,16},{28,20},{1,9},{5... | collective-permute-start | bytes 307208 | tf_op jit(solution)/shard_map/ppermute | solution.py:28
  63.6 10.2 %collective-permute-start.15 = (bf16[50,1024]{1,0:T(8,128)(2,1)S(1)}, bf16[50,1024]{1,0:T(8,128)(2,1)S(1)}, u32[]{:S(2)}, u32[]{:S(2)}) collective-permute-start(bf16[50,1024]{1,0:T(8,128)(2,1)S(1)} %select_convert_fusion.own), channel_id=1, source_target_pairs={{0,16},{4,20},{8,24},{12,28},{16,0},{20,4},{24,8},{28,12},{1,17},{... | collective-permute-start | bytes 307208 | tf_op jit(solution)/shard_map/ppermute | solution.py:28
  64.1 9.7 %collective-permute-start.16 = (bf16[50,1024]{1,0:T(8,128)(2,1)S(1)}, bf16[50,1024]{1,0:T(8,128)(2,1)S(1)}, u32[]{:S(2)}, u32[]{:S(2)}) collective-permute-start(bf16[50,1024]{1,0:T(8,128)(2,1)S(1)} %select_convert_fusion.own), channel_id=1, source_target_pairs={{0,24},{4,28},{8,16},{12,20},{16,8},{20,12},{24,0},{28,4},{1,25},{... | collective-permute-start | bytes 307208 | tf_op jit(solution)/shard_map/ppermute | solution.py:28
  67.1 6.7 %copy-start.4 = (bf16[50,1024]{1,0:T(8,128)(2,1)}, bf16[50,1024]{1,0:T(8,128)(2,1)S(1)}, u32[]{:S(2)}) copy-start(bf16[50,1024]{1,0:T(8,128)(2,1)S(1)} %collective-permute-done.14.first) | copy-start | bytes 307204
  77.3 1.4 %collective-permute-start.17 = (f32[8,128]{1,0:T(8,128)}, f32[8,128]{1,0:T(8,128)S(1)}, u32[]{:S(2)}, u32[]{:S(2)}) collective-permute-start(f32[8,128]{1,0:T(8,128)} %get-tuple-element.13), channel_id=1, source_target_pairs={{0,1},{1,0},{2,3},{3,2},{4,5},{5,4},{6,7},{7,6},{8,9},{9,8},{10,11... | collective-permute-start | bytes 12296 | tf_op jit(solution)/shard_map/ppermute | solution.py:28
  79.4 3.6 %collective-permute-start.18 = (f32[8,128]{1,0:T(8,128)S(1)}, f32[8,128]{1,0:T(8,128)S(1)}, u32[]{:S(2)}, u32[]{:S(2)}) collective-permute-start(f32[8,128]{1,0:T(8,128)S(1)} %add.40), channel_id=1, source_target_pairs={{0,2},{1,3},{2,0},{3,1},{4,6},{5,7},{6,4},{7,5},{8,10},{9,11},{10,... | collective-permute-start | bytes 12296 | tf_op jit(solution)/shard_map/ppermute | solution.py:28
  (4 other events, 6.2 us)
where the time goes:
time: 87.6 us; the launch traced here: 87.3 us
  starting transfers between devices  28.9 us (33%)
  waiting for transfers between devices  28.4 us (32%)
  Pallas kernels  20.8 us (24%)
  other arithmetic  5.01 us (6%)
  local copies, waits for them, and re-layouts  2.57 us (3%)
  between operations  1.62 us (2%)
    ppermute x19, starting transfers between devices, swapped(): return lax.ppermute(value, axis, [p for p in pairs if 0 <= p[1] < count])  28.9 us
    ppermute x19, waiting for transfers between devices, swapped(): return lax.ppermute(value, axis, [p for p in pairs if 0 <= p[1] < count])  28.4 us
    pallas_call x1, Pallas kernels, per_device(): pl.pallas_call(functools.partial(main_kernel, len(pieces)), out_shape=(ja...  18.6 us
    mul x2, other arithmetic, per_device(): return (activations, weight_sum * scaling, bias_sum[0] * scaling)  2.37 us
    pallas_call x1, Pallas kernels, per_device(): pl.pallas_call(functools.partial(finish_kernel, entries), out_shape=(jax....  2.22 us
    unnamed x18, local copies, waits for them, and re-layouts  1.95 us
  transfers between devices with their start and end apart: 19, of which 9 were waited for; matrix products, arithmetic and copies ran while one was open for 1% of the time, Pallas kernels for 0%

commit v1 on v0

--- a/solution.py
+++ b/solution.py
@@ -15,6 +15,8 @@
 HALF_TAPS = 13
 PIECE_ROWS = 528
 SUM_LANES = 1024
+HALF_SUM = SUM_LANES // 2
+BIAS_AT = KS * KS * GROUP - HALF_SUM
 XROWS = 208
 VMEM = pl.BlockSpec(memory_space=pltpu.VMEM)
 SMEM = pl.BlockSpec(memory_space=pltpu.SMEM)
@@ -36,11 +38,11 @@
 
 
 def main_kernel(
-    piece_count, near, fields, cot, above, below, far0, far1, close0, close1, edge0, edge1, *rest
+    piece_count, near, fields, cot, above, below, far0, far1, close0, close1, *rest
 ):
     pieces = rest[:piece_count]
     act, keep, send = rest[piece_count : piece_count + 3]
-    pool_l, pool_r, xf, xs, xst, wc, wd, g, gd, shares = rest[piece_count + 3 :]
+    pool_l, pool_r, edges, xf, xs, xst, wc, wd, g, gd, shares = rest[piece_count + 3 :]
     tiles, rows, side, chans = fields.shape
     tall = rows + 2 * RIM
     cells = tiles * side
@@ -63,13 +65,16 @@
         hi = close1[t * tall : (t + 1) * tall].astype(F32)
         pool_l[2 * tiles + t, :, :, :chans] = jnp.where(close_odd, lo, hi)
         pool_r[tiles + t, :, :, :chans] = jnp.where(close_odd, hi, lo)
-    lo = close0[tiles * tall :].astype(F32)
-    hi = close1[tiles * tall :].astype(F32)
+    lo = close0[tiles * tall : tiles * tall + RIM].astype(F32)
+    hi = close1[tiles * tall : tiles * tall + RIM].astype(F32)
     pool_l[tiles - 1, :RIM, :, :chans] = jnp.where(close_odd, lo, hi)
     pool_r[3 * tiles, rows + RIM :, :, :chans] = jnp.where(close_odd, hi, lo)
-    lo, hi = edge0[...].astype(F32), edge1[...].astype(F32)
-    edge_north = jnp.where(close_odd, lo, hi)
-    edge_south = jnp.where(close_odd, hi, lo)
+    lo = close0[tiles * tall + RIM :].astype(F32)
+    hi = close1[tiles * tall + RIM :].astype(F32)
+    edges[0, :, :, :chans] = jnp.where(close_odd, lo, hi)
+    edges[1, :, :, :chans] = jnp.where(close_odd, hi, lo)
+    edge_north = jnp.stack([edges[0, :, r, :chans] for r in range(RIM)])
+    edge_south = jnp.stack([edges[1, :, r, :chans] for r in range(RIM)])
 
     lane = lax.broadcasted_iota(jnp.int32, (tiles, side + 16, 128), 2)
     one_behind = jnp.where(lane == chans - 128, 1.0, 0.0).astype(F32)
@@ -112,7 +117,7 @@
         if piece_count == fsdp_count and fsdp_count != 4:
             owner.append(i)
         else:
-            owner.append((fsdp, 3 - fsdp, fsdp ^ 1, 3 - (fsdp ^ 1))[i])
+            owner.append((fsdp, 3 - fsdp, fsdp ^ 1, fsdp ^ 2)[i])
     from_lane = lax.broadcasted_iota(jnp.int32, (128, LANES), 0)
     to_lane = lax.broadcasted_iota(jnp.int32, (128, LANES), 1)
     for half in range(2):
@@ -179,25 +184,68 @@
     for i in range(fsdp_count):
         shares[i] = turned[i * share : (i + 1) * share]
     for i in range(fsdp_count // 2):
-        keep[i] = shares[fsdp ^ (2 * i)]
-        send[i] = shares[fsdp ^ (2 * i + 1)]
-
-
-def finish_kernel(entries, own, first, second, third, weight_out, bias_out, squares_out):
-    del entries
-    total = (own[...].astype(F32) + first[...].astype(F32)) + (
-        second[...].astype(F32) + third[...].astype(F32)
-    )
+        for into, whose in ((keep, fsdp ^ (2 * i)), (send, fsdp ^ (2 * i + 1))):
+            low, high = shares[whose, :, :HALF_SUM], shares[whose, :, HALF_SUM:]
+            into[i, 0] = jnp.where(close_odd, high, low)
+            into[i, 1] = jnp.where(close_odd, low, high)
+
+
+def bias_lane(shape, half, at):
+    lane = lax.broadcasted_iota(jnp.int32, shape, len(shape) - 1)
+    return (lane == at) & (half == 1)
+
+
+def narrowed(value, half):
+    lead = value.shape[:-2]
+    index = lax.broadcasted_iota(jnp.int32, value.shape, len(lead) - 1)
+    whose = index ^ half
+    bias_sum = value[..., BIAS_AT : BIAS_AT + 1] + value[..., BIAS_AT + 1 : BIAS_AT + 2]
+    bias_low = bias_sum - lax.reduce_precision(bias_sum, 8, 7)
+    value = jnp.where(bias_lane(value.shape, whose, BIAS_AT), bias_sum, value)
+    return jnp.where(bias_lane(value.shape, whose, BIAS_AT + 1), bias_low, value).astype(BF16)
+
+
+def scale_kernel(entries, own, beside, *rest):
+    squares, (weight_out, bias_out) = rest[:-2], rest[-2:]
+    odd = lax.rem(lax.axis_index("space"), 2) == 1
     count = KS * KS * GROUP
-    lane = lax.broadcasted_iota(jnp.int32, total.shape, 1)
-    exact = total[:, count : count + 1] + total[:, count + 1 : count + 2]
-    total = jnp.where(lane < count, total, jnp.where(lane == count, exact, 0.0))
-    squares_out[...] = jnp.full((8, 128), jnp.sum(total * total), F32)
-    share = total.shape[0]
-    padded = jnp.concatenate([total, jnp.zeros((128 - share, total.shape[1]), F32)], axis=0)
-    turned = padded.T
+    share = own.shape[0]
+    sums = [value[0:1, :] for value in squares]
+    while len(sums) > 1:
+        sums = [a + b for a, b in zip(sums[::2], sums[1::2])]
+    scaling = lax.rsqrt(jnp.sum(sums[0], axis=1, keepdims=True) / entries + 1e-06)
+    low = jnp.where(odd, beside[...], own[...])
+    high = jnp.where(odd, own[...], beside[...])
+    whole = jnp.concatenate([low, high], axis=1) * scaling
+    whole = jnp.concatenate([whole, jnp.zeros((128 - share, SUM_LANES), F32)], axis=0)
+    turned = whole.T
     weight_out[...] = turned[:count, :share].reshape(weight_out.shape)
     bias_out[...] = turned[count : count + 1, :share]
+
+
+def pack_kernel(fields, weight, bias, rows_outward, rows_core, packed, west, east, wide):
+    tiles, rows, side, chans = fields.shape
+    share = weight.shape[2]
+    even = lax.rem(lax.axis_index("fsdp"), 2) == 0
+
+    @pl.when(even)
+    def _():
+        rows_outward[...] = fields[:, :RIM]
+        rows_core[...] = fields[:, rows - RIM :]
+
+    @pl.when(jnp.logical_not(even))
+    def _():
+        rows_core[...] = fields[:, :RIM]
+        rows_outward[...] = fields[:, rows - RIM :]
+
+    west[...] = fields[:, :, :RIM]
+    east[...] = fields[:, :, side - RIM :]
+    high = KS * KS - HALF_TAPS
+    wide[...] = jnp.zeros(wide.shape, F32)
+    wide[: HALF_TAPS * GROUP, :share] = weight[:HALF_TAPS].astype(F32).reshape(-1, share)
+    wide[: high * GROUP, HALF : HALF + share] = weight[HALF_TAPS:].astype(F32).reshape(-1, share)
+    wide[high * GROUP : high * GROUP + 1, HALF : HALF + share] = bias[...].astype(F32)
+    packed[...] = wide[...].astype(BF16)
 
 
 def per_device(fields, weight, bias, cotangent, neighbours):
@@ -210,61 +258,76 @@
     taps = KS * KS
     tall = rows + 2 * RIM
 
-    flat = weight.reshape(taps * GROUP, share)
-    low = flat[: HALF_TAPS * GROUP]
-    high = jnp.concatenate([flat[HALF_TAPS * GROUP :], bias[None, :]], axis=0)
-    low = jnp.pad(low, ((0, PIECE_ROWS - low.shape[0]), (0, HALF - share)))
-    high = jnp.pad(high, ((0, PIECE_ROWS - high.shape[0]), (0, HALF - share)))
-    packed = jnp.concatenate([low, high], axis=1)
-
     even = fsdp % 2 == 0
     first_rows, last_rows = fields[:, :RIM], fields[:, rows - RIM :]
 
     def outward(i):
         return (i + 1) % fsdp_count if i % 2 else (i - 1) % fsdp_count
 
-    from_outward = swapped(jnp.where(even, first_rows, last_rows), "fsdp", outward)
-    from_core = swapped(jnp.where(even, last_rows, first_rows), "fsdp", lambda i: i ^ 1)
-    above = jnp.where(even, from_outward, from_core)
-    below = jnp.where(even, from_core, from_outward)
+    def joined(name_outward, name_core):
+        up = jnp.where(even, name_outward, name_core)
+        return up, jnp.where(even, name_core, name_outward)
+
+    def inward(i):
+        return i ^ 1
+
+    first_ends = jnp.concatenate([first_rows[:, :, :RIM], first_rows[:, :, side - RIM :]], 2)
+    last_ends = jnp.concatenate([last_rows[:, :, :RIM], last_rows[:, :, side - RIM :]], 2)
+    ends_outward = swapped(jnp.where(even, first_ends, last_ends), "fsdp", outward)
+    ends_core = swapped(jnp.where(even, last_ends, first_ends), "fsdp", inward)
+    rim = jax.ShapeDtypeStruct((tiles, RIM, side, chans), BF16)
+    columns = jax.ShapeDtypeStruct((tiles, rows, RIM, chans), BF16)
+    rows_outward, rows_core, packed, west_own, east_own = pl.pallas_call(
+        pack_kernel,
+        out_shape=(rim, rim, jax.ShapeDtypeStruct((PIECE_ROWS, 128), BF16), columns, columns),
+        in_specs=[VMEM] * 3,
+        out_specs=(VMEM,) * 5,
+        scratch_shapes=[pltpu.VMEM((PIECE_ROWS, 128), F32)],
+        name="pack",
+    )(fields, weight.reshape(taps, GROUP, share), bias[None, :])
+    from_outward = swapped(rows_outward, "fsdp", outward)
+    from_core = swapped(rows_core, "fsdp", inward)
     if fsdp_count == 4:
         packed_out = swapped(packed, "fsdp", outward)
-        pieces = [
-            packed,
-            packed_out,
-            swapped(packed, "fsdp", lambda i: i ^ 1),
-            swapped(packed_out, "fsdp", lambda i: i ^ 1),
-        ]
-    else:
-        gathered = lax.all_gather(packed, "fsdp")
-        pieces = [gathered[i] for i in range(fsdp_count)]
-
-    tall_rows = jnp.concatenate([above, fields, below], 1)
-    west, east = tall_rows[:, :, :RIM], tall_rows[:, :, side - RIM :]
+        packed_core = swapped(packed, "fsdp", inward)
+    ends_above, ends_below = joined(ends_outward, ends_core)
+
+    west = jnp.concatenate([ends_above[:, :, :RIM], west_own, ends_below[:, :, :RIM]], 1)
+    east = jnp.concatenate([ends_above[:, :, RIM:], east_own, ends_below[:, :, RIM:]], 1)
     far_odd = (space // 2) % 2 == 1
     close_odd = space % 2 == 1
     far0 = hop_pairs(jnp.where(far_odd, west, east), 2, 0)
     far1 = hop_pairs(jnp.where(far_odd, east, west), 2, 1)
+    if fsdp_count == 4:
+        far0, packed_out = lax.optimization_barrier((far0, packed_out))
+        packed_last = swapped(packed_out, "fsdp", inward)
+    above, below = joined(from_outward, from_core)
     east_far = jnp.where(far_odd, far0, far1)[tiles - 1, :RIM]
     west_far = jnp.where(far_odd, far1, far0)[0, rows + RIM :]
     flat_side = (tiles * tall, RIM, chans)
-    to_east = jnp.concatenate([east.reshape(flat_side), east_far], 0)
-    to_west = jnp.concatenate([west.reshape(flat_side), west_far], 0)
+    edge_east = jnp.swapaxes(above[tiles - 1], 0, 1)
+    edge_west = jnp.swapaxes(below[0], 0, 1)
+    to_east = jnp.concatenate([east.reshape(flat_side), east_far, edge_east], 0)
+    to_west = jnp.concatenate([west.reshape(flat_side), west_far, edge_west], 0)
     close0 = hop_pairs(jnp.where(close_odd, to_west, to_east), 1, 0)
     close1 = hop_pairs(jnp.where(close_odd, to_east, to_west), 1, 1)
-    edge0 = hop_pairs(jnp.where(close_odd, below[0], above[tiles - 1]), 1, 0)
-    edge1 = hop_pairs(jnp.where(close_odd, above[tiles - 1], below[0]), 1, 1)
+    if fsdp_count == 4:
+        pieces = [packed, packed_out, packed_core, packed_last]
+    else:
+        gathered = lax.all_gather(packed, "fsdp")
+        pieces = [gathered[i] for i in range(fsdp_count)]
 
     cells = tiles * side
-    part = jax.ShapeDtypeStruct((fsdp_count // 2, share, SUM_LANES), F32)
+    part = jax.ShapeDtypeStruct((fsdp_count // 2, 2, share, HALF_SUM), F32)
     activations, keep, send = pl.pallas_call(
         functools.partial(main_kernel, len(pieces)),
         out_shape=(jax.ShapeDtypeStruct(fields.shape, BF16), part, part),
-        in_specs=[SMEM] + [VMEM] * (10 + len(pieces)),
+        in_specs=[SMEM] + [VMEM] * (8 + len(pieces)),
         out_specs=(VMEM, VMEM, VMEM),
         scratch_shapes=[
             pltpu.VMEM((4 * tiles + 1, tall, RIM, LANES), F32),
             pltpu.VMEM((4 * tiles + 1, tall, RIM, LANES), F32),
+            pltpu.VMEM((2, side, RIM, LANES), F32),
             pltpu.VMEM((tall, tiles, side + 16, LANES), F32),
             pltpu.VMEM((tall, cells, KS * LANES), BF16),
             pltpu.VMEM((tall, KS * XROWS, cells), BF16),
@@ -278,44 +341,48 @@
         name="section",
     )(
         neighbours, fields, cotangent, above, below,
-        far0, far1, close0, close1, edge0, edge1, *pieces,
+        far0, far1, close0, close1, *pieces,
     )
 
     held = keep + swapped(send, "fsdp", lambda i: i ^ 1)
+    half = space % 2
     distance = 2
     while held.shape[0] > 1:
-        pairs = held.reshape(held.shape[0] // 2, 2, share, SUM_LANES)
-        held = pairs[:, 0] + swapped(pairs[:, 1], "fsdp", lambda i: i ^ distance)
+        pairs = held.reshape(held.shape[0] // 2, 2, 2, share, HALF_SUM)
+        sent = narrowed(pairs[:, 1], half)
+        held = pairs[:, 0] + swapped(sent, "fsdp", lambda i: i ^ distance).astype(F32)
         distance *= 2
-    held = held[0]
-    distance = 1
+    held = held[0, 0] + swapped(held[0, 1], "space", lambda i: i ^ 1)
+    distance = 2
     while distance * 4 < space_count:
         held = held + swapped(held, "space", lambda i: i ^ distance)
         distance *= 2
-    count = taps * GROUP
-    lane = lax.broadcasted_iota(jnp.int32, held.shape, 1)
-    bias_sum = held[:, count : count + 1]
-    bias_low = bias_sum - lax.reduce_precision(bias_sum, 8, 7)
-    rounded = jnp.where(lane == count + 1, bias_low, held).astype(BF16)
+    rounded = narrowed(jnp.stack([held]), half)[0]
     others = [swapped(rounded, "space", lambda i, k=k: i ^ (distance * k)) for k in (1, 2, 3)]
-    entries = count * chans + chans
-    weight_sum, bias_sum, squares = pl.pallas_call(
-        functools.partial(finish_kernel, entries),
+    total = (rounded.astype(F32) + others[0].astype(F32)) + (
+        others[1].astype(F32) + others[2].astype(F32)
+    )
+    exact = total[:, BIAS_AT : BIAS_AT + 1] + total[:, BIAS_AT + 1 : BIAS_AT + 2]
+    total = jnp.where(bias_lane(total.shape, half, BIAS_AT), exact, total)
+    total = jnp.where(bias_lane(total.shape, half, BIAS_AT + 1), 0.0, total)
+    total_beside = swapped(total, "space", lambda i: i ^ 1)
+
+    squares = jnp.sum(total * total, 0, keepdims=True) + jnp.sum(total_beside * total_beside, 0, keepdims=True)
+    squares = jnp.broadcast_to(squares, (8, HALF_SUM))
+    all_squares = [squares] + [
+        swapped(squares, "fsdp", lambda i, k=k: i ^ k) for k in range(1, fsdp_count)
+    ]
+    weight_step, bias_step = pl.pallas_call(
+        functools.partial(scale_kernel, taps * GROUP * chans + chans),
         out_shape=(
             jax.ShapeDtypeStruct((KS, KS, GROUP, share), F32),
             jax.ShapeDtypeStruct((1, share), F32),
-            jax.ShapeDtypeStruct((8, 128), F32),
         ),
-        in_specs=[VMEM] * 4,
-        out_specs=(VMEM, VMEM, VMEM),
-        name="finish",
-    )(rounded, *others)
-    distance = 1
-    while distance < fsdp_count:
-        squares = squares + swapped(squares, "fsdp", lambda i: i ^ distance)
-        distance *= 2
-    scaling = lax.rsqrt(squares[0, 0] / entries + 1e-06)
-    return (activations, weight_sum * scaling, bias_sum[0] * scaling)
+        in_specs=[VMEM] * (2 + fsdp_count),
+        out_specs=(VMEM, VMEM),
+        name="scale",
+    )(total, total_beside, *all_squares)
+    return (activations, weight_step, bias_step[0])
 
 
 def solution(mesh):

time: 87.6 us -> 81.7 us (0.933)
  other arithmetic: 5.01 us -> 1.64 us
  starting transfers between devices: 28.9 us -> 25.9 us
  waiting for transfers between devices: 28.4 us -> 25.6 us
  Pallas kernels: 20.8 us -> 23.1 us
  local copies, waits for them, and re-layouts: 2.57 us -> 4.1 us
    ppermute x19 -> x21, starting transfers between devices: 28.9 us -> 25.9 us  [swapped(): return lax.ppermute(value, axis, [p for p in pairs if 0 <= p[1] < count])]
    ppermute x19 -> x21, waiting for transfers between devices: 28.4 us -> 25.6 us  [swapped(): return lax.ppermute(value, axis, [p for p in pairs if 0 <= p[1] < count])]
    mul x2 -> x0, other arithmetic: 2.37 us -> none  [per_device(): return (activations, weight_sum * scaling, bias_sum[0] * scaling)]
    pallas_call x1 -> x2, Pallas kernels: 2.22 us -> 4.25 us  [the longest x1 2.18 us: per_device(): pl.pallas_call(pack_kernel, out_shape=(rim, rim, jax.ShapeDtypeStruct((PI...]
    pallas_call x0 -> x2, local copies, waits for them, and re-layouts: none -> 1.21 us  [per_device(): pl.pallas_call(pack_kernel, out_shape=(rim, rim, jax.ShapeDtypeStruct((PI...]
    select_n x3, other arithmetic: 1.13 us -> 0.06 us  [the longest x1 0.03 us: per_device(): jnp.where(even, first_ends, last_ends)]
    unnamed x18 -> x22, local copies, waits for them, and re-layouts: 1.95 us -> 1.92 us
  transfers between devices with their start and end apart: 19 -> 21, of which waited for: 9 -> 9; matrix products, arithmetic and copies ran while one was open for 1% -> 2% of each run, Pallas kernels for 0% -> 3%
where the time goes in v1:
time: 81.7 us; the launch traced here: 81.3 us
  starting transfers between devices  25.9 us (32%)
  waiting for transfers between devices  25.6 us (31%)
  Pallas kernels  23.1 us (28%)
  local copies, waits for them, and re-layouts  4.1 us (5%)
  other arithmetic  1.64 us (2%)
  between operations  0.99 us (1%)
    ppermute x21, starting transfers between devices, swapped(): return lax.ppermute(value, axis, [p for p in pairs if 0 <= p[1] < count])  25.9 us
    ppermute x21, waiting for transfers between devices, swapped(): return lax.ppermute(value, axis, [p for p in pairs if 0 <= p[1] < count])  25.6 us
    pallas_call x1, Pallas kernels, per_device(): pl.pallas_call(functools.partial(main_kernel, len(pieces)), out_shape=(ja...  18.8 us
    pallas_call x1, Pallas kernels, per_device(): pl.pallas_call(pack_kernel, out_shape=(rim, rim, jax.ShapeDtypeStruct((PI...  2.18 us
    pallas_call x1, Pallas kernels, per_device(): pl.pallas_call(functools.partial(scale_kernel, taps * GROUP * chans + cha...  2.07 us
    unnamed x22, local copies, waits for them, and re-layouts  1.92 us
  transfers between devices with their start and end apart: 21, of which 9 were waited for; matrix products, arithmetic and copies ran while one was open for 2% of the time, Pallas kernels for 3%

profile of v1, /device:TPU:0, one launch (start us, length us, event | category | flops | bytes accessed | tf_op | source)
XLA Modules:
  0.0 81.3 jit_solution(9874006660170586946)
XLA Ops:
  0.6 0.8 fusion.10
  1.5 2.4 %collective-permute-start.2 = (bf16[2,2,4,200]{3,2,1,0:T(4,128)(2,1)S(1)}, bf16[2,2,4,200]{3,2,1,0:T(4,128)(2,1)S(1)}, u32[]{:S(2)}, u32[]{:S(2)}) collective-permute-start(bf16[2,2,4,200]{3,2,1,0:T(4,128)(2,1)S(1)} %get-tuple-element.48), channel_id=1, source_target_pairs={{0,3},{1,2},{2,1},{3,0},{4,7},{5,6},{6,5},{7,4},{8,11},{9,10},{10,... | collective-permute-start | bytes 19208 | tf_op jit(solution)/shard_map/ppermute | solution.py:30
  4.6 2.2 %pack.1 = (bf16[2,2,64,200]{3,2,1,0:T(8,128)(2,1)}, bf16[2,2,64,200]{3,2,1,0:T(8,128)(2,1)}, bf16[528,128]{1,0:T(8,128)(2,1)}, bf16[2,16,2,200]{3,2,1,0:T(2,128)(2,1)}, bf16[2,16,2,200]{3,2,1,0:T(2,128)(2,1)}) custom-call(bf16[2,16,64,200]{3,2,1,0:T(8,128)(2,1)} %fields.3, bf16[25,40,50]{2,1,0:T(8,128)(2,1)} %bitcast.58, bf16[1,50]{1,0:T(2,128)(2,1)} %bitcast.66), custom_call_target="tpu_custom_call" | custom-call | tf_op jit(solution)/shard_map/pack/pallas_call | solution.py:280
  6.9 1.1 %copy.13 = bf16[2,2,64,200]{3,1,2,0:T(2,128)(2,1)S(1)} copy(bf16[2,2,64,200]{3,2,1,0:T(8,128)(2,1)} %get-tuple-element.16) | data formatting | bytes 204800 | tf_op jit(solution)/shard_map/pack/pallas_call | solution.py:280
  8.7 1.7 %collective-permute-start = (bf16[2,2,64,200]{3,1,2,0:T(2,128)(2,1)S(1)}, bf16[2,2,64,200]{3,1,2,0:T(2,128)(2,1)S(1)}, u32[]{:S(2)}, u32[]{:S(2)}) collective-permute-start(bf16[2,2,64,200]{3,1,2,0:T(2,128)(2,1)S(1)} %copy.12), channel_id=1, source_target_pairs={{0,3},{1,2},{2,1},{3,0},{4,7},{5,6},{6,5},{7,4},{8,11},{9,10},{10,... | collective-permute-start | bytes 307208 | tf_op jit(solution)/shard_map/ppermute | solution.py:30
  10.4 0.7 copy-done.7
  11.4 1.6 %collective-permute-start.4 = (bf16[2,20,2,200]{3,2,1,0:T(2,128)(2,1)S(1)}, bf16[2,20,2,200]{3,2,1,0:T(2,128)(2,1)S(1)}, u32[]{:S(2)}, u32[]{:S(2)}) collective-permute-start(bf16[2,20,2,200]{3,2,1,0:T(2,128)(2,1)S(1)} %bitcast.61), channel_id=1, source_target_pairs={{0,8},{4,12},{8,0},{12,4},{16,24},{20,28},{24,16},{28,20},{1,9},{5... | collective-permute-start | bytes 96008 | tf_op jit(solution)/shard_map/ppermute | solution.py:30
  13.7 1.8 %collective-permute-done = bf16[2,2,64,200]{3,1,2,0:T(2,128)(2,1)S(1)} collective-permute-done((bf16[2,2,64,200]{3,1,2,0:T(2,128)(2,1)S(1)}, bf16[2,2,64,200]{3,1,2,0:T(2,128)(2,1)S(1)}, u32[]{:S(2)}, u32[]{:S(2)}) %collective-permute-start) | collective-permute-done | bytes 102432 | tf_op jit(solution)/shard_map/ppermute | solution.py:30
  16.2 1.6 %collective-permute-start.7 = (bf16[106,2,200]{2,1,0:T(2,128)(2,1)S(1)}, bf16[106,2,200]{2,1,0:T(2,128)(2,1)S(1)}, u32[]{:S(2)}, u32[]{:S(2)}) collective-permute-start(bf16[106,2,200]{2,1,0:T(2,128)(2,1)S(1)} %get-tuple-element.43), channel_id=1, source_target_pairs={{0,4},{4,0},{8,12},{12,8},{16,20},{20,16},{24,28},{28,24},{1,5},{5... | collective-permute-start | bytes 254408 | tf_op jit(solution)/shard_map/ppermute | solution.py:30
  18.6 3.0 %collective-permute-done.7.close0 = bf16[106,2,200]{2,1,0:T(2,128)(2,1)S(1)} collective-permute-done((bf16[106,2,200]{2,1,0:T(2,128)(2,1)S(1)}, bf16[106,2,200]{2,1,0:T(2,128)(2,1)S(1)}, u32[]{:S(2)}, u32[]{:S(2)}) %collective-permute-start.7) | collective-permute-done | bytes 84832 | tf_op jit(solution)/shard_map/ppermute | solution.py:30
  21.6 18.8 %section.1 = (bf16[2,16,64,200]{3,2,1,0:T(8,128)(2,1)}, f32[2,2,50,512]{3,2,1,0:T(8,128)S(1)}, f32[2,2,50,512]{3,2,1,0:T(8,128)S(1)}) custom-call(s32[2,8]{1,0:T(2,128)S(1)} %copy-done.1, bf16[2,16,64,200]{3,2,1,0:T(8,128)(2,1)} %fields.3, bf16[2,16,64,200]{3,2,1,0:T(8,128)(2,1)} %cot.1, bf16[2,2,64,200]{3,2,1,0:T(8,128)(2,1)S(1)} %copy.14.above, ...), custom_call_target="tpu_custom_call" | custom-call | tf_op jit(solution)/shard_map/section/pallas_call | solution.py:322
  40.5 1.8 %collective-permute-done.11 = f32[2,2,50,512]{3,2,1,0:T(8,128)S(1)} collective-permute-done((f32[2,2,50,512]{3,2,1,0:T(8,128)S(1)}, f32[2,2,50,512]{3,2,1,0:T(8,128)S(1)}, u32[]{:S(2)}, u32[]{:S(2)}) %collective-permute-start.11) | collective-permute-done | bytes 409632 | tf_op jit(solution)/shard_map/ppermute | solution.py:30
  42.9 5.1 %collective-permute-done.12 = bf16[1,2,50,512]{3,2,1,0:T(8,128)(2,1)S(1)} collective-permute-done((bf16[1,2,50,512]{3,2,1,0:T(8,128)(2,1)S(1)}, bf16[1,2,50,512]{3,2,1,0:T(8,128)(2,1)S(1)}, u32[]{:S(2)}, u32[]{:S(2)}) %collective-permute-start.12) | collective-permute-done | bytes 102432 | tf_op jit(solution)/shard_map/ppermute | solution.py:30
  48.0 6.5 %collective-permute-start.13 = (f32[50,512]{1,0:T(8,128)S(1)}, f32[50,512]{1,0:T(8,128)S(1)}, u32[]{:S(2)}, u32[]{:S(2)}) collective-permute-start(f32[50,512]{1,0:T(8,128)S(1)} %slice_bitcast_fusion.2), channel_id=1, source_target_pairs={{0,4},{4,0},{8,12},{12,8},{16,20},{20,16},{24,28},{28,24},{1,5},{5... | collective-permute-start | bytes 307208 | tf_op jit(solution)/shard_map/ppermute | solution.py:30
  54.6 2.8 %collective-permute-done.13 = f32[50,512]{1,0:T(8,128)S(1)} collective-permute-done((f32[50,512]{1,0:T(8,128)S(1)}, f32[50,512]{1,0:T(8,128)S(1)}, u32[]{:S(2)}, u32[]{:S(2)}) %collective-permute-start.13) | collective-permute-done | bytes 102432 | tf_op jit(solution)/shard_map/ppermute | solution.py:30
  57.6 3.5 %collective-permute-start.14 = (bf16[50,512]{1,0:T(8,128)(2,1)S(1)}, bf16[50,512]{1,0:T(8,128)(2,1)S(1)}, u32[]{:S(2)}, u32[]{:S(2)}) collective-permute-start(bf16[50,512]{1,0:T(8,128)(2,1)S(1)} %select_convert_fusion.1), channel_id=1, source_target_pairs={{0,8},{4,12},{8,0},{12,4},{16,24},{20,28},{24,16},{28,20},{1,9},{5... | collective-permute-start | bytes 153608 | tf_op jit(solution)/shard_map/ppermute | solution.py:30
  61.2 1.5 %collective-permute-start.15 = (bf16[50,512]{1,0:T(8,128)(2,1)S(1)}, bf16[50,512]{1,0:T(8,128)(2,1)S(1)}, u32[]{:S(2)}, u32[]{:S(2)}) collective-permute-start(bf16[50,512]{1,0:T(8,128)(2,1)S(1)} %select_convert_fusion.1), channel_id=1, source_target_pairs={{0,16},{4,20},{8,24},{12,28},{16,0},{20,4},{24,8},{28,12},{1,17},{... | collective-permute-start | bytes 153608 | tf_op jit(solution)/shard_map/ppermute | solution.py:30
  62.7 1.4 %collective-permute-start.16 = (bf16[50,512]{1,0:T(8,128)(2,1)S(1)}, bf16[50,512]{1,0:T(8,128)(2,1)S(1)}, u32[]{:S(2)}, u32[]{:S(2)}) collective-permute-start(bf16[50,512]{1,0:T(8,128)(2,1)S(1)} %select_convert_fusion.1), channel_id=1, source_target_pairs={{0,24},{4,28},{8,16},{12,20},{16,8},{20,12},{24,0},{28,4},{1,25},{... | collective-permute-start | bytes 153608 | tf_op jit(solution)/shard_map/ppermute | solution.py:30
  64.1 2.2 %collective-permute-done.15 = bf16[50,512]{1,0:T(8,128)(2,1)S(1)} collective-permute-done((bf16[50,512]{1,0:T(8,128)(2,1)S(1)}, bf16[50,512]{1,0:T(8,128)(2,1)S(1)}, u32[]{:S(2)}, u32[]{:S(2)}) %collective-permute-start.15) | collective-permute-done | bytes 51232 | tf_op jit(solution)/shard_map/ppermute | solution.py:30
  66.3 2.5 %collective-permute-done.16 = bf16[50,512]{1,0:T(8,128)(2,1)S(1)} collective-permute-done((bf16[50,512]{1,0:T(8,128)(2,1)S(1)}, bf16[50,512]{1,0:T(8,128)(2,1)S(1)}, u32[]{:S(2)}, u32[]{:S(2)}) %collective-permute-start.16) | collective-permute-done | bytes 51232 | tf_op jit(solution)/shard_map/ppermute | solution.py:30
  69.7 4.3 %collective-permute-done.17.beside = f32[50,512]{1,0:T(8,128)S(1)} collective-permute-done((f32[50,512]{1,0:T(8,128)S(1)}, f32[50,512]{1,0:T(8,128)S(1)}, u32[]{:S(2)}, u32[]{:S(2)}) %collective-permute-start.17) | collective-permute-done | bytes 102432 | tf_op jit(solution)/shard_map/ppermute | solution.py:30
  74.7 1.3 %collective-permute-start.20 = (f32[8,512]{1,0:T(8,128)S(1)}, f32[8,512]{1,0:T(8,128)S(1)}, u32[]{:S(2)}, u32[]{:S(2)}) collective-permute-start(f32[8,512]{1,0:T(8,128)S(1)} %broadcast_in_dim.70.rest_0_), channel_id=1, source_target_pairs={{0,3},{1,2},{2,1},{3,0},{4,7},{5,6},{6,5},{7,4},{8,11},{9,10},{10,... | collective-permute-start | bytes 49160 | tf_op jit(solution)/shard_map/ppermute | solution.py:30
  76.0 2.1 %collective-permute-done.19.rest_2_ = f32[8,512]{1,0:T(8,128)S(1)} collective-permute-done((f32[8,512]{1,0:T(8,128)S(1)}, f32[8,512]{1,0:T(8,128)S(1)}, u32[]{:S(2)}, u32[]{:S(2)}) %collective-permute-start.19) | collective-permute-done | bytes 16416 | tf_op jit(solution)/shard_map/ppermute | solution.py:30
  79.2 2.1 %scale.1 = (f32[5,5,40,50]{3,2,1,0:T(8,128)}, f32[1,50]{1,0:T(1,128)}) custom-call(f32[50,512]{1,0:T(8,128)} %copy-done.2, f32[50,512]{1,0:T(8,128)} %copy-done.3, f32[8,512]{1,0:T(8,128)} %copy-done.5, f32[8,512]{1,0:T(8,128)} %copy-done.8, f32[8,512]{1,0:T(8,128)} %copy-done.9, f32[8,512]{1,0:T(8,128)} %copy-done.10), custom_call_target="tpu_custom_call" | custom-call | tf_op jit(solution)/shard_map/scale/pallas_call | solution.py:375
  (75 shorter events, 7.5 us)
Async XLA Ops:
  1.5 7.2 %collective-permute-start.2 = (bf16[2,2,4,200]{3,2,1,0:T(4,128)(2,1)S(1)}, bf16[2,2,4,200]{3,2,1,0:T(4,128)(2,1)S(1)}, u32[]{:S(2)}, u32[]{:S(2)}) collective-permute-start(bf16[2,2,4,200]{3,2,1,0:T(4,128)(2,1)S(1)} %get-tuple-element.48), channel_id=1, source_target_pairs={{0,3},{1,2},{2,1},{3,0},{4,7},{5,6},{6,5},{7,4},{8,11},{9,10},{10,... | collective-permute-start | bytes 19208 | tf_op jit(solution)/shard_map/ppermute | solution.py:30
  3.9 6.5 %collective-permute-start.3 = (bf16[2,2,4,200]{3,2,1,0:T(4,128)(2,1)S(1)}, bf16[2,2,4,200]{3,2,1,0:T(4,128)(2,1)S(1)}, u32[]{:S(2)}, u32[]{:S(2)}) collective-permute-start(bf16[2,2,4,200]{3,2,1,0:T(4,128)(2,1)S(1)} %get-tuple-element.49), channel_id=1, source_target_pairs={{0,1},{1,0},{2,3},{3,2},{4,5},{5,4},{6,7},{7,6},{8,9},{9,8},{10,11... | collective-permute-start | bytes 19208 | tf_op jit(solution)/shard_map/ppermute | solution.py:30
  6.8 8.9 %collective-permute-start.5 = (bf16[528,128]{1,0:T(8,128)(2,1)}, bf16[528,128]{1,0:T(8,128)(2,1)S(1)}, u32[]{:S(2)}, u32[]{:S(2)}) collective-permute-start(bf16[528,128]{1,0:T(8,128)(2,1)} %get-tuple-element.19.rest_0_), channel_id=1, source_target_pairs={{0,3},{1,2},{2,1},{3,0},{4,7},{5,6},{6,5},{7,4},{8,11},{9,10},{10,... | collective-permute-start | bytes 405512 | tf_op jit(solution)/shard_map/ppermute | solution.py:30
  6.8 11.7 %collective-permute-start.9 = (bf16[528,128]{1,0:T(8,128)(2,1)}, bf16[528,128]{1,0:T(8,128)(2,1)S(1)}, u32[]{:S(2)}, u32[]{:S(2)}) collective-permute-start(bf16[528,128]{1,0:T(8,128)(2,1)} %get-tuple-element.19.rest_0_), channel_id=1, source_target_pairs={{0,1},{1,0},{2,3},{3,2},{4,5},{5,4},{6,7},{7,6},{8,9},{9,8},{10,11... | collective-permute-start | bytes 405512 | tf_op jit(solution)/shard_map/ppermute | solution.py:30
  7.9 5.1 %collective-permute-start.1 = (bf16[2,2,64,200]{3,1,2,0:T(2,128)(2,1)S(1)}, bf16[2,2,64,200]{3,1,2,0:T(2,128)(2,1)S(1)}, u32[]{:S(2)}, u32[]{:S(2)}) collective-permute-start(bf16[2,2,64,200]{3,1,2,0:T(2,128)(2,1)S(1)} %copy.13), channel_id=1, source_target_pairs={{0,1},{1,0},{2,3},{3,2},{4,5},{5,4},{6,7},{7,6},{8,9},{9,8},{10,11... | collective-permute-start | bytes 307208 | tf_op jit(solution)/shard_map/ppermute | solution.py:30
  8.7 6.8 %collective-permute-start = (bf16[2,2,64,200]{3,1,2,0:T(2,128)(2,1)S(1)}, bf16[2,2,64,200]{3,1,2,0:T(2,128)(2,1)S(1)}, u32[]{:S(2)}, u32[]{:S(2)}) collective-permute-start(bf16[2,2,64,200]{3,1,2,0:T(2,128)(2,1)S(1)} %copy.12), channel_id=1, source_target_pairs={{0,3},{1,2},{2,1},{3,0},{4,7},{5,6},{6,5},{7,4},{8,11},{9,10},{10,... | collective-permute-start | bytes 307208 | tf_op jit(solution)/shard_map/ppermute | solution.py:30
  11.4 4.3 %collective-permute-start.4 = (bf16[2,20,2,200]{3,2,1,0:T(2,128)(2,1)S(1)}, bf16[2,20,2,200]{3,2,1,0:T(2,128)(2,1)S(1)}, u32[]{:S(2)}, u32[]{:S(2)}) collective-permute-start(bf16[2,20,2,200]{3,2,1,0:T(2,128)(2,1)S(1)} %bitcast.61), channel_id=1, source_target_pairs={{0,8},{4,12},{8,0},{12,4},{16,24},{20,28},{24,16},{28,20},{1,9},{5... | collective-permute-start | bytes 96008 | tf_op jit(solution)/shard_map/ppermute | solution.py:30
  13.0 2.8 %collective-permute-start.6 = (bf16[2,20,2,200]{3,2,1,0:T(2,128)(2,1)S(1)}, bf16[2,20,2,200]{3,2,1,0:T(2,128)(2,1)S(1)}, u32[]{:S(2)}, u32[]{:S(2)}) collective-permute-start(bf16[2,20,2,200]{3,2,1,0:T(2,128)(2,1)S(1)} %get-tuple-element.33), channel_id=1, source_target_pairs={{8,16},{12,20},{16,8},{20,12},{9,17},{13,21},{17,9},{21,13},{10,18... | collective-permute-start | bytes 96008 | tf_op jit(solution)/shard_map/ppermute | solution.py:30
  15.6 5.9 %collective-permute-start.10 = (bf16[528,128]{1,0:T(8,128)(2,1)S(1)}, bf16[528,128]{1,0:T(8,128)(2,1)S(1)}, u32[]{:S(2)}, u32[]{:S(2)}) collective-permute-start(bf16[528,128]{1,0:T(8,128)(2,1)S(1)} %collective-permute-done.5.rest_1_), channel_id=1, source_target_pairs={{0,1},{1,0},{2,3},{3,2},{4,5},{5,4},{6,7},{7,6},{8,9},{9,8},{10,11... | collective-permute-start | bytes 405512 | tf_op jit(solution)/shard_map/ppermute | solution.py:30
  16.2 5.4 %collective-permute-start.7 = (bf16[106,2,200]{2,1,0:T(2,128)(2,1)S(1)}, bf16[106,2,200]{2,1,0:T(2,128)(2,1)S(1)}, u32[]{:S(2)}, u32[]{:S(2)}) collective-permute-start(bf16[106,2,200]{2,1,0:T(2,128)(2,1)S(1)} %get-tuple-element.43), channel_id=1, source_target_pairs={{0,4},{4,0},{8,12},{12,8},{16,20},{20,16},{24,28},{28,24},{1,5},{5... | collective-permute-start | bytes 254408 | tf_op jit(solution)/shard_map/ppermute | solution.py:30
  17.8 3.8 %collective-permute-start.8 = (bf16[106,2,200]{2,1,0:T(2,128)(2,1)S(1)}, bf16[106,2,200]{2,1,0:T(2,128)(2,1)S(1)}, u32[]{:S(2)}, u32[]{:S(2)}) collective-permute-start(bf16[106,2,200]{2,1,0:T(2,128)(2,1)S(1)} %get-tuple-element.42), channel_id=1, source_target_pairs={{4,8},{8,4},{12,16},{16,12},{20,24},{24,20},{5,9},{9,5},{13,17},{1... | collective-permute-start | bytes 254408 | tf_op jit(solution)/shard_map/ppermute | solution.py:30
  40.4 1.9 %collective-permute-start.11 = (f32[2,2,50,512]{3,2,1,0:T(8,128)S(1)}, f32[2,2,50,512]{3,2,1,0:T(8,128)S(1)}, u32[]{:S(2)}, u32[]{:S(2)}) collective-permute-start(f32[2,2,50,512]{3,2,1,0:T(8,128)S(1)} %get-tuple-element.24), channel_id=1, source_target_pairs={{0,1},{1,0},{2,3},{3,2},{4,5},{5,4},{6,7},{7,6},{8,9},{9,8},{10,11... | collective-permute-start | bytes 1228808 | tf_op jit(solution)/shard_map/ppermute | solution.py:30
  42.7 5.3 %collective-permute-start.12 = (bf16[1,2,50,512]{3,2,1,0:T(8,128)(2,1)S(1)}, bf16[1,2,50,512]{3,2,1,0:T(8,128)(2,1)S(1)}, u32[]{:S(2)}, u32[]{:S(2)}) collective-permute-start(bf16[1,2,50,512]{3,2,1,0:T(8,128)(2,1)S(1)} %select_convert_fusion), channel_id=1, source_target_pairs={{0,2},{1,3},{2,0},{3,1},{4,6},{5,7},{6,4},{7,5},{8,10},{9,11},{10,... | collective-permute-start | bytes 307208 | tf_op jit(solution)/shard_map/ppermute | solution.py:30
  48.0 9.3 %collective-permute-start.13 = (f32[50,512]{1,0:T(8,128)S(1)}, f32[50,512]{1,0:T(8,128)S(1)}, u32[]{:S(2)}, u32[]{:S(2)}) collective-permute-start(f32[50,512]{1,0:T(8,128)S(1)} %slice_bitcast_fusion.2), channel_id=1, source_target_pairs={{0,4},{4,0},{8,12},{12,8},{16,20},{20,16},{24,28},{28,24},{1,5},{5... | collective-permute-start | bytes 307208 | tf_op jit(solution)/shard_map/ppermute | solution.py:30
  57.6 6.4 %collective-permute-start.14 = (bf16[50,512]{1,0:T(8,128)(2,1)S(1)}, bf16[50,512]{1,0:T(8,128)(2,1)S(1)}, u32[]{:S(2)}, u32[]{:S(2)}) collective-permute-start(bf16[50,512]{1,0:T(8,128)(2,1)S(1)} %select_convert_fusion.1), channel_id=1, source_target_pairs={{0,8},{4,12},{8,0},{12,4},{16,24},{20,28},{24,16},{28,20},{1,9},{5... | collective-permute-start | bytes 153608 | tf_op jit(solution)/shard_map/ppermute | solution.py:30
  61.2 5.1 %collective-permute-start.15 = (bf16[50,512]{1,0:T(8,128)(2,1)S(1)}, bf16[50,512]{1,0:T(8,128)(2,1)S(1)}, u32[]{:S(2)}, u32[]{:S(2)}) collective-permute-start(bf16[50,512]{1,0:T(8,128)(2,1)S(1)} %select_convert_fusion.1), channel_id=1, source_target_pairs={{0,16},{4,20},{8,24},{12,28},{16,0},{20,4},{24,8},{28,12},{1,17},{... | collective-permute-start | bytes 153608 | tf_op jit(solution)/shard_map/ppermute | solution.py:30
  62.7 6.1 %collective-permute-start.16 = (bf16[50,512]{1,0:T(8,128)(2,1)S(1)}, bf16[50,512]{1,0:T(8,128)(2,1)S(1)}, u32[]{:S(2)}, u32[]{:S(2)}) collective-permute-start(bf16[50,512]{1,0:T(8,128)(2,1)S(1)} %select_convert_fusion.1), channel_id=1, source_target_pairs={{0,24},{4,28},{8,16},{12,20},{16,8},{20,12},{24,0},{28,4},{1,25},{... | collective-permute-start | bytes 153608 | tf_op jit(solution)/shard_map/ppermute | solution.py:30
  69.1 9.0 %copy-start.2 = (f32[50,512]{1,0:T(8,128)}, f32[50,512]{1,0:T(8,128)S(1)}, u32[]{:S(2)}) copy-start(f32[50,512]{1,0:T(8,128)S(1)} %get-tuple-element.32.own) | copy-start | bytes 307204
  69.1 4.9 %collective-permute-start.17 = (f32[50,512]{1,0:T(8,128)S(1)}, f32[50,512]{1,0:T(8,128)S(1)}, u32[]{:S(2)}, u32[]{:S(2)}) collective-permute-start(f32[50,512]{1,0:T(8,128)S(1)} %get-tuple-element.32.own), channel_id=1, source_target_pairs={{0,4},{4,0},{8,12},{12,8},{16,20},{20,16},{24,28},{28,24},{1,5},{5... | collective-permute-start | bytes 307208 | tf_op jit(solution)/shard_map/ppermute | solution.py:30
  74.0 4.1 %copy-start.3 = (f32[50,512]{1,0:T(8,128)}, f32[50,512]{1,0:T(8,128)S(1)}, u32[]{:S(2)}) copy-start(f32[50,512]{1,0:T(8,128)S(1)} %collective-permute-done.17.beside) | copy-start | bytes 307204
  74.0 4.1 %copy-start.5 = (f32[8,512]{1,0:T(8,128)}, f32[8,512]{1,0:T(8,128)S(1)}, u32[]{:S(2)}) copy-start(f32[8,512]{1,0:T(8,128)S(1)} %broadcast_in_dim.70.rest_0_) | copy-start | bytes 49156
  74.0 1.9 %collective-permute-start.18 = (f32[8,512]{1,0:T(8,128)S(1)}, f32[8,512]{1,0:T(8,128)S(1)}, u32[]{:S(2)}, u32[]{:S(2)}) collective-permute-start(f32[8,512]{1,0:T(8,128)S(1)} %broadcast_in_dim.70.rest_0_), channel_id=1, source_target_pairs={{0,1},{1,0},{2,3},{3,2},{4,5},{5,4},{6,7},{7,6},{8,9},{9,8},{10,11... | collective-permute-start | bytes 49160 | tf_op jit(solution)/shard_map/ppermute | solution.py:30
  74.1 3.9 %collective-permute-start.19 = (f32[8,512]{1,0:T(8,128)S(1)}, f32[8,512]{1,0:T(8,128)S(1)}, u32[]{:S(2)}, u32[]{:S(2)}) collective-permute-start(f32[8,512]{1,0:T(8,128)S(1)} %broadcast_in_dim.70.rest_0_), channel_id=1, source_target_pairs={{0,2},{1,3},{2,0},{3,1},{4,6},{5,7},{6,4},{7,5},{8,10},{9,11},{10,... | collective-permute-start | bytes 49160 | tf_op jit(solution)/shard_map/ppermute | solution.py:30
  74.7 3.3 %collective-permute-start.20 = (f32[8,512]{1,0:T(8,128)S(1)}, f32[8,512]{1,0:T(8,128)S(1)}, u32[]{:S(2)}, u32[]{:S(2)}) collective-permute-start(f32[8,512]{1,0:T(8,128)S(1)} %broadcast_in_dim.70.rest_0_), channel_id=1, source_target_pairs={{0,3},{1,2},{2,1},{3,0},{4,7},{5,6},{6,5},{7,4},{8,11},{9,10},{10,... | collective-permute-start | bytes 49160 | tf_op jit(solution)/shard_map/ppermute | solution.py:30
  (8 other events, 12.6 us)

commit v2 on v1

--- a/solution.py
+++ b/solution.py
@@ -15,12 +15,15 @@
 HALF_TAPS = 13
 PIECE_ROWS = 528
 SUM_LANES = 1024
+STEP = 4
 HALF_SUM = SUM_LANES // 2
 BIAS_AT = KS * KS * GROUP - HALF_SUM
 XROWS = 208
 VMEM = pl.BlockSpec(memory_space=pltpu.VMEM)
+ANY = pl.BlockSpec(memory_space=pl.ANY)
 SMEM = pl.BlockSpec(memory_space=pltpu.SMEM)
 F32 = jnp.float32
+SMALL = pltpu.CompilerParams(vmem_limit_bytes=12 * 1024 * 1024)
 BF16 = jnp.bfloat16
 
 
@@ -38,11 +41,15 @@
 
 
 def main_kernel(
-    piece_count, near, fields, cot, above, below, far0, far1, close0, close1, *rest
+    piece_count, near, fields_far, cot_far, above, below, far0, far1, close0, close1, edge, *rest
 ):
     pieces = rest[:piece_count]
-    act, keep, send = rest[piece_count : piece_count + 3]
-    pool_l, pool_r, edges, xf, xs, xst, wc, wd, g, gd, shares = rest[piece_count + 3 :]
+    act_far, keep, send = rest[piece_count : piece_count + 3]
+    fields, cot, act, sems, pool_l, pool_r, xf, xs, xst, wc, wd, g, gd, shares = rest[piece_count + 3 :]
+    fields_in = pltpu.make_async_copy(fields_far, fields, sems.at[0])
+    cot_in = pltpu.make_async_copy(cot_far, cot, sems.at[1])
+    fields_in.start()
+    cot_in.start()
     tiles, rows, side, chans = fields.shape
     tall = rows + 2 * RIM
     cells = tiles * side
@@ -52,64 +59,6 @@
     far_odd = lax.rem(lax.div(space, 2), 2) == 1
     close_odd = lax.rem(space, 2) == 1
     share = chans // fsdp_count
-
-    zero_side = jnp.zeros((tall, RIM, LANES), F32)
-    zero_slot = 4 * tiles
-    pool_l[zero_slot] = zero_side
-    pool_r[zero_slot] = zero_side
-    for t in range(tiles):
-        lo, hi = far0[t].astype(F32), far1[t].astype(F32)
-        pool_l[tiles + t, :, :, :chans] = jnp.where(far_odd, lo, hi)
-        pool_r[2 * tiles + t, :, :, :chans] = jnp.where(far_odd, hi, lo)
-        lo = close0[t * tall : (t + 1) * tall].astype(F32)
-        hi = close1[t * tall : (t + 1) * tall].astype(F32)
-        pool_l[2 * tiles + t, :, :, :chans] = jnp.where(close_odd, lo, hi)
-        pool_r[tiles + t, :, :, :chans] = jnp.where(close_odd, hi, lo)
-    lo = close0[tiles * tall : tiles * tall + RIM].astype(F32)
-    hi = close1[tiles * tall : tiles * tall + RIM].astype(F32)
-    pool_l[tiles - 1, :RIM, :, :chans] = jnp.where(close_odd, lo, hi)
-    pool_r[3 * tiles, rows + RIM :, :, :chans] = jnp.where(close_odd, hi, lo)
-    lo = close0[tiles * tall + RIM :].astype(F32)
-    hi = close1[tiles * tall + RIM :].astype(F32)
-    edges[0, :, :, :chans] = jnp.where(close_odd, lo, hi)
-    edges[1, :, :, :chans] = jnp.where(close_odd, hi, lo)
-    edge_north = jnp.stack([edges[0, :, r, :chans] for r in range(RIM)])
-    edge_south = jnp.stack([edges[1, :, r, :chans] for r in range(RIM)])
-
-    lane = lax.broadcasted_iota(jnp.int32, (tiles, side + 16, 128), 2)
-    one_behind = jnp.where(lane == chans - 128, 1.0, 0.0).astype(F32)
-    for r in range(tall):
-        xf[r, :, :, 128:] = one_behind
-    for t in range(tiles):
-        top, bottom = above[t].astype(F32), below[t].astype(F32)
-        centre = fields[t].astype(F32)
-        for part, first in ((top, 0), (centre, RIM), (bottom, RIM + rows)):
-            length = part.shape[0]
-            pool_l[3 * tiles + t, first : first + length, :, :chans] = part[:, side - RIM :]
-            pool_r[t, first : first + length, :, :chans] = part[:, :RIM]
-        xf[RIM : RIM + rows, t, 8 : 8 + side, :chans] = centre
-        north = edge_north if t == 0 else above[t - 1].astype(F32)
-        south = edge_south if t == tiles - 1 else below[t + 1].astype(F32)
-        north = jnp.where(near[t, 0] >= 0, north, 0.0)
-        south = jnp.where(near[t, 1] >= 0, south, 0.0)
-        xf[:RIM, t, 8 : 8 + side, :chans] = jnp.where(fsdp == 0, north, top)
-        xf[RIM + rows :, t, 8 : 8 + side, :chans] = jnp.where(fsdp == fsdp_count - 1, south, bottom)
-
-    def slot(tile_id, first):
-        return jnp.where(tile_id < 0, zero_slot, jnp.clip(tile_id - first * tiles, 0, zero_slot))
-
-    for t in range(tiles):
-        for pool, column, first, beside, up, down in (
-            (pool_l, 6, space - 3, near[t, 2], near[t, 4], near[t, 6]),
-            (pool_r, 8 + side, space, near[t, 3], near[t, 5], near[t, 7]),
-        ):
-            mid = slot(beside, first)
-            top = jnp.where(fsdp == 0, slot(up, first), mid)
-            bottom = jnp.where(fsdp == fsdp_count - 1, slot(down, first), mid)
-            into = pl.ds(column, RIM)
-            xf[RIM : RIM + rows, t, into, :chans] = pool[mid, RIM : RIM + rows, :, :chans]
-            xf[:RIM, t, into, :chans] = pool[top, :RIM, :, :chans]
-            xf[RIM + rows :, t, into, :chans] = pool[bottom, RIM + rows :, :, :chans]
 
     lined = jnp.concatenate([p[...] for p in pieces], axis=1)
     owner = []
@@ -141,15 +90,75 @@
         blocks.append(jnp.zeros((LANES - chans - 8, LANES), F32))
         wd[tap * LANES : (tap + 1) * LANES] = jnp.concatenate(blocks, axis=0).astype(BF16)
 
-    @pl.loop(0, tall)
-    def _(r):
-        for b in range(KS):
-            piece = xf[r, :, 6 + b : 6 + b + side, :].astype(BF16).reshape(cells, LANES)
-            xs[r, :, b * LANES : (b + 1) * LANES] = piece
-            xst[r, b * XROWS : (b + 1) * XROWS, :] = piece.T[:XROWS]
-
-    step = min(8, rows)
+    zero_side = jnp.zeros((tall, RIM, LANES), F32)
+    zero_slot = 4 * tiles
+    pool_l[zero_slot] = zero_side
+    pool_r[zero_slot] = zero_side
+    for t in range(tiles):
+        lo, hi = far0[t].astype(F32), far1[t].astype(F32)
+        pool_l[tiles + t, :, :, :chans] = jnp.where(far_odd, lo, hi)
+        pool_r[2 * tiles + t, :, :, :chans] = jnp.where(far_odd, hi, lo)
+        lo = close0[t * tall : (t + 1) * tall].astype(F32)
+        hi = close1[t * tall : (t + 1) * tall].astype(F32)
+        pool_l[2 * tiles + t, :, :, :chans] = jnp.where(close_odd, lo, hi)
+        pool_r[tiles + t, :, :, :chans] = jnp.where(close_odd, hi, lo)
+    lo = close0[tiles * tall :].astype(F32)
+    hi = close1[tiles * tall :].astype(F32)
+    pool_l[tiles - 1, :RIM, :, :chans] = jnp.where(close_odd, lo, hi)
+    pool_r[3 * tiles, rows + RIM :, :, :chans] = jnp.where(close_odd, hi, lo)
+
+    fields_in.wait()
+
+    lane = lax.broadcasted_iota(jnp.int32, (tiles, side + 16, 128), 2)
+    one_behind = jnp.where(lane == chans - 128, 1.0, 0.0).astype(F32)
+    for r in range(tall):
+        xf[r, :, :, 128:] = one_behind
+    for t in range(tiles):
+        top, bottom = above[t].astype(F32), below[t].astype(F32)
+        centre = fields[t].astype(F32)
+        for part, first in ((top, 0), (centre, RIM), (bottom, RIM + rows)):
+            length = part.shape[0]
+            pool_l[3 * tiles + t, first : first + length, :, :chans] = part[:, side - RIM :]
+            pool_r[t, first : first + length, :, :chans] = part[:, :RIM]
+        xf[RIM : RIM + rows, t, 8 : 8 + side, :chans] = centre
+        north = edge[...].astype(F32) if t == 0 else above[t - 1].astype(F32)
+        south = edge[...].astype(F32) if t == tiles - 1 else below[t + 1].astype(F32)
+        north = jnp.where(near[t, 0] >= 0, north, 0.0)
+        south = jnp.where(near[t, 1] >= 0, south, 0.0)
+        xf[:RIM, t, 8 : 8 + side, :chans] = jnp.where(fsdp == 0, north, top)
+        xf[RIM + rows :, t, 8 : 8 + side, :chans] = jnp.where(fsdp == fsdp_count - 1, south, bottom)
+
+    def slot(tile_id, first):
+        return jnp.where(tile_id < 0, zero_slot, jnp.clip(tile_id - first * tiles, 0, zero_slot))
+
+    for t in range(tiles):
+        for pool, column, first, beside, up, down in (
+            (pool_l, 6, space - 3, near[t, 2], near[t, 4], near[t, 6]),
+            (pool_r, 8 + side, space, near[t, 3], near[t, 5], near[t, 7]),
+        ):
+            mid = slot(beside, first)
+            top = jnp.where(fsdp == 0, slot(up, first), mid)
+            bottom = jnp.where(fsdp == fsdp_count - 1, slot(down, first), mid)
+            into = pl.ds(column, RIM)
+            xf[RIM : RIM + rows, t, into, :chans] = pool[mid, RIM : RIM + rows, :, :chans]
+            xf[:RIM, t, into, :chans] = pool[top, :RIM, :, :chans]
+            xf[RIM + rows :, t, into, :chans] = pool[bottom, RIM + rows :, :, :chans]
+
+    def shift(some_rows):
+        for r in some_rows:
+            for b in range(KS):
+                piece = xf[r, :, 6 + b : 6 + b + side, :].astype(BF16).reshape(cells, LANES)
+                xs[r, :, b * LANES : (b + 1) * LANES] = piece
+                xst[r, b * XROWS : (b + 1) * XROWS, :] = piece.T[:XROWS]
+
+    cot_in.wait()
+    act_out = []
+    step = min(STEP, rows)
+    reach = step + KS - 1
+    shift(range(reach))
     for r0 in range(0, rows, step):
+        if r0 + step < rows:
+            shift(range(r0 + reach, r0 + reach + step))
         total = None
         for a in range(KS):
             left = xs[r0 + a : r0 + a + step].reshape(step * cells, KS * LANES)
@@ -165,6 +174,12 @@
             g[r0 : r0 + step, t * side : (t + 1) * side, :chans] = (
                 up * logistic * (1.0 + pre * (1.0 - logistic))
             ).astype(BF16)
+
+        chunk = pl.ds(r0, step)
+        act_out.append(
+            pltpu.make_async_copy(act.at[:, chunk], act_far.at[:, chunk], sems.at[2 + r0 // step])
+        )
+        act_out[-1].start()
 
     right = g[...].reshape(rows * cells, LANES)
     for a in range(KS):
@@ -188,6 +203,8 @@
             low, high = shares[whose, :, :HALF_SUM], shares[whose, :, HALF_SUM:]
             into[i, 0] = jnp.where(close_odd, high, low)
             into[i, 1] = jnp.where(close_odd, low, high)
+    for copy in act_out:
+        copy.wait()
 
 
 def bias_lane(shape, half, at):
@@ -223,23 +240,42 @@
     bias_out[...] = turned[count : count + 1, :share]
 
 
-def pack_kernel(fields, weight, bias, rows_outward, rows_core, packed, west, east, wide):
-    tiles, rows, side, chans = fields.shape
-    share = weight.shape[2]
+def rim_kernel(
+    fields, ends_outward, ends_core, rows_outward, rows_core, west, east, rims, sides, sems
+):
+    rows, side = fields.shape[1:3]
     even = lax.rem(lax.axis_index("fsdp"), 2) == 0
+    copies = [
+        pltpu.make_async_copy(fields.at[:, pl.ds(0, RIM)], rims.at[0], sems.at[0]),
+        pltpu.make_async_copy(fields.at[:, pl.ds(rows - RIM, RIM)], rims.at[1], sems.at[1]),
+        pltpu.make_async_copy(fields.at[:, :, pl.ds(0, 16)], sides.at[0], sems.at[2]),
+        pltpu.make_async_copy(fields.at[:, :, pl.ds(side - 16, 16)], sides.at[1], sems.at[3]),
+    ]
+    for copy in copies:
+        copy.start()
+    for copy in copies:
+        copy.wait()
+
+    def give(first_ends, first_rows, last_ends, last_rows):
+        for i, (ends, outer) in enumerate(((first_ends, first_rows), (last_ends, last_rows))):
+            outer[...] = rims[i]
+            ends[:, :, :RIM] = rims[i, :, :, :RIM]
+            ends[:, :, RIM:] = rims[i, :, :, side - RIM :]
 
     @pl.when(even)
     def _():
-        rows_outward[...] = fields[:, :RIM]
-        rows_core[...] = fields[:, rows - RIM :]
+        give(ends_outward, rows_outward, ends_core, rows_core)
 
     @pl.when(jnp.logical_not(even))
     def _():
-        rows_core[...] = fields[:, :RIM]
-        rows_outward[...] = fields[:, rows - RIM :]
-
-    west[...] = fields[:, :, :RIM]
-    east[...] = fields[:, :, side - RIM :]
+        give(ends_core, rows_core, ends_outward, rows_outward)
+
+    west[...] = sides[0, :, :, :RIM]
+    east[...] = sides[1, :, :, 16 - RIM :]
+
+
+def pack_kernel(weight, bias, packed, wide):
+    share = weight.shape[2]
     high = KS * KS - HALF_TAPS
     wide[...] = jnp.zeros(wide.shape, F32)
     wide[: HALF_TAPS * GROUP, :share] = weight[:HALF_TAPS].astype(F32).reshape(-1, share)
@@ -259,7 +295,6 @@
     tall = rows + 2 * RIM
 
     even = fsdp % 2 == 0
-    first_rows, last_rows = fields[:, :RIM], fields[:, rows - RIM :]
 
     def outward(i):
         return (i + 1) % fsdp_count if i % 2 else (i - 1) % fsdp_count
@@ -271,20 +306,33 @@
     def inward(i):
         return i ^ 1
 
-    first_ends = jnp.concatenate([first_rows[:, :, :RIM], first_rows[:, :, side - RIM :]], 2)
-    last_ends = jnp.concatenate([last_rows[:, :, :RIM], last_rows[:, :, side - RIM :]], 2)
-    ends_outward = swapped(jnp.where(even, first_ends, last_ends), "fsdp", outward)
-    ends_core = swapped(jnp.where(even, last_ends, first_ends), "fsdp", inward)
+    ends = jax.ShapeDtypeStruct((tiles, RIM, 2 * RIM, chans), BF16)
     rim = jax.ShapeDtypeStruct((tiles, RIM, side, chans), BF16)
     columns = jax.ShapeDtypeStruct((tiles, rows, RIM, chans), BF16)
-    rows_outward, rows_core, packed, west_own, east_own = pl.pallas_call(
+    ends_outward, ends_core, rows_outward, rows_core, west_own, east_own = pl.pallas_call(
+        rim_kernel,
+        out_shape=(ends, ends, rim, rim, columns, columns),
+        in_specs=[ANY],
+        out_specs=(VMEM,) * 6,
+        scratch_shapes=[
+            pltpu.VMEM((2, tiles, RIM, side, chans), BF16),
+            pltpu.VMEM((2, tiles, rows, 16, chans), BF16),
+            pltpu.SemaphoreType.DMA((4,)),
+        ],
+        compiler_params=SMALL,
+        name="rims",
+    )(fields)
+    packed = pl.pallas_call(
         pack_kernel,
-        out_shape=(rim, rim, jax.ShapeDtypeStruct((PIECE_ROWS, 128), BF16), columns, columns),
-        in_specs=[VMEM] * 3,
-        out_specs=(VMEM,) * 5,
+        out_shape=jax.ShapeDtypeStruct((PIECE_ROWS, 128), BF16),
+        in_specs=[VMEM] * 2,
+        out_specs=VMEM,
         scratch_shapes=[pltpu.VMEM((PIECE_ROWS, 128), F32)],
+        compiler_params=SMALL,
         name="pack",
-    )(fields, weight.reshape(taps, GROUP, share), bias[None, :])
+    )(weight.reshape(taps, GROUP, share), bias[None, :])
+    ends_outward = swapped(ends_outward, "fsdp", outward)
+    ends_core = swapped(ends_core, "fsdp", inward)
     from_outward = swapped(rows_outward, "fsdp", outward)
     from_core = swapped(rows_core, "fsdp", inward)
     if fsdp_count == 4:
@@ -299,16 +347,23 @@
     far0 = hop_pairs(jnp.where(far_odd, west, east), 2, 0)
     far1 = hop_pairs(jnp.where(far_odd, east, west), 2, 1)
     if fsdp_count == 4:
-        far0, packed_out = lax.optimization_barrier((far0, packed_out))
+        far1, packed_out = lax.optimization_barrier((far1, packed_out))
         packed_last = swapped(packed_out, "fsdp", inward)
+    far1, from_outward, from_core = lax.optimization_barrier((far1, from_outward, from_core))
     above, below = joined(from_outward, from_core)
     east_far = jnp.where(far_odd, far0, far1)[tiles - 1, :RIM]
     west_far = jnp.where(far_odd, far1, far0)[0, rows + RIM :]
     flat_side = (tiles * tall, RIM, chans)
-    edge_east = jnp.swapaxes(above[tiles - 1], 0, 1)
-    edge_west = jnp.swapaxes(below[0], 0, 1)
-    to_east = jnp.concatenate([east.reshape(flat_side), east_far, edge_east], 0)
-    to_west = jnp.concatenate([west.reshape(flat_side), west_far, edge_west], 0)
+    last_row = fsdp_count - 1
+    edge_pairs = [(i * fsdp_count, (i + 1) * fsdp_count) for i in range(space_count - 1)]
+    edge_pairs += [
+        ((i + 1) * fsdp_count + last_row, i * fsdp_count + last_row) for i in range(space_count - 1)
+    ]
+    edge = lax.ppermute(
+        jnp.where(fsdp == 0, above[tiles - 1], below[0]), ("space", "fsdp"), edge_pairs
+    )
+    to_east = jnp.concatenate([east.reshape(flat_side), east_far], 0)
+    to_west = jnp.concatenate([west.reshape(flat_side), west_far], 0)
     close0 = hop_pairs(jnp.where(close_odd, to_west, to_east), 1, 0)
     close1 = hop_pairs(jnp.where(close_odd, to_east, to_west), 1, 1)
     if fsdp_count == 4:
@@ -322,12 +377,15 @@
     activations, keep, send = pl.pallas_call(
         functools.partial(main_kernel, len(pieces)),
         out_shape=(jax.ShapeDtypeStruct(fields.shape, BF16), part, part),
-        in_specs=[SMEM] + [VMEM] * (8 + len(pieces)),
-        out_specs=(VMEM, VMEM, VMEM),
+        in_specs=[SMEM, ANY, ANY] + [VMEM] * (7 + len(pieces)),
+        out_specs=(ANY, VMEM, VMEM),
         scratch_shapes=[
+            pltpu.VMEM(fields.shape, BF16),
+            pltpu.VMEM(fields.shape, BF16),
+            pltpu.VMEM(fields.shape, BF16),
+            pltpu.SemaphoreType.DMA((2 + rows // min(STEP, rows),)),
             pltpu.VMEM((4 * tiles + 1, tall, RIM, LANES), F32),
             pltpu.VMEM((4 * tiles + 1, tall, RIM, LANES), F32),
-            pltpu.VMEM((2, side, RIM, LANES), F32),
             pltpu.VMEM((tall, tiles, side + 16, LANES), F32),
             pltpu.VMEM((tall, cells, KS * LANES), BF16),
             pltpu.VMEM((tall, KS * XROWS, cells), BF16),
@@ -341,7 +399,7 @@
         name="section",
     )(
         neighbours, fields, cotangent, above, below,
-        far0, far1, close0, close1, *pieces,
+        far0, far1, close0, close1, edge, *pieces,
     )
 
     held = keep + swapped(send, "fsdp", lambda i: i ^ 1)
@@ -365,21 +423,25 @@
     exact = total[:, BIAS_AT : BIAS_AT + 1] + total[:, BIAS_AT + 1 : BIAS_AT + 2]
     total = jnp.where(bias_lane(total.shape, half, BIAS_AT), exact, total)
     total = jnp.where(bias_lane(total.shape, half, BIAS_AT + 1), 0.0, total)
+    squares = jnp.broadcast_to(jnp.sum(total * total, 0, keepdims=True), (8, HALF_SUM))
+    squares_beside = swapped(squares, "space", lambda i: i ^ 1)
+    squares_beside, total = lax.optimization_barrier((squares_beside, total))
     total_beside = swapped(total, "space", lambda i: i ^ 1)
-
-    squares = jnp.sum(total * total, 0, keepdims=True) + jnp.sum(total_beside * total_beside, 0, keepdims=True)
-    squares = jnp.broadcast_to(squares, (8, HALF_SUM))
-    all_squares = [squares] + [
-        swapped(squares, "fsdp", lambda i, k=k: i ^ k) for k in range(1, fsdp_count)
-    ]
+    squares = squares + squares_beside
+    distance = 1
+    while distance * 2 < fsdp_count:
+        squares = squares + swapped(squares, "fsdp", lambda i: i ^ distance)
+        distance *= 2
+    all_squares = [squares, swapped(squares, "fsdp", lambda i: i ^ distance)]
     weight_step, bias_step = pl.pallas_call(
         functools.partial(scale_kernel, taps * GROUP * chans + chans),
         out_shape=(
             jax.ShapeDtypeStruct((KS, KS, GROUP, share), F32),
             jax.ShapeDtypeStruct((1, share), F32),
         ),
-        in_specs=[VMEM] * (2 + fsdp_count),
+        in_specs=[VMEM] * 4,
         out_specs=(VMEM, VMEM),
+        compiler_params=SMALL,
         name="scale",
     )(total, total_beside, *all_squares)
     return (activations, weight_step, bias_step[0])

time: 81.7 us -> 75.5 us (0.924)
  Pallas kernels: 23.1 us -> 17.6 us
  starting transfers between devices: 25.9 us -> 28.7 us
  local copies, waits for them, and re-layouts: 4.1 us -> 1.93 us
    ppermute x0 -> x1, starting transfers between devices: none -> 3.43 us  [per_device(): lax.ppermute(jnp.where(fsdp == 0, above[tiles - 1], below[0]), ('space',...]
    pallas_call x1, Pallas kernels: 18.8 us -> 16 us  [per_device(): pl.pallas_call(functools.partial(main_kernel, len(pieces)), out_shape=(ja...]
    pallas_call x1 -> x2, Pallas kernels: 2.18 us -> 0.42 us  [the longest x1 0.3 us: per_device(): pl.pallas_call(rim_kernel, out_shape=(ends, ends, rim, rim, columns, colu...]
    pallas_call x2 -> x0, local copies, waits for them, and re-layouts: 1.21 us -> none  [per_device(): pl.pallas_call(pack_kernel, out_shape=(rim, rim, jax.ShapeDtypeStruct((PI...]
    pallas_call x1, Pallas kernels: 2.07 us -> 1.09 us  [per_device(): pl.pallas_call(functools.partial(scale_kernel, taps * GROUP * chans + cha...]
    unnamed x22 -> x8, local copies, waits for them, and re-layouts: 1.92 us -> 1.88 us
  transfers between devices with their start and end apart: 21 -> 22, of which waited for: 9 -> 11; matrix products, arithmetic and copies ran while one was open for 2% -> 1% of each run, Pallas kernels for 3% -> 0%
where the time goes in v2:
time: 75.5 us; the launch traced here: 75.2 us
  starting transfers between devices  28.7 us (38%)
  waiting for transfers between devices  24.8 us (33%)
  Pallas kernels  17.6 us (23%)
  local copies, waits for them, and re-layouts  1.93 us (3%)
  other arithmetic  1.39 us (2%)
  between operations  0.91 us (1%)
    ppermute x21, starting transfers between devices, swapped(): return lax.ppermute(value, axis, [p for p in pairs if 0 <= p[1] < count])  25.3 us
    ppermute x21, waiting for transfers between devices, swapped(): return lax.ppermute(value, axis, [p for p in pairs if 0 <= p[1] < count])  24.8 us
    pallas_call x1, Pallas kernels, per_device(): pl.pallas_call(functools.partial(main_kernel, len(pieces)), out_shape=(ja...  16 us
    ppermute x1, starting transfers between devices, per_device(): lax.ppermute(jnp.where(fsdp == 0, above[tiles - 1], below[0]), ('space',...  3.43 us
    unnamed x8, local copies, waits for them, and re-layouts  1.88 us
  transfers between devices with their start and end apart: 22, of which 11 were waited for; matrix products, arithmetic and copies ran while one was open for 1% of the time, Pallas kernels for 0%

profile of v2, /device:TPU:0, one launch (start us, length us, event | category | flops | bytes accessed | tf_op | source)
XLA Modules:
  0.0 75.2 jit_solution(6101549961080375045)
XLA Ops:
  0.6 1.2 %copy-done = bf16[2,16,64,200]{3,2,1,0:T(8,128)(2,1)S(1)} copy-done((bf16[2,16,64,200]{3,2,1,0:T(8,128)(2,1)S(1)}, bf16[2,16,64,200]{3,2,1,0:T(8,128)(2,1)}, u32[]{:S(2)}) %copy-start) | copy-done | bytes 819224
  2.2 2.4 %collective-permute-start = (bf16[2,2,4,200]{3,2,1,0:T(4,128)(2,1)S(1)}, bf16[2,2,4,200]{3,2,1,0:T(4,128)(2,1)S(1)}, u32[]{:S(2)}, u32[]{:S(2)}) collective-permute-start(bf16[2,2,4,200]{3,2,1,0:T(4,128)(2,1)S(1)} %get-tuple-element.21), channel_id=1, source_target_pairs={{0,3},{1,2},{2,1},{3,0},{4,7},{5,6},{6,5},{7,4},{8,11},{9,10},{10,... | collective-permute-start | bytes 19208 | tf_op jit(solution)/shard_map/ppermute | solution.py:33
  4.6 0.7 collective-permute-start.1
  5.3 0.7 copy-done.3
  6.2 1.7 %collective-permute-start.4 = (bf16[2,2,64,200]{3,2,1,0:T(8,128)(2,1)S(1)}, bf16[2,2,64,200]{3,2,1,0:T(8,128)(2,1)S(1)}, u32[]{:S(2)}, u32[]{:S(2)}) collective-permute-start(bf16[2,2,64,200]{3,2,1,0:T(8,128)(2,1)S(1)} %get-tuple-element.26), channel_id=1, source_target_pairs={{0,3},{1,2},{2,1},{3,0},{4,7},{5,6},{6,5},{7,4},{8,11},{9,10},{10,... | collective-permute-start | bytes 307208 | tf_op jit(solution)/shard_map/ppermute | solution.py:33
  8.1 0.7 collective-permute-start.2
  9.4 6.2 %collective-permute-start.6 = (bf16[2,20,2,200]{3,2,1,0:T(2,128)(2,1)S(1)}, bf16[2,20,2,200]{3,2,1,0:T(2,128)(2,1)S(1)}, u32[]{:S(2)}, u32[]{:S(2)}) collective-permute-start(bf16[2,20,2,200]{3,2,1,0:T(2,128)(2,1)S(1)} %get-tuple-element.45), channel_id=1, source_target_pairs={{0,8},{4,12},{8,0},{12,4},{16,24},{20,28},{24,16},{28,20},{1,9},{5... | collective-permute-start | bytes 96008 | tf_op jit(solution)/shard_map/ppermute | solution.py:33
  15.7 3.4 %collective-permute-start.9 = (bf16[2,64,200]{2,1,0:T(8,128)(2,1)S(1)}, bf16[2,64,200]{2,1,0:T(8,128)(2,1)S(1)}, u32[]{:S(2)}, u32[]{:S(2)}) collective-permute-start(bf16[2,64,200]{2,1,0:T(8,128)(2,1)S(1)} %fusion.2), channel_id=1, source_target_pairs={{0,4},{4,8},{8,12},{12,16},{16,20},{20,24},{24,28},{7,3},{11,7},{1... | collective-permute-start | bytes 153608 | tf_op jit(solution)/shard_map/ppermute | solution.py:362
  20.0 0.7 collective-permute-start.8
  20.6 2.8 %collective-permute-done.7.close0 = bf16[42,2,200]{2,1,0:T(2,128)(2,1)S(1)} collective-permute-done((bf16[42,2,200]{2,1,0:T(2,128)(2,1)S(1)}, bf16[42,2,200]{2,1,0:T(2,128)(2,1)S(1)}, u32[]{:S(2)}, u32[]{:S(2)}) %collective-permute-start.7) | collective-permute-done | bytes 33632 | tf_op jit(solution)/shard_map/ppermute | solution.py:33
  23.5 16.0 %section.1 = (bf16[2,16,64,200]{3,2,1,0:T(8,128)(2,1)}, f32[2,2,50,512]{3,2,1,0:T(8,128)S(1)}, f32[2,2,50,512]{3,2,1,0:T(8,128)S(1)}) custom-call(s32[2,8]{1,0:T(2,128)S(1)} %copy-done.2, bf16[2,16,64,200]{3,2,1,0:T(8,128)(2,1)} %fields_far.1, bf16[2,16,64,200]{3,2,1,0:T(8,128)(2,1)} %cot_far.1, bf16[2,2,64,200]{3,2,1,0:T(8,128)(2,1)S(1)} %get-tuple-element.49.above, ...), custom_call_target="tpu_custom_call" | custom-call | tf_op jit(solution)/shard_map/section/pallas_call | solution.py:377
  39.6 1.8 %collective-permute-done.12 = f32[2,2,50,512]{3,2,1,0:T(8,128)S(1)} collective-permute-done((f32[2,2,50,512]{3,2,1,0:T(8,128)S(1)}, f32[2,2,50,512]{3,2,1,0:T(8,128)S(1)}, u32[]{:S(2)}, u32[]{:S(2)}) %collective-permute-start.12) | collective-permute-done | bytes 409632 | tf_op jit(solution)/shard_map/ppermute | solution.py:33
  41.9 5.2 %collective-permute-done.13 = bf16[1,2,50,512]{3,2,1,0:T(8,128)(2,1)S(1)} collective-permute-done((bf16[1,2,50,512]{3,2,1,0:T(8,128)(2,1)S(1)}, bf16[1,2,50,512]{3,2,1,0:T(8,128)(2,1)S(1)}, u32[]{:S(2)}, u32[]{:S(2)}) %collective-permute-start.13) | collective-permute-done | bytes 102432 | tf_op jit(solution)/shard_map/ppermute | solution.py:33
  47.1 4.9 %collective-permute-start.14 = (f32[50,512]{1,0:T(8,128)S(1)}, f32[50,512]{1,0:T(8,128)S(1)}, u32[]{:S(2)}, u32[]{:S(2)}) collective-permute-start(f32[50,512]{1,0:T(8,128)S(1)} %slice_bitcast_fusion.2), channel_id=1, source_target_pairs={{0,4},{4,0},{8,12},{12,8},{16,20},{20,16},{24,28},{28,24},{1,5},{5... | collective-permute-start | bytes 307208 | tf_op jit(solution)/shard_map/ppermute | solution.py:33
  52.0 2.8 %collective-permute-done.14 = f32[50,512]{1,0:T(8,128)S(1)} collective-permute-done((f32[50,512]{1,0:T(8,128)S(1)}, f32[50,512]{1,0:T(8,128)S(1)}, u32[]{:S(2)}, u32[]{:S(2)}) %collective-permute-start.14) | collective-permute-done | bytes 102432 | tf_op jit(solution)/shard_map/ppermute | solution.py:33
  55.0 2.2 %collective-permute-start.15 = (bf16[50,512]{1,0:T(8,128)(2,1)S(1)}, bf16[50,512]{1,0:T(8,128)(2,1)S(1)}, u32[]{:S(2)}, u32[]{:S(2)}) collective-permute-start(bf16[50,512]{1,0:T(8,128)(2,1)S(1)} %select_convert_fusion.1), channel_id=1, source_target_pairs={{0,8},{4,12},{8,0},{12,4},{16,24},{20,28},{24,16},{28,20},{1,9},{5... | collective-permute-start | bytes 153608 | tf_op jit(solution)/shard_map/ppermute | solution.py:33
  57.2 1.1 %collective-permute-start.16 = (bf16[50,512]{1,0:T(8,128)(2,1)S(1)}, bf16[50,512]{1,0:T(8,128)(2,1)S(1)}, u32[]{:S(2)}, u32[]{:S(2)}) collective-permute-start(bf16[50,512]{1,0:T(8,128)(2,1)S(1)} %select_convert_fusion.1), channel_id=1, source_target_pairs={{0,16},{4,20},{8,24},{12,28},{16,0},{20,4},{24,8},{28,12},{1,17},{... | collective-permute-start | bytes 153608 | tf_op jit(solution)/shard_map/ppermute | solution.py:33
  58.4 1.4 %collective-permute-start.17 = (bf16[50,512]{1,0:T(8,128)(2,1)S(1)}, bf16[50,512]{1,0:T(8,128)(2,1)S(1)}, u32[]{:S(2)}, u32[]{:S(2)}) collective-permute-start(bf16[50,512]{1,0:T(8,128)(2,1)S(1)} %select_convert_fusion.1), channel_id=1, source_target_pairs={{0,24},{4,28},{8,16},{12,20},{16,8},{20,12},{24,0},{28,4},{1,25},{... | collective-permute-start | bytes 153608 | tf_op jit(solution)/shard_map/ppermute | solution.py:33
  59.8 3.2 %collective-permute-done.16 = bf16[50,512]{1,0:T(8,128)(2,1)S(1)} collective-permute-done((bf16[50,512]{1,0:T(8,128)(2,1)S(1)}, bf16[50,512]{1,0:T(8,128)(2,1)S(1)}, u32[]{:S(2)}, u32[]{:S(2)}) %collective-permute-start.16) | collective-permute-done | bytes 51232 | tf_op jit(solution)/shard_map/ppermute | solution.py:33
  62.9 1.5 %collective-permute-done.17 = bf16[50,512]{1,0:T(8,128)(2,1)S(1)} collective-permute-done((bf16[50,512]{1,0:T(8,128)(2,1)S(1)}, bf16[50,512]{1,0:T(8,128)(2,1)S(1)}, u32[]{:S(2)}, u32[]{:S(2)}) %collective-permute-start.17) | collective-permute-done | bytes 51232 | tf_op jit(solution)/shard_map/ppermute | solution.py:33
  65.3 3.2 %collective-permute-done.18 = f32[8,512]{1,0:T(8,128)S(1)} collective-permute-done((f32[8,512]{1,0:T(8,128)S(1)}, f32[8,512]{1,0:T(8,128)S(1)}, u32[]{:S(2)}, u32[]{:S(2)}) %collective-permute-start.18) | collective-permute-done | bytes 16416 | tf_op jit(solution)/shard_map/ppermute | solution.py:33
  69.8 0.7 collective-permute-start.21
  70.5 3.0 %collective-permute-done.21.rest_1_ = f32[8,512]{1,0:T(8,128)S(1)} collective-permute-done((f32[8,512]{1,0:T(8,128)S(1)}, f32[8,512]{1,0:T(8,128)S(1)}, u32[]{:S(2)}, u32[]{:S(2)}) %collective-permute-start.21) | collective-permute-done | bytes 16416 | tf_op jit(solution)/shard_map/ppermute | solution.py:33
  74.1 1.1 %scale.1 = (f32[5,5,40,50]{3,2,1,0:T(8,128)}, f32[1,50]{1,0:T(1,128)}) custom-call(f32[50,512]{1,0:T(8,128)S(1)} %get-tuple-element.35.own, f32[50,512]{1,0:T(8,128)S(1)} %collective-permute-done.19.beside, f32[8,512]{1,0:T(8,128)S(1)} %fusion.13.rest_0_, f32[8,512]{1,0:T(8,128)S(1)} %collective-permute-done.21.rest_1_), custom_call_target="tpu_custom_call" | custom-call | tf_op jit(solution)/shard_map/scale/pallas_call | solution.py:436
  (58 shorter events, 5.9 us)
Async XLA Ops:
  1.9 3.4 %copy-start.1 = (bf16[5,5,40,50]{3,2,1,0:T(8,128)(2,1)S(1)}, bf16[5,5,40,50]{3,2,1,0:T(8,128)(2,1)}, u32[]{:S(2)}) copy-start(bf16[5,5,40,50]{3,2,1,0:T(8,128)(2,1)} %param.6) | copy-start | bytes 300004
  2.2 5.7 %collective-permute-start = (bf16[2,2,4,200]{3,2,1,0:T(4,128)(2,1)S(1)}, bf16[2,2,4,200]{3,2,1,0:T(4,128)(2,1)S(1)}, u32[]{:S(2)}, u32[]{:S(2)}) collective-permute-start(bf16[2,2,4,200]{3,2,1,0:T(4,128)(2,1)S(1)} %get-tuple-element.21), channel_id=1, source_target_pairs={{0,3},{1,2},{2,1},{3,0},{4,7},{5,6},{6,5},{7,4},{8,11},{9,10},{10,... | collective-permute-start | bytes 19208 | tf_op jit(solution)/shard_map/ppermute | solution.py:33
  4.6 3.3 %collective-permute-start.1 = (bf16[2,2,4,200]{3,2,1,0:T(4,128)(2,1)S(1)}, bf16[2,2,4,200]{3,2,1,0:T(4,128)(2,1)S(1)}, u32[]{:S(2)}, u32[]{:S(2)}) collective-permute-start(bf16[2,2,4,200]{3,2,1,0:T(4,128)(2,1)S(1)} %get-tuple-element.22), channel_id=1, source_target_pairs={{0,1},{1,0},{2,3},{3,2},{4,5},{5,4},{6,7},{7,6},{8,9},{9,8},{10,11... | collective-permute-start | bytes 19208 | tf_op jit(solution)/shard_map/ppermute | solution.py:33
  6.1 9.5 %collective-permute-start.3 = (bf16[528,128]{1,0:T(8,128)(2,1)S(1)}, bf16[528,128]{1,0:T(8,128)(2,1)S(1)}, u32[]{:S(2)}, u32[]{:S(2)}) collective-permute-start(bf16[528,128]{1,0:T(8,128)(2,1)S(1)} %pack.1.rest_0_), channel_id=1, source_target_pairs={{0,3},{1,2},{2,1},{3,0},{4,7},{5,6},{6,5},{7,4},{8,11},{9,10},{10,... | collective-permute-start | bytes 405512 | tf_op jit(solution)/shard_map/ppermute | solution.py:33
  6.2 9.4 %collective-permute-start.4 = (bf16[2,2,64,200]{3,2,1,0:T(8,128)(2,1)S(1)}, bf16[2,2,64,200]{3,2,1,0:T(8,128)(2,1)S(1)}, u32[]{:S(2)}, u32[]{:S(2)}) collective-permute-start(bf16[2,2,64,200]{3,2,1,0:T(8,128)(2,1)S(1)} %get-tuple-element.26), channel_id=1, source_target_pairs={{0,3},{1,2},{2,1},{3,0},{4,7},{5,6},{6,5},{7,4},{8,11},{9,10},{10,... | collective-permute-start | bytes 307208 | tf_op jit(solution)/shard_map/ppermute | solution.py:33
  7.9 7.7 %collective-permute-start.5 = (bf16[2,2,64,200]{3,2,1,0:T(8,128)(2,1)S(1)}, bf16[2,2,64,200]{3,2,1,0:T(8,128)(2,1)S(1)}, u32[]{:S(2)}, u32[]{:S(2)}) collective-permute-start(bf16[2,2,64,200]{3,2,1,0:T(8,128)(2,1)S(1)} %get-tuple-element.27), channel_id=1, source_target_pairs={{0,1},{1,0},{2,3},{3,2},{4,5},{5,4},{6,7},{7,6},{8,9},{9,8},{10,11... | collective-permute-start | bytes 307208 | tf_op jit(solution)/shard_map/ppermute | solution.py:33
  8.1 1.2 %collective-permute-start.2 = (bf16[2,20,2,200]{3,2,1,0:T(2,128)(2,1)S(1)}, bf16[2,20,2,200]{3,2,1,0:T(2,128)(2,1)S(1)}, u32[]{:S(2)}, u32[]{:S(2)}) collective-permute-start(bf16[2,20,2,200]{3,2,1,0:T(2,128)(2,1)S(1)} %bitcast.46), channel_id=1, source_target_pairs={{8,16},{12,20},{16,8},{20,12},{9,17},{13,21},{17,9},{21,13},{10,18... | collective-permute-start | bytes 96008 | tf_op jit(solution)/shard_map/ppermute | solution.py:33
  8.8 11.9 %collective-permute-start.10 = (bf16[528,128]{1,0:T(8,128)(2,1)S(1)}, bf16[528,128]{1,0:T(8,128)(2,1)S(1)}, u32[]{:S(2)}, u32[]{:S(2)}) collective-permute-start(bf16[528,128]{1,0:T(8,128)(2,1)S(1)} %pack.1.rest_0_), channel_id=1, source_target_pairs={{0,1},{1,0},{2,3},{3,2},{4,5},{5,4},{6,7},{7,6},{8,9},{9,8},{10,11... | collective-permute-start | bytes 405512 | tf_op jit(solution)/shard_map/ppermute | solution.py:33
  9.4 9.8 %collective-permute-start.6 = (bf16[2,20,2,200]{3,2,1,0:T(2,128)(2,1)S(1)}, bf16[2,20,2,200]{3,2,1,0:T(2,128)(2,1)S(1)}, u32[]{:S(2)}, u32[]{:S(2)}) collective-permute-start(bf16[2,20,2,200]{3,2,1,0:T(2,128)(2,1)S(1)} %get-tuple-element.45), channel_id=1, source_target_pairs={{0,8},{4,12},{8,0},{12,4},{16,24},{20,28},{24,16},{28,20},{1,9},{5... | collective-permute-start | bytes 96008 | tf_op jit(solution)/shard_map/ppermute | solution.py:33
  15.7 7.8 %collective-permute-start.9 = (bf16[2,64,200]{2,1,0:T(8,128)(2,1)S(1)}, bf16[2,64,200]{2,1,0:T(8,128)(2,1)S(1)}, u32[]{:S(2)}, u32[]{:S(2)}) collective-permute-start(bf16[2,64,200]{2,1,0:T(8,128)(2,1)S(1)} %fusion.2), channel_id=1, source_target_pairs={{0,4},{4,8},{8,12},{12,16},{16,20},{20,24},{24,28},{7,3},{11,7},{1... | collective-permute-start | bytes 153608 | tf_op jit(solution)/shard_map/ppermute | solution.py:362
  19.1 4.4 %collective-permute-start.11 = (bf16[528,128]{1,0:T(8,128)(2,1)S(1)}, bf16[528,128]{1,0:T(8,128)(2,1)S(1)}, u32[]{:S(2)}, u32[]{:S(2)}) collective-permute-start(bf16[528,128]{1,0:T(8,128)(2,1)S(1)} %collective-permute-done.3.rest_1_), channel_id=1, source_target_pairs={{0,1},{1,0},{2,3},{3,2},{4,5},{5,4},{6,7},{7,6},{8,9},{9,8},{10,11... | collective-permute-start | bytes 405512 | tf_op jit(solution)/shard_map/ppermute | solution.py:33
  19.3 4.1 %copy-start.2 = (s32[2,8]{1,0:T(2,128)S(1)}, s32[2,8]{1,0:T(2,128)}, u32[]{:S(2)}) copy-start(s32[2,8]{1,0:T(2,128)} %near.1) | copy-start | bytes 196
  19.4 4.1 %collective-permute-start.7 = (bf16[42,2,200]{2,1,0:T(2,128)(2,1)S(1)}, bf16[42,2,200]{2,1,0:T(2,128)(2,1)S(1)}, u32[]{:S(2)}, u32[]{:S(2)}) collective-permute-start(bf16[42,2,200]{2,1,0:T(2,128)(2,1)S(1)} %get-tuple-element.51), channel_id=1, source_target_pairs={{0,4},{4,0},{8,12},{12,8},{16,20},{20,16},{24,28},{28,24},{1,5},{5... | collective-permute-start | bytes 100808 | tf_op jit(solution)/shard_map/ppermute | solution.py:33
  20.0 3.5 %collective-permute-start.8 = (bf16[42,2,200]{2,1,0:T(2,128)(2,1)S(1)}, bf16[42,2,200]{2,1,0:T(2,128)(2,1)S(1)}, u32[]{:S(2)}, u32[]{:S(2)}) collective-permute-start(bf16[42,2,200]{2,1,0:T(2,128)(2,1)S(1)} %get-tuple-element.50), channel_id=1, source_target_pairs={{4,8},{8,4},{12,16},{16,12},{20,24},{24,20},{5,9},{9,5},{13,17},{1... | collective-permute-start | bytes 100808 | tf_op jit(solution)/shard_map/ppermute | solution.py:33
  39.5 1.9 %collective-permute-start.12 = (f32[2,2,50,512]{3,2,1,0:T(8,128)S(1)}, f32[2,2,50,512]{3,2,1,0:T(8,128)S(1)}, u32[]{:S(2)}, u32[]{:S(2)}) collective-permute-start(f32[2,2,50,512]{3,2,1,0:T(8,128)S(1)} %get-tuple-element.34), channel_id=1, source_target_pairs={{0,1},{1,0},{2,3},{3,2},{4,5},{5,4},{6,7},{7,6},{8,9},{9,8},{10,11... | collective-permute-start | bytes 1228808 | tf_op jit(solution)/shard_map/ppermute | solution.py:33
  41.8 5.3 %collective-permute-start.13 = (bf16[1,2,50,512]{3,2,1,0:T(8,128)(2,1)S(1)}, bf16[1,2,50,512]{3,2,1,0:T(8,128)(2,1)S(1)}, u32[]{:S(2)}, u32[]{:S(2)}) collective-permute-start(bf16[1,2,50,512]{3,2,1,0:T(8,128)(2,1)S(1)} %select_convert_fusion), channel_id=1, source_target_pairs={{0,2},{1,3},{2,0},{3,1},{4,6},{5,7},{6,4},{7,5},{8,10},{9,11},{10,... | collective-permute-start | bytes 307208 | tf_op jit(solution)/shard_map/ppermute | solution.py:33
  47.1 7.6 %collective-permute-start.14 = (f32[50,512]{1,0:T(8,128)S(1)}, f32[50,512]{1,0:T(8,128)S(1)}, u32[]{:S(2)}, u32[]{:S(2)}) collective-permute-start(f32[50,512]{1,0:T(8,128)S(1)} %slice_bitcast_fusion.2), channel_id=1, source_target_pairs={{0,4},{4,0},{8,12},{12,8},{16,20},{20,16},{24,28},{28,24},{1,5},{5... | collective-permute-start | bytes 307208 | tf_op jit(solution)/shard_map/ppermute | solution.py:33
  55.0 4.7 %collective-permute-start.15 = (bf16[50,512]{1,0:T(8,128)(2,1)S(1)}, bf16[50,512]{1,0:T(8,128)(2,1)S(1)}, u32[]{:S(2)}, u32[]{:S(2)}) collective-permute-start(bf16[50,512]{1,0:T(8,128)(2,1)S(1)} %select_convert_fusion.1), channel_id=1, source_target_pairs={{0,8},{4,12},{8,0},{12,4},{16,24},{20,28},{24,16},{28,20},{1,9},{5... | collective-permute-start | bytes 153608 | tf_op jit(solution)/shard_map/ppermute | solution.py:33
  57.2 5.7 %collective-permute-start.16 = (bf16[50,512]{1,0:T(8,128)(2,1)S(1)}, bf16[50,512]{1,0:T(8,128)(2,1)S(1)}, u32[]{:S(2)}, u32[]{:S(2)}) collective-permute-start(bf16[50,512]{1,0:T(8,128)(2,1)S(1)} %select_convert_fusion.1), channel_id=1, source_target_pairs={{0,16},{4,20},{8,24},{12,28},{16,0},{20,4},{24,8},{28,12},{1,17},{... | collective-permute-start | bytes 153608 | tf_op jit(solution)/shard_map/ppermute | solution.py:33
  58.4 6.1 %collective-permute-start.17 = (bf16[50,512]{1,0:T(8,128)(2,1)S(1)}, bf16[50,512]{1,0:T(8,128)(2,1)S(1)}, u32[]{:S(2)}, u32[]{:S(2)}) collective-permute-start(bf16[50,512]{1,0:T(8,128)(2,1)S(1)} %select_convert_fusion.1), channel_id=1, source_target_pairs={{0,24},{4,28},{8,16},{12,20},{16,8},{20,12},{24,0},{28,4},{1,25},{... | collective-permute-start | bytes 153608 | tf_op jit(solution)/shard_map/ppermute | solution.py:33
  64.8 3.8 %collective-permute-start.18 = (f32[8,512]{1,0:T(8,128)S(1)}, f32[8,512]{1,0:T(8,128)S(1)}, u32[]{:S(2)}, u32[]{:S(2)}) collective-permute-start(f32[8,512]{1,0:T(8,128)S(1)} %broadcast_in_dim.69), channel_id=1, source_target_pairs={{0,4},{4,0},{8,12},{12,8},{16,20},{20,16},{24,28},{28,24},{1,5},{5... | collective-permute-start | bytes 49160 | tf_op jit(solution)/shard_map/ppermute | solution.py:33
  68.6 1.2 %collective-permute-start.20 = (f32[8,512]{1,0:T(8,128)S(1)}, f32[8,512]{1,0:T(8,128)S(1)}, u32[]{:S(2)}, u32[]{:S(2)}) collective-permute-start(f32[8,512]{1,0:T(8,128)S(1)} %broadcast_add_fusion), channel_id=1, source_target_pairs={{0,1},{1,0},{2,3},{3,2},{4,5},{5,4},{6,7},{7,6},{8,9},{9,8},{10,11... | collective-permute-start | bytes 49160 | tf_op jit(solution)/shard_map/ppermute | solution.py:33
  68.6 5.6 %collective-permute-start.19 = (f32[50,512]{1,0:T(8,128)S(1)}, f32[50,512]{1,0:T(8,128)S(1)}, u32[]{:S(2)}, u32[]{:S(2)}) collective-permute-start(f32[50,512]{1,0:T(8,128)S(1)} %get-tuple-element.35.own), channel_id=1, source_target_pairs={{0,4},{4,0},{8,12},{12,8},{16,20},{20,16},{24,28},{28,24},{1,5},{5... | collective-permute-start | bytes 307208 | tf_op jit(solution)/shard_map/ppermute | solution.py:33
  69.8 3.7 %collective-permute-start.21 = (f32[8,512]{1,0:T(8,128)S(1)}, f32[8,512]{1,0:T(8,128)S(1)}, u32[]{:S(2)}, u32[]{:S(2)}) collective-permute-start(f32[8,512]{1,0:T(8,128)S(1)} %fusion.13.rest_0_), channel_id=1, source_target_pairs={{0,2},{1,3},{2,0},{3,1},{4,6},{5,7},{6,4},{7,5},{8,10},{9,11},{10,... | collective-permute-start | bytes 49160 | tf_op jit(solution)/shard_map/ppermute | solution.py:33
  (2 other events, 1.9 us)

commit v3 on v2

--- a/solution.py
+++ b/solution.py
@@ -41,11 +41,11 @@
 
 
 def main_kernel(
-    piece_count, near, fields_far, cot_far, above, below, far0, far1, close0, close1, edge, *rest
+    piece_count, near, fields_far, cot_far, above, below, far0, far1, close0, close1, *rest
 ):
     pieces = rest[:piece_count]
     act_far, keep, send = rest[piece_count : piece_count + 3]
-    fields, cot, act, sems, pool_l, pool_r, xf, xs, xst, wc, wd, g, gd, shares = rest[piece_count + 3 :]
+    fields, cot, act, sems, pool_l, pool_r, edges, xf, xs, xst, wc, wd, g, gd, shares = rest[piece_count + 3 :]
     fields_in = pltpu.make_async_copy(fields_far, fields, sems.at[0])
     cot_in = pltpu.make_async_copy(cot_far, cot, sems.at[1])
     fields_in.start()
@@ -102,11 +102,17 @@
         hi = close1[t * tall : (t + 1) * tall].astype(F32)
         pool_l[2 * tiles + t, :, :, :chans] = jnp.where(close_odd, lo, hi)
         pool_r[tiles + t, :, :, :chans] = jnp.where(close_odd, hi, lo)
-    lo = close0[tiles * tall :].astype(F32)
-    hi = close1[tiles * tall :].astype(F32)
+    lo = close0[tiles * tall : tiles * tall + RIM].astype(F32)
+    hi = close1[tiles * tall : tiles * tall + RIM].astype(F32)
     pool_l[tiles - 1, :RIM, :, :chans] = jnp.where(close_odd, lo, hi)
     pool_r[3 * tiles, rows + RIM :, :, :chans] = jnp.where(close_odd, hi, lo)
 
+    lo = close0[tiles * tall + RIM :].astype(F32)
+    hi = close1[tiles * tall + RIM :].astype(F32)
+    edges[0, :, :, :chans] = jnp.where(close_odd, lo, hi)
+    edges[1, :, :, :chans] = jnp.where(close_odd, hi, lo)
+    edge_north = jnp.stack([edges[0, :, r, :chans] for r in range(RIM)])
+    edge_south = jnp.stack([edges[1, :, r, :chans] for r in range(RIM)])
     fields_in.wait()
 
     lane = lax.broadcasted_iota(jnp.int32, (tiles, side + 16, 128), 2)
@@ -121,8 +127,8 @@
             pool_l[3 * tiles + t, first : first + length, :, :chans] = part[:, side - RIM :]
             pool_r[t, first : first + length, :, :chans] = part[:, :RIM]
         xf[RIM : RIM + rows, t, 8 : 8 + side, :chans] = centre
-        north = edge[...].astype(F32) if t == 0 else above[t - 1].astype(F32)
-        south = edge[...].astype(F32) if t == tiles - 1 else below[t + 1].astype(F32)
+        north = edge_north if t == 0 else above[t - 1].astype(F32)
+        south = edge_south if t == tiles - 1 else below[t + 1].astype(F32)
         north = jnp.where(near[t, 0] >= 0, north, 0.0)
         south = jnp.where(near[t, 1] >= 0, south, 0.0)
         xf[:RIM, t, 8 : 8 + side, :chans] = jnp.where(fsdp == 0, north, top)
@@ -347,23 +353,19 @@
     far0 = hop_pairs(jnp.where(far_odd, west, east), 2, 0)
     far1 = hop_pairs(jnp.where(far_odd, east, west), 2, 1)
     if fsdp_count == 4:
-        far1, packed_out = lax.optimization_barrier((far1, packed_out))
+        far0, far1, packed_out = lax.optimization_barrier((far0, far1, packed_out))
         packed_last = swapped(packed_out, "fsdp", inward)
-    far1, from_outward, from_core = lax.optimization_barrier((far1, from_outward, from_core))
+    far0, far1, from_outward, from_core = lax.optimization_barrier(
+        (far0, far1, from_outward, from_core)
+    )
     above, below = joined(from_outward, from_core)
     east_far = jnp.where(far_odd, far0, far1)[tiles - 1, :RIM]
     west_far = jnp.where(far_odd, far1, far0)[0, rows + RIM :]
     flat_side = (tiles * tall, RIM, chans)
-    last_row = fsdp_count - 1
-    edge_pairs = [(i * fsdp_count, (i + 1) * fsdp_count) for i in range(space_count - 1)]
-    edge_pairs += [
-        ((i + 1) * fsdp_count + last_row, i * fsdp_count + last_row) for i in range(space_count - 1)
-    ]
-    edge = lax.ppermute(
-        jnp.where(fsdp == 0, above[tiles - 1], below[0]), ("space", "fsdp"), edge_pairs
-    )
-    to_east = jnp.concatenate([east.reshape(flat_side), east_far], 0)
-    to_west = jnp.concatenate([west.reshape(flat_side), west_far], 0)
+    edge_east = jnp.swapaxes(above[tiles - 1], 0, 1)
+    edge_west = jnp.swapaxes(below[0], 0, 1)
+    to_east = jnp.concatenate([east.reshape(flat_side), east_far, edge_east], 0)
+    to_west = jnp.concatenate([west.reshape(flat_side), west_far, edge_west], 0)
     close0 = hop_pairs(jnp.where(close_odd, to_west, to_east), 1, 0)
     close1 = hop_pairs(jnp.where(close_odd, to_east, to_west), 1, 1)
     if fsdp_count == 4:
@@ -377,7 +379,7 @@
     activations, keep, send = pl.pallas_call(
         functools.partial(main_kernel, len(pieces)),
         out_shape=(jax.ShapeDtypeStruct(fields.shape, BF16), part, part),
-        in_specs=[SMEM, ANY, ANY] + [VMEM] * (7 + len(pieces)),
+        in_specs=[SMEM, ANY, ANY] + [VMEM] * (6 + len(pieces)),
         out_specs=(ANY, VMEM, VMEM),
         scratch_shapes=[
             pltpu.VMEM(fields.shape, BF16),
@@ -386,6 +388,7 @@
             pltpu.SemaphoreType.DMA((2 + rows // min(STEP, rows),)),
             pltpu.VMEM((4 * tiles + 1, tall, RIM, LANES), F32),
             pltpu.VMEM((4 * tiles + 1, tall, RIM, LANES), F32),
+            pltpu.VMEM((2, side, RIM, LANES), F32),
             pltpu.VMEM((tall, tiles, side + 16, LANES), F32),
             pltpu.VMEM((tall, cells, KS * LANES), BF16),
             pltpu.VMEM((tall, KS * XROWS, cells), BF16),
@@ -399,7 +402,7 @@
         name="section",
     )(
         neighbours, fields, cotangent, above, below,
-        far0, far1, close0, close1, edge, *pieces,
+        far0, far1, close0, close1, *pieces,
     )
 
     held = keep + swapped(send, "fsdp", lambda i: i ^ 1)
@@ -424,22 +427,29 @@
     total = jnp.where(bias_lane(total.shape, half, BIAS_AT), exact, total)
     total = jnp.where(bias_lane(total.shape, half, BIAS_AT + 1), 0.0, total)
     squares = jnp.broadcast_to(jnp.sum(total * total, 0, keepdims=True), (8, HALF_SUM))
-    squares_beside = swapped(squares, "space", lambda i: i ^ 1)
-    squares_beside, total = lax.optimization_barrier((squares_beside, total))
     total_beside = swapped(total, "space", lambda i: i ^ 1)
-    squares = squares + squares_beside
     distance = 1
     while distance * 2 < fsdp_count:
         squares = squares + swapped(squares, "fsdp", lambda i: i ^ distance)
         distance *= 2
-    all_squares = [squares, swapped(squares, "fsdp", lambda i: i ^ distance)]
+    both = [
+        (s * fsdp_count + q, (s ^ 1) * fsdp_count + (q ^ distance))
+        for s in range(space_count)
+        for q in range(fsdp_count)
+    ]
+    all_squares = [
+        squares,
+        swapped(squares, "space", lambda i: i ^ 1),
+        swapped(squares, "fsdp", lambda i: i ^ distance),
+        lax.ppermute(squares, ("space", "fsdp"), both),
+    ]
     weight_step, bias_step = pl.pallas_call(
         functools.partial(scale_kernel, taps * GROUP * chans + chans),
         out_shape=(
             jax.ShapeDtypeStruct((KS, KS, GROUP, share), F32),
             jax.ShapeDtypeStruct((1, share), F32),
         ),
-        in_specs=[VMEM] * 4,
+        in_specs=[VMEM] * 6,
         out_specs=(VMEM, VMEM),
         compiler_params=SMALL,
         name="scale",

time: 75.5 us -> 73.1 us (0.968)
  starting transfers between devices: 28.7 us -> 26.1 us
    ppermute x21, waiting for transfers between devices: 24.8 us -> 22.9 us  [swapped(): return lax.ppermute(value, axis, [p for p in pairs if 0 <= p[1] < count])]
    ppermute x1, starting transfers between devices: 3.43 us -> 2.02 us  [per_device(): lax.ppermute(squares, ('space', 'fsdp'), both)]
    ppermute x1, waiting for transfers between devices: 0.01 us -> 1.19 us  [per_device(): lax.ppermute(squares, ('space', 'fsdp'), both)]
    ppermute x21, starting transfers between devices: 25.3 us -> 24.1 us  [swapped(): return lax.ppermute(value, axis, [p for p in pairs if 0 <= p[1] < count])]
where the time goes in v3:
time: 73.1 us; the launch traced here: 72.9 us
  starting transfers between devices  26.1 us (36%)
  waiting for transfers between devices  24.1 us (33%)
  Pallas kernels  17.8 us (24%)
  local copies, waits for them, and re-layouts  2.33 us (3%)
  other arithmetic  1.58 us (2%)
  between operations  0.97 us (1%)
    ppermute x21, starting transfers between devices, swapped(): return lax.ppermute(value, axis, [p for p in pairs if 0 <= p[1] < count])  24.1 us
    ppermute x21, waiting for transfers between devices, swapped(): return lax.ppermute(value, axis, [p for p in pairs if 0 <= p[1] < count])  22.9 us
    pallas_call x1, Pallas kernels, per_device(): pl.pallas_call(functools.partial(main_kernel, len(pieces)), out_shape=(ja...  16.3 us
    ppermute x1, starting transfers between devices, per_device(): lax.ppermute(squares, ('space', 'fsdp'), both)  2.02 us
    unnamed x8, local copies, waits for them, and re-layouts  1.88 us
  transfers between devices with their start and end apart: 22, of which 11 were waited for; matrix products, arithmetic and copies ran while one was open for 1% of the time, Pallas kernels for 0%

profile of v3, /device:TPU:0, one launch (start us, length us, event | category | flops | bytes accessed | tf_op | source)
XLA Modules:
  0.0 72.9 jit_solution(11651126833058835709)
XLA Ops:
  0.6 1.2 %copy-done = bf16[2,16,64,200]{3,2,1,0:T(8,128)(2,1)S(1)} copy-done((bf16[2,16,64,200]{3,2,1,0:T(8,128)(2,1)S(1)}, bf16[2,16,64,200]{3,2,1,0:T(8,128)(2,1)}, u32[]{:S(2)}) %copy-start) | copy-done | bytes 819224
  2.2 2.4 %collective-permute-start = (bf16[2,2,4,200]{3,2,1,0:T(4,128)(2,1)S(1)}, bf16[2,2,4,200]{3,2,1,0:T(4,128)(2,1)S(1)}, u32[]{:S(2)}, u32[]{:S(2)}) collective-permute-start(bf16[2,2,4,200]{3,2,1,0:T(4,128)(2,1)S(1)} %get-tuple-element.21), channel_id=1, source_target_pairs={{0,3},{1,2},{2,1},{3,0},{4,7},{5,6},{6,5},{7,4},{8,11},{9,10},{10,... | collective-permute-start | bytes 19208 | tf_op jit(solution)/shard_map/ppermute | solution.py:33
  4.6 0.7 collective-permute-start.1
  6.3 1.7 %collective-permute-start.5 = (bf16[2,2,64,200]{3,1,2,0:T(2,128)(2,1)S(1)}, bf16[2,2,64,200]{3,1,2,0:T(2,128)(2,1)S(1)}, u32[]{:S(2)}, u32[]{:S(2)}) collective-permute-start(bf16[2,2,64,200]{3,1,2,0:T(2,128)(2,1)S(1)} %copy.12), channel_id=1, source_target_pairs={{0,3},{1,2},{2,1},{3,0},{4,7},{5,6},{6,5},{7,4},{8,11},{9,10},{10,... | collective-permute-start | bytes 307208 | tf_op jit(solution)/shard_map/ppermute | solution.py:33
  8.6 1.6 %collective-permute-start.2 = (bf16[2,20,2,200]{3,2,1,0:T(2,128)(2,1)S(1)}, bf16[2,20,2,200]{3,2,1,0:T(2,128)(2,1)S(1)}, u32[]{:S(2)}, u32[]{:S(2)}) collective-permute-start(bf16[2,20,2,200]{3,2,1,0:T(2,128)(2,1)S(1)} %bitcast.62), channel_id=1, source_target_pairs={{0,8},{4,12},{8,0},{12,4},{16,24},{20,28},{24,16},{28,20},{1,9},{5... | collective-permute-start | bytes 96008 | tf_op jit(solution)/shard_map/ppermute | solution.py:33
  10.9 1.8 %collective-permute-done.2.far0 = bf16[2,20,2,200]{3,2,1,0:T(2,128)(2,1)S(1)} collective-permute-done((bf16[2,20,2,200]{3,2,1,0:T(2,128)(2,1)S(1)}, bf16[2,20,2,200]{3,2,1,0:T(2,128)(2,1)S(1)}, u32[]{:S(2)}, u32[]{:S(2)}) %collective-permute-start.2) | collective-permute-done | bytes 32032 | tf_op jit(solution)/shard_map/ppermute | solution.py:33
  12.7 2.0 %collective-permute-done.5 = bf16[2,2,64,200]{3,1,2,0:T(2,128)(2,1)S(1)} collective-permute-done((bf16[2,2,64,200]{3,1,2,0:T(2,128)(2,1)S(1)}, bf16[2,2,64,200]{3,1,2,0:T(2,128)(2,1)S(1)}, u32[]{:S(2)}, u32[]{:S(2)}) %collective-permute-start.5) | collective-permute-done | bytes 102432 | tf_op jit(solution)/shard_map/ppermute | solution.py:33
  15.3 1.6 %collective-permute-start.7 = (bf16[106,2,200]{2,1,0:T(2,128)(2,1)S(1)}, bf16[106,2,200]{2,1,0:T(2,128)(2,1)S(1)}, u32[]{:S(2)}, u32[]{:S(2)}) collective-permute-start(bf16[106,2,200]{2,1,0:T(2,128)(2,1)S(1)} %get-tuple-element.51), channel_id=1, source_target_pairs={{0,4},{4,0},{8,12},{12,8},{16,20},{20,16},{24,28},{28,24},{1,5},{5... | collective-permute-start | bytes 254408 | tf_op jit(solution)/shard_map/ppermute | solution.py:33
  17.7 3.0 %collective-permute-done.7.close0 = bf16[106,2,200]{2,1,0:T(2,128)(2,1)S(1)} collective-permute-done((bf16[106,2,200]{2,1,0:T(2,128)(2,1)S(1)}, bf16[106,2,200]{2,1,0:T(2,128)(2,1)S(1)}, u32[]{:S(2)}, u32[]{:S(2)}) %collective-permute-start.7) | collective-permute-done | bytes 84832 | tf_op jit(solution)/shard_map/ppermute | solution.py:33
  20.7 16.3 %section.1 = (bf16[2,16,64,200]{3,2,1,0:T(8,128)(2,1)}, f32[2,2,50,512]{3,2,1,0:T(8,128)S(1)}, f32[2,2,50,512]{3,2,1,0:T(8,128)S(1)}) custom-call(s32[2,8]{1,0:T(2,128)S(1)} %copy-done.2, bf16[2,16,64,200]{3,2,1,0:T(8,128)(2,1)} %fields_far.1, bf16[2,16,64,200]{3,2,1,0:T(8,128)(2,1)} %cot_far.1, bf16[2,2,64,200]{3,2,1,0:T(8,128)(2,1)S(1)} %copy.14.above, ...), custom_call_target="tpu_custom_call" | custom-call | tf_op jit(solution)/shard_map/section/pallas_call | solution.py:379
  37.2 1.8 %collective-permute-done.11 = f32[2,2,50,512]{3,2,1,0:T(8,128)S(1)} collective-permute-done((f32[2,2,50,512]{3,2,1,0:T(8,128)S(1)}, f32[2,2,50,512]{3,2,1,0:T(8,128)S(1)}, u32[]{:S(2)}, u32[]{:S(2)}) %collective-permute-start.11) | collective-permute-done | bytes 409632 | tf_op jit(solution)/shard_map/ppermute | solution.py:33
  39.7 4.9 %collective-permute-done.12 = bf16[1,2,50,512]{3,2,1,0:T(8,128)(2,1)S(1)} collective-permute-done((bf16[1,2,50,512]{3,2,1,0:T(8,128)(2,1)S(1)}, bf16[1,2,50,512]{3,2,1,0:T(8,128)(2,1)S(1)}, u32[]{:S(2)}, u32[]{:S(2)}) %collective-permute-start.12) | collective-permute-done | bytes 102432 | tf_op jit(solution)/shard_map/ppermute | solution.py:33
  44.7 5.5 %collective-permute-start.13 = (f32[50,512]{1,0:T(8,128)S(1)}, f32[50,512]{1,0:T(8,128)S(1)}, u32[]{:S(2)}, u32[]{:S(2)}) collective-permute-start(f32[50,512]{1,0:T(8,128)S(1)} %slice_bitcast_fusion.2), channel_id=1, source_target_pairs={{0,4},{4,0},{8,12},{12,8},{16,20},{20,16},{24,28},{28,24},{1,5},{5... | collective-permute-start | bytes 307208 | tf_op jit(solution)/shard_map/ppermute | solution.py:33
  50.2 2.8 %collective-permute-done.13 = f32[50,512]{1,0:T(8,128)S(1)} collective-permute-done((f32[50,512]{1,0:T(8,128)S(1)}, f32[50,512]{1,0:T(8,128)S(1)}, u32[]{:S(2)}, u32[]{:S(2)}) %collective-permute-start.13) | collective-permute-done | bytes 102432 | tf_op jit(solution)/shard_map/ppermute | solution.py:33
  53.3 3.3 %collective-permute-start.14 = (bf16[50,512]{1,0:T(8,128)(2,1)S(1)}, bf16[50,512]{1,0:T(8,128)(2,1)S(1)}, u32[]{:S(2)}, u32[]{:S(2)}) collective-permute-start(bf16[50,512]{1,0:T(8,128)(2,1)S(1)} %select_convert_fusion.1), channel_id=1, source_target_pairs={{0,8},{4,12},{8,0},{12,4},{16,24},{20,28},{24,16},{28,20},{1,9},{5... | collective-permute-start | bytes 153608 | tf_op jit(solution)/shard_map/ppermute | solution.py:33
  56.5 1.5 %collective-permute-start.15 = (bf16[50,512]{1,0:T(8,128)(2,1)S(1)}, bf16[50,512]{1,0:T(8,128)(2,1)S(1)}, u32[]{:S(2)}, u32[]{:S(2)}) collective-permute-start(bf16[50,512]{1,0:T(8,128)(2,1)S(1)} %select_convert_fusion.1), channel_id=1, source_target_pairs={{0,16},{4,20},{8,24},{12,28},{16,0},{20,4},{24,8},{28,12},{1,17},{... | collective-permute-start | bytes 153608 | tf_op jit(solution)/shard_map/ppermute | solution.py:33
  58.1 1.4 %collective-permute-start.16 = (bf16[50,512]{1,0:T(8,128)(2,1)S(1)}, bf16[50,512]{1,0:T(8,128)(2,1)S(1)}, u32[]{:S(2)}, u32[]{:S(2)}) collective-permute-start(bf16[50,512]{1,0:T(8,128)(2,1)S(1)} %select_convert_fusion.1), channel_id=1, source_target_pairs={{0,24},{4,28},{8,16},{12,20},{16,8},{20,12},{24,0},{28,4},{1,25},{... | collective-permute-start | bytes 153608 | tf_op jit(solution)/shard_map/ppermute | solution.py:33
  59.4 2.2 %collective-permute-done.15 = bf16[50,512]{1,0:T(8,128)(2,1)S(1)} collective-permute-done((bf16[50,512]{1,0:T(8,128)(2,1)S(1)}, bf16[50,512]{1,0:T(8,128)(2,1)S(1)}, u32[]{:S(2)}, u32[]{:S(2)}) %collective-permute-start.15) | collective-permute-done | bytes 51232 | tf_op jit(solution)/shard_map/ppermute | solution.py:33
  61.6 2.5 %collective-permute-done.16 = bf16[50,512]{1,0:T(8,128)(2,1)S(1)} collective-permute-done((bf16[50,512]{1,0:T(8,128)(2,1)S(1)}, bf16[50,512]{1,0:T(8,128)(2,1)S(1)}, u32[]{:S(2)}, u32[]{:S(2)}) %collective-permute-start.16) | collective-permute-done | bytes 51232 | tf_op jit(solution)/shard_map/ppermute | solution.py:33
  65.7 0.9 %collective-permute-start.19 = (f32[8,512]{1,0:T(8,128)S(1)}, f32[8,512]{1,0:T(8,128)S(1)}, u32[]{:S(2)}, u32[]{:S(2)}) collective-permute-start(f32[8,512]{1,0:T(8,128)S(1)} %broadcast_add_fusion.rest_0_), channel_id=1, source_target_pairs={{0,4},{4,0},{8,12},{12,8},{16,20},{20,16},{24,28},{28,24},{1,5},{5... | collective-permute-start | bytes 49160 | tf_op jit(solution)/shard_map/ppermute | solution.py:33
  67.2 2.0 %collective-permute-start.21 = (f32[8,512]{1,0:T(8,128)S(1)}, f32[8,512]{1,0:T(8,128)S(1)}, u32[]{:S(2)}, u32[]{:S(2)}) collective-permute-start(f32[8,512]{1,0:T(8,128)S(1)} %broadcast_add_fusion.rest_0_), channel_id=1, source_target_pairs={{0,6},{1,7},{2,4},{3,5},{4,2},{5,3},{6,0},{7,1},{8,14},{9,15},{10,... | collective-permute-start | bytes 49160 | tf_op jit(solution)/shard_map/ppermute | solution.py:444
  69.2 1.4 %collective-permute-done.19.rest_1_ = f32[8,512]{1,0:T(8,128)S(1)} collective-permute-done((f32[8,512]{1,0:T(8,128)S(1)}, f32[8,512]{1,0:T(8,128)S(1)}, u32[]{:S(2)}, u32[]{:S(2)}) %collective-permute-start.19) | collective-permute-done | bytes 16416 | tf_op jit(solution)/shard_map/ppermute | solution.py:33
  70.6 1.2 %collective-permute-done.21.rest_3_ = f32[8,512]{1,0:T(8,128)S(1)} collective-permute-done((f32[8,512]{1,0:T(8,128)S(1)}, f32[8,512]{1,0:T(8,128)S(1)}, u32[]{:S(2)}, u32[]{:S(2)}) %collective-permute-start.21) | collective-permute-done | bytes 16416 | tf_op jit(solution)/shard_map/ppermute | solution.py:444
  71.8 1.1 %scale.1 = (f32[5,5,40,50]{3,2,1,0:T(8,128)}, f32[1,50]{1,0:T(1,128)}) custom-call(f32[50,512]{1,0:T(8,128)S(1)} %get-tuple-element.44.own, f32[50,512]{1,0:T(8,128)S(1)} %collective-permute-done.17.beside, f32[8,512]{1,0:T(8,128)S(1)} %broadcast_add_fusion.rest_0_, f32[8,512]{1,0:T(8,128)S(1)} %collective-permute-done.19.rest_1_, ...), custom_call_target="tpu_custom_call" | custom-call | tf_op jit(solution)/shard_map/scale/pallas_call | solution.py:446
  (62 shorter events, 7.1 us)
Async XLA Ops:
  1.9 3.4 %copy-start.1 = (bf16[5,5,40,50]{3,2,1,0:T(8,128)(2,1)S(1)}, bf16[5,5,40,50]{3,2,1,0:T(8,128)(2,1)}, u32[]{:S(2)}) copy-start(bf16[5,5,40,50]{3,2,1,0:T(8,128)(2,1)} %param.6) | copy-start | bytes 300004
  2.2 6.2 %collective-permute-start = (bf16[2,2,4,200]{3,2,1,0:T(4,128)(2,1)S(1)}, bf16[2,2,4,200]{3,2,1,0:T(4,128)(2,1)S(1)}, u32[]{:S(2)}, u32[]{:S(2)}) collective-permute-start(bf16[2,2,4,200]{3,2,1,0:T(4,128)(2,1)S(1)} %get-tuple-element.21), channel_id=1, source_target_pairs={{0,3},{1,2},{2,1},{3,0},{4,7},{5,6},{6,5},{7,4},{8,11},{9,10},{10,... | collective-permute-start | bytes 19208 | tf_op jit(solution)/shard_map/ppermute | solution.py:33
  4.6 3.7 %collective-permute-start.1 = (bf16[2,2,4,200]{3,2,1,0:T(4,128)(2,1)S(1)}, bf16[2,2,4,200]{3,2,1,0:T(4,128)(2,1)S(1)}, u32[]{:S(2)}, u32[]{:S(2)}) collective-permute-start(bf16[2,2,4,200]{3,2,1,0:T(4,128)(2,1)S(1)} %get-tuple-element.22), channel_id=1, source_target_pairs={{0,1},{1,0},{2,3},{3,2},{4,5},{5,4},{6,7},{7,6},{8,9},{9,8},{10,11... | collective-permute-start | bytes 19208 | tf_op jit(solution)/shard_map/ppermute | solution.py:33
  6.1 6.6 %collective-permute-start.4 = (bf16[528,128]{1,0:T(8,128)(2,1)S(1)}, bf16[528,128]{1,0:T(8,128)(2,1)S(1)}, u32[]{:S(2)}, u32[]{:S(2)}) collective-permute-start(bf16[528,128]{1,0:T(8,128)(2,1)S(1)} %pack.1.rest_0_), channel_id=1, source_target_pairs={{0,3},{1,2},{2,1},{3,0},{4,7},{5,6},{6,5},{7,4},{8,11},{9,10},{10,... | collective-permute-start | bytes 405512 | tf_op jit(solution)/shard_map/ppermute | solution.py:33
  6.3 8.3 %collective-permute-start.5 = (bf16[2,2,64,200]{3,1,2,0:T(2,128)(2,1)S(1)}, bf16[2,2,64,200]{3,1,2,0:T(2,128)(2,1)S(1)}, u32[]{:S(2)}, u32[]{:S(2)}) collective-permute-start(bf16[2,2,64,200]{3,1,2,0:T(2,128)(2,1)S(1)} %copy.12), channel_id=1, source_target_pairs={{0,3},{1,2},{2,1},{3,0},{4,7},{5,6},{6,5},{7,4},{8,11},{9,10},{10,... | collective-permute-start | bytes 307208 | tf_op jit(solution)/shard_map/ppermute | solution.py:33
  8.2 6.4 %collective-permute-start.6 = (bf16[2,2,64,200]{3,1,2,0:T(2,128)(2,1)S(1)}, bf16[2,2,64,200]{3,1,2,0:T(2,128)(2,1)S(1)}, u32[]{:S(2)}, u32[]{:S(2)}) collective-permute-start(bf16[2,2,64,200]{3,1,2,0:T(2,128)(2,1)S(1)} %copy.13), channel_id=1, source_target_pairs={{0,1},{1,0},{2,3},{3,2},{4,5},{5,4},{6,7},{7,6},{8,9},{9,8},{10,11... | collective-permute-start | bytes 307208 | tf_op jit(solution)/shard_map/ppermute | solution.py:33
  8.6 4.1 %collective-permute-start.2 = (bf16[2,20,2,200]{3,2,1,0:T(2,128)(2,1)S(1)}, bf16[2,20,2,200]{3,2,1,0:T(2,128)(2,1)S(1)}, u32[]{:S(2)}, u32[]{:S(2)}) collective-permute-start(bf16[2,20,2,200]{3,2,1,0:T(2,128)(2,1)S(1)} %bitcast.62), channel_id=1, source_target_pairs={{0,8},{4,12},{8,0},{12,4},{16,24},{20,28},{24,16},{28,20},{1,9},{5... | collective-permute-start | bytes 96008 | tf_op jit(solution)/shard_map/ppermute | solution.py:33
  10.2 2.4 %collective-permute-start.3 = (bf16[2,20,2,200]{3,2,1,0:T(2,128)(2,1)S(1)}, bf16[2,20,2,200]{3,2,1,0:T(2,128)(2,1)S(1)}, u32[]{:S(2)}, u32[]{:S(2)}) collective-permute-start(bf16[2,20,2,200]{3,2,1,0:T(2,128)(2,1)S(1)} %get-tuple-element.45), channel_id=1, source_target_pairs={{8,16},{12,20},{16,8},{20,12},{9,17},{13,21},{17,9},{21,13},{10,18... | collective-permute-start | bytes 96008 | tf_op jit(solution)/shard_map/ppermute | solution.py:33
  12.7 5.0 %collective-permute-start.9 = (bf16[528,128]{1,0:T(8,128)(2,1)S(1)}, bf16[528,128]{1,0:T(8,128)(2,1)S(1)}, u32[]{:S(2)}, u32[]{:S(2)}) collective-permute-start(bf16[528,128]{1,0:T(8,128)(2,1)S(1)} %pack.1.rest_0_), channel_id=1, source_target_pairs={{0,1},{1,0},{2,3},{3,2},{4,5},{5,4},{6,7},{7,6},{8,9},{9,8},{10,11... | collective-permute-start | bytes 405512 | tf_op jit(solution)/shard_map/ppermute | solution.py:33
  14.8 5.9 %collective-permute-start.10 = (bf16[528,128]{1,0:T(8,128)(2,1)S(1)}, bf16[528,128]{1,0:T(8,128)(2,1)S(1)}, u32[]{:S(2)}, u32[]{:S(2)}) collective-permute-start(bf16[528,128]{1,0:T(8,128)(2,1)S(1)} %collective-permute-done.4.rest_1_), channel_id=1, source_target_pairs={{0,1},{1,0},{2,3},{3,2},{4,5},{5,4},{6,7},{7,6},{8,9},{9,8},{10,11... | collective-permute-start | bytes 405512 | tf_op jit(solution)/shard_map/ppermute | solution.py:33
  15.3 5.4 %collective-permute-start.7 = (bf16[106,2,200]{2,1,0:T(2,128)(2,1)S(1)}, bf16[106,2,200]{2,1,0:T(2,128)(2,1)S(1)}, u32[]{:S(2)}, u32[]{:S(2)}) collective-permute-start(bf16[106,2,200]{2,1,0:T(2,128)(2,1)S(1)} %get-tuple-element.51), channel_id=1, source_target_pairs={{0,4},{4,0},{8,12},{12,8},{16,20},{20,16},{24,28},{28,24},{1,5},{5... | collective-permute-start | bytes 254408 | tf_op jit(solution)/shard_map/ppermute | solution.py:33
  17.0 3.8 %collective-permute-start.8 = (bf16[106,2,200]{2,1,0:T(2,128)(2,1)S(1)}, bf16[106,2,200]{2,1,0:T(2,128)(2,1)S(1)}, u32[]{:S(2)}, u32[]{:S(2)}) collective-permute-start(bf16[106,2,200]{2,1,0:T(2,128)(2,1)S(1)} %get-tuple-element.50), channel_id=1, source_target_pairs={{4,8},{8,4},{12,16},{16,12},{20,24},{24,20},{5,9},{9,5},{13,17},{1... | collective-permute-start | bytes 254408 | tf_op jit(solution)/shard_map/ppermute | solution.py:33
  17.6 3.1 %copy-start.2 = (s32[2,8]{1,0:T(2,128)S(1)}, s32[2,8]{1,0:T(2,128)}, u32[]{:S(2)}) copy-start(s32[2,8]{1,0:T(2,128)} %near.1) | copy-start | bytes 196
  37.1 1.9 %collective-permute-start.11 = (f32[2,2,50,512]{3,2,1,0:T(8,128)S(1)}, f32[2,2,50,512]{3,2,1,0:T(8,128)S(1)}, u32[]{:S(2)}, u32[]{:S(2)}) collective-permute-start(f32[2,2,50,512]{3,2,1,0:T(8,128)S(1)} %get-tuple-element.36), channel_id=1, source_target_pairs={{0,1},{1,0},{2,3},{3,2},{4,5},{5,4},{6,7},{7,6},{8,9},{9,8},{10,11... | collective-permute-start | bytes 1228808 | tf_op jit(solution)/shard_map/ppermute | solution.py:33
  39.4 5.3 %collective-permute-start.12 = (bf16[1,2,50,512]{3,2,1,0:T(8,128)(2,1)S(1)}, bf16[1,2,50,512]{3,2,1,0:T(8,128)(2,1)S(1)}, u32[]{:S(2)}, u32[]{:S(2)}) collective-permute-start(bf16[1,2,50,512]{3,2,1,0:T(8,128)(2,1)S(1)} %select_convert_fusion), channel_id=1, source_target_pairs={{0,2},{1,3},{2,0},{3,1},{4,6},{5,7},{6,4},{7,5},{8,10},{9,11},{10,... | collective-permute-start | bytes 307208 | tf_op jit(solution)/shard_map/ppermute | solution.py:33
  44.7 8.3 %collective-permute-start.13 = (f32[50,512]{1,0:T(8,128)S(1)}, f32[50,512]{1,0:T(8,128)S(1)}, u32[]{:S(2)}, u32[]{:S(2)}) collective-permute-start(f32[50,512]{1,0:T(8,128)S(1)} %slice_bitcast_fusion.2), channel_id=1, source_target_pairs={{0,4},{4,0},{8,12},{12,8},{16,20},{20,16},{24,28},{28,24},{1,5},{5... | collective-permute-start | bytes 307208 | tf_op jit(solution)/shard_map/ppermute | solution.py:33
  53.3 6.2 %collective-permute-start.14 = (bf16[50,512]{1,0:T(8,128)(2,1)S(1)}, bf16[50,512]{1,0:T(8,128)(2,1)S(1)}, u32[]{:S(2)}, u32[]{:S(2)}) collective-permute-start(bf16[50,512]{1,0:T(8,128)(2,1)S(1)} %select_convert_fusion.1), channel_id=1, source_target_pairs={{0,8},{4,12},{8,0},{12,4},{16,24},{20,28},{24,16},{28,20},{1,9},{5... | collective-permute-start | bytes 153608 | tf_op jit(solution)/shard_map/ppermute | solution.py:33
  56.5 5.1 %collective-permute-start.15 = (bf16[50,512]{1,0:T(8,128)(2,1)S(1)}, bf16[50,512]{1,0:T(8,128)(2,1)S(1)}, u32[]{:S(2)}, u32[]{:S(2)}) collective-permute-start(bf16[50,512]{1,0:T(8,128)(2,1)S(1)} %select_convert_fusion.1), channel_id=1, source_target_pairs={{0,16},{4,20},{8,24},{12,28},{16,0},{20,4},{24,8},{28,12},{1,17},{... | collective-permute-start | bytes 153608 | tf_op jit(solution)/shard_map/ppermute | solution.py:33
  58.1 6.1 %collective-permute-start.16 = (bf16[50,512]{1,0:T(8,128)(2,1)S(1)}, bf16[50,512]{1,0:T(8,128)(2,1)S(1)}, u32[]{:S(2)}, u32[]{:S(2)}) collective-permute-start(bf16[50,512]{1,0:T(8,128)(2,1)S(1)} %select_convert_fusion.1), channel_id=1, source_target_pairs={{0,24},{4,28},{8,16},{12,20},{16,8},{20,12},{24,0},{28,4},{1,25},{... | collective-permute-start | bytes 153608 | tf_op jit(solution)/shard_map/ppermute | solution.py:33
  64.5 1.2 %collective-permute-start.18 = (f32[8,512]{1,0:T(8,128)S(1)}, f32[8,512]{1,0:T(8,128)S(1)}, u32[]{:S(2)}, u32[]{:S(2)}) collective-permute-start(f32[8,512]{1,0:T(8,128)S(1)} %broadcast_in_dim.69), channel_id=1, source_target_pairs={{0,1},{1,0},{2,3},{3,2},{4,5},{5,4},{6,7},{7,6},{8,9},{9,8},{10,11... | collective-permute-start | bytes 49160 | tf_op jit(solution)/shard_map/ppermute | solution.py:33
  64.6 7.3 %collective-permute-start.17 = (f32[50,512]{1,0:T(8,128)S(1)}, f32[50,512]{1,0:T(8,128)S(1)}, u32[]{:S(2)}, u32[]{:S(2)}) collective-permute-start(f32[50,512]{1,0:T(8,128)S(1)} %get-tuple-element.44.own), channel_id=1, source_target_pairs={{0,4},{4,0},{8,12},{12,8},{16,20},{20,16},{24,28},{28,24},{1,5},{5... | collective-permute-start | bytes 307208 | tf_op jit(solution)/shard_map/ppermute | solution.py:33
  65.7 4.9 %collective-permute-start.19 = (f32[8,512]{1,0:T(8,128)S(1)}, f32[8,512]{1,0:T(8,128)S(1)}, u32[]{:S(2)}, u32[]{:S(2)}) collective-permute-start(f32[8,512]{1,0:T(8,128)S(1)} %broadcast_add_fusion.rest_0_), channel_id=1, source_target_pairs={{0,4},{4,0},{8,12},{12,8},{16,20},{20,16},{24,28},{28,24},{1,5},{5... | collective-permute-start | bytes 49160 | tf_op jit(solution)/shard_map/ppermute | solution.py:33
  66.7 4.0 %collective-permute-start.20 = (f32[8,512]{1,0:T(8,128)S(1)}, f32[8,512]{1,0:T(8,128)S(1)}, u32[]{:S(2)}, u32[]{:S(2)}) collective-permute-start(f32[8,512]{1,0:T(8,128)S(1)} %broadcast_add_fusion.rest_0_), channel_id=1, source_target_pairs={{0,2},{1,3},{2,0},{3,1},{4,6},{5,7},{6,4},{7,5},{8,10},{9,11},{10,... | collective-permute-start | bytes 49160 | tf_op jit(solution)/shard_map/ppermute | solution.py:33
  67.2 4.6 %collective-permute-start.21 = (f32[8,512]{1,0:T(8,128)S(1)}, f32[8,512]{1,0:T(8,128)S(1)}, u32[]{:S(2)}, u32[]{:S(2)}) collective-permute-start(f32[8,512]{1,0:T(8,128)S(1)} %broadcast_add_fusion.rest_0_), channel_id=1, source_target_pairs={{0,6},{1,7},{2,4},{3,5},{4,2},{5,3},{6,0},{7,1},{8,14},{9,15},{10,... | collective-permute-start | bytes 49160 | tf_op jit(solution)/shard_map/ppermute | solution.py:444
  (2 other events, 1.9 us)

commit v4 on v3

--- a/solution.py
+++ b/solution.py
@@ -40,24 +40,11 @@
     return swapped(value, "space", partner)
 
 
-def main_kernel(
-    piece_count, near, fields_far, cot_far, above, below, far0, far1, close0, close1, *rest
-):
-    pieces = rest[:piece_count]
-    act_far, keep, send = rest[piece_count : piece_count + 3]
-    fields, cot, act, sems, pool_l, pool_r, edges, xf, xs, xst, wc, wd, g, gd, shares = rest[piece_count + 3 :]
-    fields_in = pltpu.make_async_copy(fields_far, fields, sems.at[0])
-    cot_in = pltpu.make_async_copy(cot_far, cot, sems.at[1])
-    fields_in.start()
-    cot_in.start()
-    tiles, rows, side, chans = fields.shape
-    tall = rows + 2 * RIM
-    cells = tiles * side
+def expand_kernel(chans, *refs):
+    *pieces, wd, wc = refs
+    piece_count = len(pieces)
     fsdp_count = lax.axis_size("fsdp")
     fsdp = lax.axis_index("fsdp")
-    space = lax.axis_index("space")
-    far_odd = lax.rem(lax.div(space, 2), 2) == 1
-    close_odd = lax.rem(space, 2) == 1
     share = chans // fsdp_count
 
     lined = jnp.concatenate([p[...] for p in pieces], axis=1)
@@ -89,6 +76,29 @@
             blocks.append(jnp.zeros((8, LANES), F32))
         blocks.append(jnp.zeros((LANES - chans - 8, LANES), F32))
         wd[tap * LANES : (tap + 1) * LANES] = jnp.concatenate(blocks, axis=0).astype(BF16)
+
+
+def main_kernel(
+    near, fields_far, cot_far, above, below, far0, far1, close0, close1, wd,
+    act_far, keep, send, fields, cot, act, sems, pool_l, pool_r, edges, xf, xs, xst, g, gd, shares,
+):
+    fields_in = pltpu.make_async_copy(fields_far, fields, sems.at[0])
+    cot_in = pltpu.make_async_copy(cot_far, cot, sems.at[1])
+    fields_in.start()
+    cot_in.start()
+    tiles, rows, side, chans = fields.shape
+    tall = rows + 2 * RIM
+    cells = tiles * side
+    fsdp_count = lax.axis_size("fsdp")
+    fsdp = lax.axis_index("fsdp")
+    space = lax.axis_index("space")
+    far_odd = lax.rem(lax.div(space, 2), 2) == 1
+    close_odd = lax.rem(space, 2) == 1
+    share = chans // fsdp_count
+
+    group_count = chans // GROUP
+    group_of = lax.broadcasted_iota(jnp.int32, (GROUP, LANES), 1) // GROUP
+    taps = KS * KS
 
     zero_side = jnp.zeros((tall, RIM, LANES), F32)
     zero_slot = 4 * tiles
@@ -376,10 +386,19 @@
 
     cells = tiles * side
     part = jax.ShapeDtypeStruct((fsdp_count // 2, 2, share, HALF_SUM), F32)
+    dense = pl.pallas_call(
+        functools.partial(expand_kernel, chans),
+        out_shape=jax.ShapeDtypeStruct((taps * LANES, LANES), BF16),
+        in_specs=[VMEM] * len(pieces),
+        out_specs=VMEM,
+        scratch_shapes=[pltpu.VMEM((2 * HALF_TAPS * GROUP, LANES), F32)],
+        compiler_params=pltpu.CompilerParams(vmem_limit_bytes=16 * 1024 * 1024),
+        name="expand",
+    )(*pieces)
     activations, keep, send = pl.pallas_call(
-        functools.partial(main_kernel, len(pieces)),
+        main_kernel,
         out_shape=(jax.ShapeDtypeStruct(fields.shape, BF16), part, part),
-        in_specs=[SMEM, ANY, ANY] + [VMEM] * (6 + len(pieces)),
+        in_specs=[SMEM, ANY, ANY] + [VMEM] * 7,
         out_specs=(ANY, VMEM, VMEM),
         scratch_shapes=[
             pltpu.VMEM(fields.shape, BF16),
@@ -392,17 +411,15 @@
             pltpu.VMEM((tall, tiles, side + 16, LANES), F32),
             pltpu.VMEM((tall, cells, KS * LANES), BF16),
             pltpu.VMEM((tall, KS * XROWS, cells), BF16),
-            pltpu.VMEM((2 * HALF_TAPS * GROUP, LANES), F32),
-            pltpu.VMEM((taps * LANES, LANES), BF16),
             pltpu.VMEM((rows, cells, LANES), BF16),
             pltpu.VMEM((SUM_LANES, LANES), F32),
             pltpu.VMEM((fsdp_count, share, SUM_LANES), F32),
         ],
-        compiler_params=pltpu.CompilerParams(vmem_limit_bytes=52 * 1024 * 1024),
+        compiler_params=pltpu.CompilerParams(vmem_limit_bytes=46 * 1024 * 1024),
         name="section",
     )(
         neighbours, fields, cotangent, above, below,
-        far0, far1, close0, close1, *pieces,
+        far0, far1, close0, close1, dense,
     )
 
     held = keep + swapped(send, "fsdp", lambda i: i ^ 1)

time: 73.1 us -> 72.8 us (level)
  waiting for transfers between devices: 24.1 us -> 22.7 us
  local copies, waits for them, and re-layouts: 2.33 us -> 3.28 us
    ppermute x21, waiting for transfers between devices: 22.9 us -> 21.5 us  [swapped(): return lax.ppermute(value, axis, [p for p in pairs if 0 <= p[1] < count])]
    unnamed x8 -> x12, local copies, waits for them, and re-layouts: 1.88 us -> 2.83 us
    pallas_call x1 -> x2, Pallas kernels: 16.3 us -> 15.7 us  [the longest x1 15.1 us: per_device(): pl.pallas_call(main_kernel, out_shape=(jax.ShapeDtypeStruct(fields.shape,...]
  transfers between devices with their start and end apart: 22 -> 22, of which waited for: 11 -> 11; matrix products, arithmetic and copies ran while one was open for 1% -> 1% of each run, Pallas kernels for 0% -> 1%
where the time goes in v4:
time: 72.8 us; the launch traced here: 72.6 us
  starting transfers between devices  26.8 us (37%)
  waiting for transfers between devices  22.7 us (31%)
  Pallas kernels  17.2 us (24%)
  local copies, waits for them, and re-layouts  3.28 us (5%)
  other arithmetic  1.58 us (2%)
  between operations  0.99 us (1%)
    ppermute x21, starting transfers between devices, swapped(): return lax.ppermute(value, axis, [p for p in pairs if 0 <= p[1] < count])  24.7 us
    ppermute x21, waiting for transfers between devices, swapped(): return lax.ppermute(value, axis, [p for p in pairs if 0 <= p[1] < count])  21.5 us
    pallas_call x1, Pallas kernels, per_device(): pl.pallas_call(main_kernel, out_shape=(jax.ShapeDtypeStruct(fields.shape,...  15.1 us
    unnamed x12, local copies, waits for them, and re-layouts  2.83 us
    ppermute x1, starting transfers between devices, per_device(): lax.ppermute(squares, ('space', 'fsdp'), both)  2.02 us
  transfers between devices with their start and end apart: 22, of which 11 were waited for; matrix products, arithmetic and copies ran while one was open for 1% of the time, Pallas kernels for 1%

profile of v4, /device:TPU:0, one launch (start us, length us, event | category | flops | bytes accessed | tf_op | source)
XLA Modules:
  0.0 72.6 jit_solution(7096455932937428528)
XLA Ops:
  0.6 1.2 %copy-done = bf16[2,16,64,200]{3,2,1,0:T(8,128)(2,1)S(1)} copy-done((bf16[2,16,64,200]{3,2,1,0:T(8,128)(2,1)S(1)}, bf16[2,16,64,200]{3,2,1,0:T(8,128)(2,1)}, u32[]{:S(2)}) %copy-start) | copy-done | bytes 819224
  2.2 2.4 %collective-permute-start = (bf16[2,2,4,200]{3,2,1,0:T(4,128)(2,1)S(1)}, bf16[2,2,4,200]{3,2,1,0:T(4,128)(2,1)S(1)}, u32[]{:S(2)}, u32[]{:S(2)}) collective-permute-start(bf16[2,2,4,200]{3,2,1,0:T(4,128)(2,1)S(1)} %get-tuple-element.21), channel_id=1, source_target_pairs={{0,3},{1,2},{2,1},{3,0},{4,7},{5,6},{6,5},{7,4},{8,11},{9,10},{10,... | collective-permute-start | bytes 19208 | tf_op jit(solution)/shard_map/ppermute | solution.py:33
  5.3 0.9 %copy-done.3 = bf16[5,5,40,50]{3,2,1,0:T(8,128)(2,1)S(1)} copy-done((bf16[5,5,40,50]{3,2,1,0:T(8,128)(2,1)S(1)}, bf16[5,5,40,50]{3,2,1,0:T(8,128)(2,1)}, u32[]{:S(2)}) %copy-start.3) | copy-done | bytes 100024
  7.3 1.7 %collective-permute-start.5 = (bf16[2,2,64,200]{3,1,2,0:T(2,128)(2,1)S(1)}, bf16[2,2,64,200]{3,1,2,0:T(2,128)(2,1)S(1)}, u32[]{:S(2)}, u32[]{:S(2)}) collective-permute-start(bf16[2,2,64,200]{3,1,2,0:T(2,128)(2,1)S(1)} %copy.12), channel_id=1, source_target_pairs={{0,3},{1,2},{2,1},{3,0},{4,7},{5,6},{6,5},{7,4},{8,11},{9,10},{10,... | collective-permute-start | bytes 307208 | tf_op jit(solution)/shard_map/ppermute | solution.py:33
  9.5 1.6 %collective-permute-start.2 = (bf16[2,20,2,200]{3,2,1,0:T(2,128)(2,1)S(1)}, bf16[2,20,2,200]{3,2,1,0:T(2,128)(2,1)S(1)}, u32[]{:S(2)}, u32[]{:S(2)}) collective-permute-start(bf16[2,20,2,200]{3,2,1,0:T(2,128)(2,1)S(1)} %bitcast.62), channel_id=1, source_target_pairs={{0,8},{4,12},{8,0},{12,4},{16,24},{20,28},{24,16},{28,20},{1,9},{5... | collective-permute-start | bytes 96008 | tf_op jit(solution)/shard_map/ppermute | solution.py:33
  11.8 1.8 %collective-permute-done.2.far0 = bf16[2,20,2,200]{3,2,1,0:T(2,128)(2,1)S(1)} collective-permute-done((bf16[2,20,2,200]{3,2,1,0:T(2,128)(2,1)S(1)}, bf16[2,20,2,200]{3,2,1,0:T(2,128)(2,1)S(1)}, u32[]{:S(2)}, u32[]{:S(2)}) %collective-permute-start.2) | collective-permute-done | bytes 32032 | tf_op jit(solution)/shard_map/ppermute | solution.py:33
  14.1 1.5 %collective-permute-done.5 = bf16[2,2,64,200]{3,1,2,0:T(2,128)(2,1)S(1)} collective-permute-done((bf16[2,2,64,200]{3,1,2,0:T(2,128)(2,1)S(1)}, bf16[2,2,64,200]{3,1,2,0:T(2,128)(2,1)S(1)}, u32[]{:S(2)}, u32[]{:S(2)}) %collective-permute-start.5) | collective-permute-done | bytes 102432 | tf_op jit(solution)/shard_map/ppermute | solution.py:33
  16.1 1.6 %collective-permute-start.7 = (bf16[106,2,200]{2,1,0:T(2,128)(2,1)S(1)}, bf16[106,2,200]{2,1,0:T(2,128)(2,1)S(1)}, u32[]{:S(2)}, u32[]{:S(2)}) collective-permute-start(bf16[106,2,200]{2,1,0:T(2,128)(2,1)S(1)} %get-tuple-element.51), channel_id=1, source_target_pairs={{0,4},{4,0},{8,12},{12,8},{16,20},{20,16},{24,28},{28,24},{1,5},{5... | collective-permute-start | bytes 254408 | tf_op jit(solution)/shard_map/ppermute | solution.py:33
  19.0 2.2 %collective-permute-done.7.close0 = bf16[106,2,200]{2,1,0:T(2,128)(2,1)S(1)} collective-permute-done((bf16[106,2,200]{2,1,0:T(2,128)(2,1)S(1)}, bf16[106,2,200]{2,1,0:T(2,128)(2,1)S(1)}, u32[]{:S(2)}, u32[]{:S(2)}) %collective-permute-start.7) | collective-permute-done | bytes 84832 | tf_op jit(solution)/shard_map/ppermute | solution.py:33
  21.2 15.1 %section.1 = (bf16[2,16,64,200]{3,2,1,0:T(8,128)(2,1)}, f32[2,2,50,512]{3,2,1,0:T(8,128)S(1)}, f32[2,2,50,512]{3,2,1,0:T(8,128)S(1)}) custom-call(s32[2,8]{1,0:T(2,128)S(1)} %copy-done.4, bf16[2,16,64,200]{3,2,1,0:T(8,128)(2,1)S(1)} %copy-done.1, bf16[2,16,64,200]{3,2,1,0:T(8,128)(2,1)S(1)} %copy-done.2, bf16[2,2,64,200]{3,2,1,0:T(8,128)(2,1)S(1)} %copy.14.above, ...), custom_call_target="tpu_custom_call" | custom-call | tf_op jit(solution)/shard_map/section/pallas_call | solution.py:398
  36.4 1.8 %collective-permute-done.11 = f32[2,2,50,512]{3,2,1,0:T(8,128)S(1)} collective-permute-done((f32[2,2,50,512]{3,2,1,0:T(8,128)S(1)}, f32[2,2,50,512]{3,2,1,0:T(8,128)S(1)}, u32[]{:S(2)}, u32[]{:S(2)}) %collective-permute-start.11) | collective-permute-done | bytes 409632 | tf_op jit(solution)/shard_map/ppermute | solution.py:33
  39.0 4.9 %collective-permute-done.12 = bf16[1,2,50,512]{3,2,1,0:T(8,128)(2,1)S(1)} collective-permute-done((bf16[1,2,50,512]{3,2,1,0:T(8,128)(2,1)S(1)}, bf16[1,2,50,512]{3,2,1,0:T(8,128)(2,1)S(1)}, u32[]{:S(2)}, u32[]{:S(2)}) %collective-permute-start.12) | collective-permute-done | bytes 102432 | tf_op jit(solution)/shard_map/ppermute | solution.py:33
  43.9 5.9 %collective-permute-start.13 = (f32[50,512]{1,0:T(8,128)S(1)}, f32[50,512]{1,0:T(8,128)S(1)}, u32[]{:S(2)}, u32[]{:S(2)}) collective-permute-start(f32[50,512]{1,0:T(8,128)S(1)} %slice_bitcast_fusion.2), channel_id=1, source_target_pairs={{0,4},{4,0},{8,12},{12,8},{16,20},{20,16},{24,28},{28,24},{1,5},{5... | collective-permute-start | bytes 307208 | tf_op jit(solution)/shard_map/ppermute | solution.py:33
  49.8 2.8 %collective-permute-done.13 = f32[50,512]{1,0:T(8,128)S(1)} collective-permute-done((f32[50,512]{1,0:T(8,128)S(1)}, f32[50,512]{1,0:T(8,128)S(1)}, u32[]{:S(2)}, u32[]{:S(2)}) %collective-permute-start.13) | collective-permute-done | bytes 102432 | tf_op jit(solution)/shard_map/ppermute | solution.py:33
  52.9 3.3 %collective-permute-start.14 = (bf16[50,512]{1,0:T(8,128)(2,1)S(1)}, bf16[50,512]{1,0:T(8,128)(2,1)S(1)}, u32[]{:S(2)}, u32[]{:S(2)}) collective-permute-start(bf16[50,512]{1,0:T(8,128)(2,1)S(1)} %select_convert_fusion.1), channel_id=1, source_target_pairs={{0,8},{4,12},{8,0},{12,4},{16,24},{20,28},{24,16},{28,20},{1,9},{5... | collective-permute-start | bytes 153608 | tf_op jit(solution)/shard_map/ppermute | solution.py:33
  56.2 1.5 %collective-permute-start.15 = (bf16[50,512]{1,0:T(8,128)(2,1)S(1)}, bf16[50,512]{1,0:T(8,128)(2,1)S(1)}, u32[]{:S(2)}, u32[]{:S(2)}) collective-permute-start(bf16[50,512]{1,0:T(8,128)(2,1)S(1)} %select_convert_fusion.1), channel_id=1, source_target_pairs={{0,16},{4,20},{8,24},{12,28},{16,0},{20,4},{24,8},{28,12},{1,17},{... | collective-permute-start | bytes 153608 | tf_op jit(solution)/shard_map/ppermute | solution.py:33
  57.7 1.4 %collective-permute-start.16 = (bf16[50,512]{1,0:T(8,128)(2,1)S(1)}, bf16[50,512]{1,0:T(8,128)(2,1)S(1)}, u32[]{:S(2)}, u32[]{:S(2)}) collective-permute-start(bf16[50,512]{1,0:T(8,128)(2,1)S(1)} %select_convert_fusion.1), channel_id=1, source_target_pairs={{0,24},{4,28},{8,16},{12,20},{16,8},{20,12},{24,0},{28,4},{1,25},{... | collective-permute-start | bytes 153608 | tf_op jit(solution)/shard_map/ppermute | solution.py:33
  59.1 2.2 %collective-permute-done.15 = bf16[50,512]{1,0:T(8,128)(2,1)S(1)} collective-permute-done((bf16[50,512]{1,0:T(8,128)(2,1)S(1)}, bf16[50,512]{1,0:T(8,128)(2,1)S(1)}, u32[]{:S(2)}, u32[]{:S(2)}) %collective-permute-start.15) | collective-permute-done | bytes 51232 | tf_op jit(solution)/shard_map/ppermute | solution.py:33
  61.2 2.5 %collective-permute-done.16 = bf16[50,512]{1,0:T(8,128)(2,1)S(1)} collective-permute-done((bf16[50,512]{1,0:T(8,128)(2,1)S(1)}, bf16[50,512]{1,0:T(8,128)(2,1)S(1)}, u32[]{:S(2)}, u32[]{:S(2)}) %collective-permute-start.16) | collective-permute-done | bytes 51232 | tf_op jit(solution)/shard_map/ppermute | solution.py:33
  65.4 0.9 %collective-permute-start.19 = (f32[8,512]{1,0:T(8,128)S(1)}, f32[8,512]{1,0:T(8,128)S(1)}, u32[]{:S(2)}, u32[]{:S(2)}) collective-permute-start(f32[8,512]{1,0:T(8,128)S(1)} %broadcast_add_fusion.rest_0_), channel_id=1, source_target_pairs={{0,4},{4,0},{8,12},{12,8},{16,20},{20,16},{24,28},{28,24},{1,5},{5... | collective-permute-start | bytes 49160 | tf_op jit(solution)/shard_map/ppermute | solution.py:33
  66.8 2.0 %collective-permute-start.21 = (f32[8,512]{1,0:T(8,128)S(1)}, f32[8,512]{1,0:T(8,128)S(1)}, u32[]{:S(2)}, u32[]{:S(2)}) collective-permute-start(f32[8,512]{1,0:T(8,128)S(1)} %broadcast_add_fusion.rest_0_), channel_id=1, source_target_pairs={{0,6},{1,7},{2,4},{3,5},{4,2},{5,3},{6,0},{7,1},{8,14},{9,15},{10,... | collective-permute-start | bytes 49160 | tf_op jit(solution)/shard_map/ppermute | solution.py:461
  68.8 1.4 %collective-permute-done.19.rest_1_ = f32[8,512]{1,0:T(8,128)S(1)} collective-permute-done((f32[8,512]{1,0:T(8,128)S(1)}, f32[8,512]{1,0:T(8,128)S(1)}, u32[]{:S(2)}, u32[]{:S(2)}) %collective-permute-start.19) | collective-permute-done | bytes 16416 | tf_op jit(solution)/shard_map/ppermute | solution.py:33
  70.3 1.2 %collective-permute-done.21.rest_3_ = f32[8,512]{1,0:T(8,128)S(1)} collective-permute-done((f32[8,512]{1,0:T(8,128)S(1)}, f32[8,512]{1,0:T(8,128)S(1)}, u32[]{:S(2)}, u32[]{:S(2)}) %collective-permute-start.21) | collective-permute-done | bytes 16416 | tf_op jit(solution)/shard_map/ppermute | solution.py:461
  71.5 1.1 %scale.1 = (f32[5,5,40,50]{3,2,1,0:T(8,128)}, f32[1,50]{1,0:T(1,128)}) custom-call(f32[50,512]{1,0:T(8,128)S(1)} %get-tuple-element.44.own, f32[50,512]{1,0:T(8,128)S(1)} %collective-permute-done.17.beside, f32[8,512]{1,0:T(8,128)S(1)} %broadcast_add_fusion.rest_0_, f32[8,512]{1,0:T(8,128)S(1)} %collective-permute-done.19.rest_1_, ...), custom_call_target="tpu_custom_call" | custom-call | tf_op jit(solution)/shard_map/scale/pallas_call | solution.py:463
  (67 shorter events, 8.7 us)
Async XLA Ops:
  2.2 7.1 %collective-permute-start = (bf16[2,2,4,200]{3,2,1,0:T(4,128)(2,1)S(1)}, bf16[2,2,4,200]{3,2,1,0:T(4,128)(2,1)S(1)}, u32[]{:S(2)}, u32[]{:S(2)}) collective-permute-start(bf16[2,2,4,200]{3,2,1,0:T(4,128)(2,1)S(1)} %get-tuple-element.21), channel_id=1, source_target_pairs={{0,3},{1,2},{2,1},{3,0},{4,7},{5,6},{6,5},{7,4},{8,11},{9,10},{10,... | collective-permute-start | bytes 19208 | tf_op jit(solution)/shard_map/ppermute | solution.py:33
  4.6 4.7 %collective-permute-start.1 = (bf16[2,2,4,200]{3,2,1,0:T(4,128)(2,1)S(1)}, bf16[2,2,4,200]{3,2,1,0:T(4,128)(2,1)S(1)}, u32[]{:S(2)}, u32[]{:S(2)}) collective-permute-start(bf16[2,2,4,200]{3,2,1,0:T(4,128)(2,1)S(1)} %get-tuple-element.22), channel_id=1, source_target_pairs={{0,1},{1,0},{2,3},{3,2},{4,5},{5,4},{6,7},{7,6},{8,9},{9,8},{10,11... | collective-permute-start | bytes 19208 | tf_op jit(solution)/shard_map/ppermute | solution.py:33
  7.0 6.6 %collective-permute-start.4 = (bf16[528,128]{1,0:T(8,128)(2,1)S(1)}, bf16[528,128]{1,0:T(8,128)(2,1)S(1)}, u32[]{:S(2)}, u32[]{:S(2)}) collective-permute-start(bf16[528,128]{1,0:T(8,128)(2,1)S(1)} %pack.1.refs_0_), channel_id=1, source_target_pairs={{0,3},{1,2},{2,1},{3,0},{4,7},{5,6},{6,5},{7,4},{8,11},{9,10},{10,... | collective-permute-start | bytes 405512 | tf_op jit(solution)/shard_map/ppermute | solution.py:33
  7.2 14.1 %copy-start.2 = (bf16[2,16,64,200]{3,2,1,0:T(8,128)(2,1)S(1)}, bf16[2,16,64,200]{3,2,1,0:T(8,128)(2,1)}, u32[]{:S(2)}) copy-start(bf16[2,16,64,200]{3,2,1,0:T(8,128)(2,1)} %cot_far.1) | copy-start | bytes 2457604
  7.2 14.1 %copy-start.4 = (s32[2,8]{1,0:T(2,128)S(1)}, s32[2,8]{1,0:T(2,128)}, u32[]{:S(2)}) copy-start(s32[2,8]{1,0:T(2,128)} %near.1) | copy-start | bytes 196
  7.3 8.3 %collective-permute-start.5 = (bf16[2,2,64,200]{3,1,2,0:T(2,128)(2,1)S(1)}, bf16[2,2,64,200]{3,1,2,0:T(2,128)(2,1)S(1)}, u32[]{:S(2)}, u32[]{:S(2)}) collective-permute-start(bf16[2,2,64,200]{3,1,2,0:T(2,128)(2,1)S(1)} %copy.12), channel_id=1, source_target_pairs={{0,3},{1,2},{2,1},{3,0},{4,7},{5,6},{6,5},{7,4},{8,11},{9,10},{10,... | collective-permute-start | bytes 307208 | tf_op jit(solution)/shard_map/ppermute | solution.py:33
  9.2 6.4 %collective-permute-start.6 = (bf16[2,2,64,200]{3,1,2,0:T(2,128)(2,1)S(1)}, bf16[2,2,64,200]{3,1,2,0:T(2,128)(2,1)S(1)}, u32[]{:S(2)}, u32[]{:S(2)}) collective-permute-start(bf16[2,2,64,200]{3,1,2,0:T(2,128)(2,1)S(1)} %copy.13), channel_id=1, source_target_pairs={{0,1},{1,0},{2,3},{3,2},{4,5},{5,4},{6,7},{7,6},{8,9},{9,8},{10,11... | collective-permute-start | bytes 307208 | tf_op jit(solution)/shard_map/ppermute | solution.py:33
  9.5 4.1 %collective-permute-start.2 = (bf16[2,20,2,200]{3,2,1,0:T(2,128)(2,1)S(1)}, bf16[2,20,2,200]{3,2,1,0:T(2,128)(2,1)S(1)}, u32[]{:S(2)}, u32[]{:S(2)}) collective-permute-start(bf16[2,20,2,200]{3,2,1,0:T(2,128)(2,1)S(1)} %bitcast.62), channel_id=1, source_target_pairs={{0,8},{4,12},{8,0},{12,4},{16,24},{20,28},{24,16},{28,20},{1,9},{5... | collective-permute-start | bytes 96008 | tf_op jit(solution)/shard_map/ppermute | solution.py:33
  11.2 2.4 %collective-permute-start.3 = (bf16[2,20,2,200]{3,2,1,0:T(2,128)(2,1)S(1)}, bf16[2,20,2,200]{3,2,1,0:T(2,128)(2,1)S(1)}, u32[]{:S(2)}, u32[]{:S(2)}) collective-permute-start(bf16[2,20,2,200]{3,2,1,0:T(2,128)(2,1)S(1)} %get-tuple-element.45), channel_id=1, source_target_pairs={{8,16},{12,20},{16,8},{20,12},{9,17},{13,21},{17,9},{21,13},{10,18... | collective-permute-start | bytes 96008 | tf_op jit(solution)/shard_map/ppermute | solution.py:33
  13.6 4.8 %collective-permute-start.9 = (bf16[528,128]{1,0:T(8,128)(2,1)S(1)}, bf16[528,128]{1,0:T(8,128)(2,1)S(1)}, u32[]{:S(2)}, u32[]{:S(2)}) collective-permute-start(bf16[528,128]{1,0:T(8,128)(2,1)S(1)} %pack.1.refs_0_), channel_id=1, source_target_pairs={{0,1},{1,0},{2,3},{3,2},{4,5},{5,4},{6,7},{7,6},{8,9},{9,8},{10,11... | collective-permute-start | bytes 405512 | tf_op jit(solution)/shard_map/ppermute | solution.py:33
  13.6 4.8 %collective-permute-start.10 = (bf16[528,128]{1,0:T(8,128)(2,1)S(1)}, bf16[528,128]{1,0:T(8,128)(2,1)S(1)}, u32[]{:S(2)}, u32[]{:S(2)}) collective-permute-start(bf16[528,128]{1,0:T(8,128)(2,1)S(1)} %collective-permute-done.4.refs_1_), channel_id=1, source_target_pairs={{0,1},{1,0},{2,3},{3,2},{4,5},{5,4},{6,7},{7,6},{8,9},{9,8},{10,11... | collective-permute-start | bytes 405512 | tf_op jit(solution)/shard_map/ppermute | solution.py:33
  16.1 5.1 %collective-permute-start.7 = (bf16[106,2,200]{2,1,0:T(2,128)(2,1)S(1)}, bf16[106,2,200]{2,1,0:T(2,128)(2,1)S(1)}, u32[]{:S(2)}, u32[]{:S(2)}) collective-permute-start(bf16[106,2,200]{2,1,0:T(2,128)(2,1)S(1)} %get-tuple-element.51), channel_id=1, source_target_pairs={{0,4},{4,0},{8,12},{12,8},{16,20},{20,16},{24,28},{28,24},{1,5},{5... | collective-permute-start | bytes 254408 | tf_op jit(solution)/shard_map/ppermute | solution.py:33
  17.7 3.5 %collective-permute-start.8 = (bf16[106,2,200]{2,1,0:T(2,128)(2,1)S(1)}, bf16[106,2,200]{2,1,0:T(2,128)(2,1)S(1)}, u32[]{:S(2)}, u32[]{:S(2)}) collective-permute-start(bf16[106,2,200]{2,1,0:T(2,128)(2,1)S(1)} %get-tuple-element.50), channel_id=1, source_target_pairs={{4,8},{8,4},{12,16},{16,12},{20,24},{24,20},{5,9},{9,5},{13,17},{1... | collective-permute-start | bytes 254408 | tf_op jit(solution)/shard_map/ppermute | solution.py:33
  36.3 1.9 %collective-permute-start.11 = (f32[2,2,50,512]{3,2,1,0:T(8,128)S(1)}, f32[2,2,50,512]{3,2,1,0:T(8,128)S(1)}, u32[]{:S(2)}, u32[]{:S(2)}) collective-permute-start(f32[2,2,50,512]{3,2,1,0:T(8,128)S(1)} %get-tuple-element.36), channel_id=1, source_target_pairs={{0,1},{1,0},{2,3},{3,2},{4,5},{5,4},{6,7},{7,6},{8,9},{9,8},{10,11... | collective-permute-start | bytes 1228808 | tf_op jit(solution)/shard_map/ppermute | solution.py:33
  38.6 5.3 %collective-permute-start.12 = (bf16[1,2,50,512]{3,2,1,0:T(8,128)(2,1)S(1)}, bf16[1,2,50,512]{3,2,1,0:T(8,128)(2,1)S(1)}, u32[]{:S(2)}, u32[]{:S(2)}) collective-permute-start(bf16[1,2,50,512]{3,2,1,0:T(8,128)(2,1)S(1)} %select_convert_fusion), channel_id=1, source_target_pairs={{0,2},{1,3},{2,0},{3,1},{4,6},{5,7},{6,4},{7,5},{8,10},{9,11},{10,... | collective-permute-start | bytes 307208 | tf_op jit(solution)/shard_map/ppermute | solution.py:33
  43.9 8.7 %collective-permute-start.13 = (f32[50,512]{1,0:T(8,128)S(1)}, f32[50,512]{1,0:T(8,128)S(1)}, u32[]{:S(2)}, u32[]{:S(2)}) collective-permute-start(f32[50,512]{1,0:T(8,128)S(1)} %slice_bitcast_fusion.2), channel_id=1, source_target_pairs={{0,4},{4,0},{8,12},{12,8},{16,20},{20,16},{24,28},{28,24},{1,5},{5... | collective-permute-start | bytes 307208 | tf_op jit(solution)/shard_map/ppermute | solution.py:33
  52.9 6.2 %collective-permute-start.14 = (bf16[50,512]{1,0:T(8,128)(2,1)S(1)}, bf16[50,512]{1,0:T(8,128)(2,1)S(1)}, u32[]{:S(2)}, u32[]{:S(2)}) collective-permute-start(bf16[50,512]{1,0:T(8,128)(2,1)S(1)} %select_convert_fusion.1), channel_id=1, source_target_pairs={{0,8},{4,12},{8,0},{12,4},{16,24},{20,28},{24,16},{28,20},{1,9},{5... | collective-permute-start | bytes 153608 | tf_op jit(solution)/shard_map/ppermute | solution.py:33
  56.2 5.1 %collective-permute-start.15 = (bf16[50,512]{1,0:T(8,128)(2,1)S(1)}, bf16[50,512]{1,0:T(8,128)(2,1)S(1)}, u32[]{:S(2)}, u32[]{:S(2)}) collective-permute-start(bf16[50,512]{1,0:T(8,128)(2,1)S(1)} %select_convert_fusion.1), channel_id=1, source_target_pairs={{0,16},{4,20},{8,24},{12,28},{16,0},{20,4},{24,8},{28,12},{1,17},{... | collective-permute-start | bytes 153608 | tf_op jit(solution)/shard_map/ppermute | solution.py:33
  57.7 6.1 %collective-permute-start.16 = (bf16[50,512]{1,0:T(8,128)(2,1)S(1)}, bf16[50,512]{1,0:T(8,128)(2,1)S(1)}, u32[]{:S(2)}, u32[]{:S(2)}) collective-permute-start(bf16[50,512]{1,0:T(8,128)(2,1)S(1)} %select_convert_fusion.1), channel_id=1, source_target_pairs={{0,24},{4,28},{8,16},{12,20},{16,8},{20,12},{24,0},{28,4},{1,25},{... | collective-permute-start | bytes 153608 | tf_op jit(solution)/shard_map/ppermute | solution.py:33
  64.1 1.2 %collective-permute-start.18 = (f32[8,512]{1,0:T(8,128)S(1)}, f32[8,512]{1,0:T(8,128)S(1)}, u32[]{:S(2)}, u32[]{:S(2)}) collective-permute-start(f32[8,512]{1,0:T(8,128)S(1)} %broadcast_in_dim.69), channel_id=1, source_target_pairs={{0,1},{1,0},{2,3},{3,2},{4,5},{5,4},{6,7},{7,6},{8,9},{9,8},{10,11... | collective-permute-start | bytes 49160 | tf_op jit(solution)/shard_map/ppermute | solution.py:33
  64.2 7.3 %collective-permute-start.17 = (f32[50,512]{1,0:T(8,128)S(1)}, f32[50,512]{1,0:T(8,128)S(1)}, u32[]{:S(2)}, u32[]{:S(2)}) collective-permute-start(f32[50,512]{1,0:T(8,128)S(1)} %get-tuple-element.44.own), channel_id=1, source_target_pairs={{0,4},{4,0},{8,12},{12,8},{16,20},{20,16},{24,28},{28,24},{1,5},{5... | collective-permute-start | bytes 307208 | tf_op jit(solution)/shard_map/ppermute | solution.py:33
  65.4 4.9 %collective-permute-start.19 = (f32[8,512]{1,0:T(8,128)S(1)}, f32[8,512]{1,0:T(8,128)S(1)}, u32[]{:S(2)}, u32[]{:S(2)}) collective-permute-start(f32[8,512]{1,0:T(8,128)S(1)} %broadcast_add_fusion.rest_0_), channel_id=1, source_target_pairs={{0,4},{4,0},{8,12},{12,8},{16,20},{20,16},{24,28},{28,24},{1,5},{5... | collective-permute-start | bytes 49160 | tf_op jit(solution)/shard_map/ppermute | solution.py:33
  66.3 4.0 %collective-permute-start.20 = (f32[8,512]{1,0:T(8,128)S(1)}, f32[8,512]{1,0:T(8,128)S(1)}, u32[]{:S(2)}, u32[]{:S(2)}) collective-permute-start(f32[8,512]{1,0:T(8,128)S(1)} %broadcast_add_fusion.rest_0_), channel_id=1, source_target_pairs={{0,2},{1,3},{2,0},{3,1},{4,6},{5,7},{6,4},{7,5},{8,10},{9,11},{10,... | collective-permute-start | bytes 49160 | tf_op jit(solution)/shard_map/ppermute | solution.py:33
  66.8 4.6 %collective-permute-start.21 = (f32[8,512]{1,0:T(8,128)S(1)}, f32[8,512]{1,0:T(8,128)S(1)}, u32[]{:S(2)}, u32[]{:S(2)}) collective-permute-start(f32[8,512]{1,0:T(8,128)S(1)} %broadcast_add_fusion.rest_0_), channel_id=1, source_target_pairs={{0,6},{1,7},{2,4},{3,5},{4,2},{5,3},{6,0},{7,1},{8,14},{9,15},{10,... | collective-permute-start | bytes 49160 | tf_op jit(solution)/shard_map/ppermute | solution.py:461
  (4 other events, 16.9 us)

commit v5 on v4

--- a/solution.py
+++ b/solution.py
@@ -430,7 +430,8 @@
         sent = narrowed(pairs[:, 1], half)
         held = pairs[:, 0] + swapped(sent, "fsdp", lambda i: i ^ distance).astype(F32)
         distance *= 2
-    held = held[0, 0] + swapped(held[0, 1], "space", lambda i: i ^ 1)
+    sent = narrowed(jnp.stack([held[0, 1]]), half ^ 1)[0]
+    held = held[0, 0] + swapped(sent, "space", lambda i: i ^ 1).astype(F32)
     distance = 2
     while distance * 4 < space_count:
         held = held + swapped(held, "space", lambda i: i ^ distance)

time: 72.8 us -> 72.4 us (level)
  no operation moved by 1% of the time
where the time goes in v5:
time: 72.4 us; the launch traced here: 72.2 us
  starting transfers between devices  26.8 us (37%)
  waiting for transfers between devices  22.1 us (31%)
  Pallas kernels  17.2 us (24%)
  local copies, waits for them, and re-layouts  3.28 us (5%)
  other arithmetic  1.85 us (3%)
  between operations  1.01 us (1%)
    ppermute x21, starting transfers between devices, swapped(): return lax.ppermute(value, axis, [p for p in pairs if 0 <= p[1] < count])  24.8 us
    ppermute x21, waiting for transfers between devices, swapped(): return lax.ppermute(value, axis, [p for p in pairs if 0 <= p[1] < count])  20.9 us
    pallas_call x1, Pallas kernels, per_device(): pl.pallas_call(main_kernel, out_shape=(jax.ShapeDtypeStruct(fields.shape,...  15.1 us
    unnamed x12, local copies, waits for them, and re-layouts  2.83 us
    ppermute x1, starting transfers between devices, per_device(): lax.ppermute(squares, ('space', 'fsdp'), both)  2.03 us
  transfers between devices with their start and end apart: 22, of which 11 were waited for; matrix products, arithmetic and copies ran while one was open for 1% of the time, Pallas kernels for 1%

profile of v5, /device:TPU:0, one launch (start us, length us, event | category | flops | bytes accessed | tf_op | source)
XLA Modules:
  0.0 72.2 jit_solution(16733104293960053124)
XLA Ops:
  0.6 1.2 %copy-done = bf16[2,16,64,200]{3,2,1,0:T(8,128)(2,1)S(1)} copy-done((bf16[2,16,64,200]{3,2,1,0:T(8,128)(2,1)S(1)}, bf16[2,16,64,200]{3,2,1,0:T(8,128)(2,1)}, u32[]{:S(2)}) %copy-start) | copy-done | bytes 819224
  2.2 2.4 %collective-permute-start = (bf16[2,2,4,200]{3,2,1,0:T(4,128)(2,1)S(1)}, bf16[2,2,4,200]{3,2,1,0:T(4,128)(2,1)S(1)}, u32[]{:S(2)}, u32[]{:S(2)}) collective-permute-start(bf16[2,2,4,200]{3,2,1,0:T(4,128)(2,1)S(1)} %get-tuple-element.21), channel_id=1, source_target_pairs={{0,3},{1,2},{2,1},{3,0},{4,7},{5,6},{6,5},{7,4},{8,11},{9,10},{10,... | collective-permute-start | bytes 19208 | tf_op jit(solution)/shard_map/ppermute | solution.py:33
  5.3 0.9 %copy-done.3 = bf16[5,5,40,50]{3,2,1,0:T(8,128)(2,1)S(1)} copy-done((bf16[5,5,40,50]{3,2,1,0:T(8,128)(2,1)S(1)}, bf16[5,5,40,50]{3,2,1,0:T(8,128)(2,1)}, u32[]{:S(2)}) %copy-start.3) | copy-done | bytes 100024
  7.3 1.7 %collective-permute-start.5 = (bf16[2,2,64,200]{3,1,2,0:T(2,128)(2,1)S(1)}, bf16[2,2,64,200]{3,1,2,0:T(2,128)(2,1)S(1)}, u32[]{:S(2)}, u32[]{:S(2)}) collective-permute-start(bf16[2,2,64,200]{3,1,2,0:T(2,128)(2,1)S(1)} %copy.12), channel_id=1, source_target_pairs={{0,3},{1,2},{2,1},{3,0},{4,7},{5,6},{6,5},{7,4},{8,11},{9,10},{10,... | collective-permute-start | bytes 307208 | tf_op jit(solution)/shard_map/ppermute | solution.py:33
  9.5 1.6 %collective-permute-start.2 = (bf16[2,20,2,200]{3,2,1,0:T(2,128)(2,1)S(1)}, bf16[2,20,2,200]{3,2,1,0:T(2,128)(2,1)S(1)}, u32[]{:S(2)}, u32[]{:S(2)}) collective-permute-start(bf16[2,20,2,200]{3,2,1,0:T(2,128)(2,1)S(1)} %bitcast.68), channel_id=1, source_target_pairs={{0,8},{4,12},{8,0},{12,4},{16,24},{20,28},{24,16},{28,20},{1,9},{5... | collective-permute-start | bytes 96008 | tf_op jit(solution)/shard_map/ppermute | solution.py:33
  11.8 1.8 %collective-permute-done.2.far0 = bf16[2,20,2,200]{3,2,1,0:T(2,128)(2,1)S(1)} collective-permute-done((bf16[2,20,2,200]{3,2,1,0:T(2,128)(2,1)S(1)}, bf16[2,20,2,200]{3,2,1,0:T(2,128)(2,1)S(1)}, u32[]{:S(2)}, u32[]{:S(2)}) %collective-permute-start.2) | collective-permute-done | bytes 32032 | tf_op jit(solution)/shard_map/ppermute | solution.py:33
  14.1 1.5 %collective-permute-done.5 = bf16[2,2,64,200]{3,1,2,0:T(2,128)(2,1)S(1)} collective-permute-done((bf16[2,2,64,200]{3,1,2,0:T(2,128)(2,1)S(1)}, bf16[2,2,64,200]{3,1,2,0:T(2,128)(2,1)S(1)}, u32[]{:S(2)}, u32[]{:S(2)}) %collective-permute-start.5) | collective-permute-done | bytes 102432 | tf_op jit(solution)/shard_map/ppermute | solution.py:33
  16.1 1.6 %collective-permute-start.7 = (bf16[106,2,200]{2,1,0:T(2,128)(2,1)S(1)}, bf16[106,2,200]{2,1,0:T(2,128)(2,1)S(1)}, u32[]{:S(2)}, u32[]{:S(2)}) collective-permute-start(bf16[106,2,200]{2,1,0:T(2,128)(2,1)S(1)} %get-tuple-element.53), channel_id=1, source_target_pairs={{0,4},{4,0},{8,12},{12,8},{16,20},{20,16},{24,28},{28,24},{1,5},{5... | collective-permute-start | bytes 254408 | tf_op jit(solution)/shard_map/ppermute | solution.py:33
  19.0 2.2 %collective-permute-done.7.close0 = bf16[106,2,200]{2,1,0:T(2,128)(2,1)S(1)} collective-permute-done((bf16[106,2,200]{2,1,0:T(2,128)(2,1)S(1)}, bf16[106,2,200]{2,1,0:T(2,128)(2,1)S(1)}, u32[]{:S(2)}, u32[]{:S(2)}) %collective-permute-start.7) | collective-permute-done | bytes 84832 | tf_op jit(solution)/shard_map/ppermute | solution.py:33
  21.2 15.1 %section.1 = (bf16[2,16,64,200]{3,2,1,0:T(8,128)(2,1)}, f32[2,2,50,512]{3,2,1,0:T(8,128)S(1)}, f32[2,2,50,512]{3,2,1,0:T(8,128)S(1)}) custom-call(s32[2,8]{1,0:T(2,128)S(1)} %copy-done.4, bf16[2,16,64,200]{3,2,1,0:T(8,128)(2,1)S(1)} %copy-done.1, bf16[2,16,64,200]{3,2,1,0:T(8,128)(2,1)S(1)} %copy-done.2, bf16[2,2,64,200]{3,2,1,0:T(8,128)(2,1)S(1)} %copy.14.above, ...), custom_call_target="tpu_custom_call" | custom-call | tf_op jit(solution)/shard_map/section/pallas_call | solution.py:398
  36.4 1.8 %collective-permute-done.11 = f32[2,2,50,512]{3,2,1,0:T(8,128)S(1)} collective-permute-done((f32[2,2,50,512]{3,2,1,0:T(8,128)S(1)}, f32[2,2,50,512]{3,2,1,0:T(8,128)S(1)}, u32[]{:S(2)}, u32[]{:S(2)}) %collective-permute-start.11) | collective-permute-done | bytes 409632 | tf_op jit(solution)/shard_map/ppermute | solution.py:33
  39.0 4.9 %collective-permute-done.12 = bf16[1,2,50,512]{3,2,1,0:T(8,128)(2,1)S(1)} collective-permute-done((bf16[1,2,50,512]{3,2,1,0:T(8,128)(2,1)S(1)}, bf16[1,2,50,512]{3,2,1,0:T(8,128)(2,1)S(1)}, u32[]{:S(2)}, u32[]{:S(2)}) %collective-permute-start.12) | collective-permute-done | bytes 102432 | tf_op jit(solution)/shard_map/ppermute | solution.py:33
  44.2 5.9 %collective-permute-start.13 = (bf16[50,512]{1,0:T(8,128)(2,1)S(1)}, bf16[50,512]{1,0:T(8,128)(2,1)S(1)}, u32[]{:S(2)}, u32[]{:S(2)}) collective-permute-start(bf16[50,512]{1,0:T(8,128)(2,1)S(1)} %fusion.3), channel_id=1, source_target_pairs={{0,4},{4,0},{8,12},{12,8},{16,20},{20,16},{24,28},{28,24},{1,5},{5... | collective-permute-start | bytes 153608 | tf_op jit(solution)/shard_map/ppermute | solution.py:33
  50.1 2.2 %collective-permute-done.13 = bf16[50,512]{1,0:T(8,128)(2,1)S(1)} collective-permute-done((bf16[50,512]{1,0:T(8,128)(2,1)S(1)}, bf16[50,512]{1,0:T(8,128)(2,1)S(1)}, u32[]{:S(2)}, u32[]{:S(2)}) %collective-permute-start.13) | collective-permute-done | bytes 51232 | tf_op jit(solution)/shard_map/ppermute | solution.py:33
  52.6 3.3 %collective-permute-start.14 = (bf16[50,512]{1,0:T(8,128)(2,1)S(1)}, bf16[50,512]{1,0:T(8,128)(2,1)S(1)}, u32[]{:S(2)}, u32[]{:S(2)}) collective-permute-start(bf16[50,512]{1,0:T(8,128)(2,1)S(1)} %select_convert_fusion.1), channel_id=1, source_target_pairs={{0,8},{4,12},{8,0},{12,4},{16,24},{20,28},{24,16},{28,20},{1,9},{5... | collective-permute-start | bytes 153608 | tf_op jit(solution)/shard_map/ppermute | solution.py:33
  55.8 1.5 %collective-permute-start.15 = (bf16[50,512]{1,0:T(8,128)(2,1)S(1)}, bf16[50,512]{1,0:T(8,128)(2,1)S(1)}, u32[]{:S(2)}, u32[]{:S(2)}) collective-permute-start(bf16[50,512]{1,0:T(8,128)(2,1)S(1)} %select_convert_fusion.1), channel_id=1, source_target_pairs={{0,16},{4,20},{8,24},{12,28},{16,0},{20,4},{24,8},{28,12},{1,17},{... | collective-permute-start | bytes 153608 | tf_op jit(solution)/shard_map/ppermute | solution.py:33
  57.3 1.4 %collective-permute-start.16 = (bf16[50,512]{1,0:T(8,128)(2,1)S(1)}, bf16[50,512]{1,0:T(8,128)(2,1)S(1)}, u32[]{:S(2)}, u32[]{:S(2)}) collective-permute-start(bf16[50,512]{1,0:T(8,128)(2,1)S(1)} %select_convert_fusion.1), channel_id=1, source_target_pairs={{0,24},{4,28},{8,16},{12,20},{16,8},{20,12},{24,0},{28,4},{1,25},{... | collective-permute-start | bytes 153608 | tf_op jit(solution)/shard_map/ppermute | solution.py:33
  58.7 2.2 %collective-permute-done.15 = bf16[50,512]{1,0:T(8,128)(2,1)S(1)} collective-permute-done((bf16[50,512]{1,0:T(8,128)(2,1)S(1)}, bf16[50,512]{1,0:T(8,128)(2,1)S(1)}, u32[]{:S(2)}, u32[]{:S(2)}) %collective-permute-start.15) | collective-permute-done | bytes 51232 | tf_op jit(solution)/shard_map/ppermute | solution.py:33
  60.9 2.5 %collective-permute-done.16 = bf16[50,512]{1,0:T(8,128)(2,1)S(1)} collective-permute-done((bf16[50,512]{1,0:T(8,128)(2,1)S(1)}, bf16[50,512]{1,0:T(8,128)(2,1)S(1)}, u32[]{:S(2)}, u32[]{:S(2)}) %collective-permute-start.16) | collective-permute-done | bytes 51232 | tf_op jit(solution)/shard_map/ppermute | solution.py:33
  65.0 0.9 %collective-permute-start.19 = (f32[8,512]{1,0:T(8,128)S(1)}, f32[8,512]{1,0:T(8,128)S(1)}, u32[]{:S(2)}, u32[]{:S(2)}) collective-permute-start(f32[8,512]{1,0:T(8,128)S(1)} %broadcast_add_fusion.rest_0_), channel_id=1, source_target_pairs={{0,4},{4,0},{8,12},{12,8},{16,20},{20,16},{24,28},{28,24},{1,5},{5... | collective-permute-start | bytes 49160 | tf_op jit(solution)/shard_map/ppermute | solution.py:33
  66.5 2.0 %collective-permute-start.21 = (f32[8,512]{1,0:T(8,128)S(1)}, f32[8,512]{1,0:T(8,128)S(1)}, u32[]{:S(2)}, u32[]{:S(2)}) collective-permute-start(f32[8,512]{1,0:T(8,128)S(1)} %broadcast_add_fusion.rest_0_), channel_id=1, source_target_pairs={{0,6},{1,7},{2,4},{3,5},{4,2},{5,3},{6,0},{7,1},{8,14},{9,15},{10,... | collective-permute-start | bytes 49160 | tf_op jit(solution)/shard_map/ppermute | solution.py:462
  68.5 1.4 %collective-permute-done.19.rest_1_ = f32[8,512]{1,0:T(8,128)S(1)} collective-permute-done((f32[8,512]{1,0:T(8,128)S(1)}, f32[8,512]{1,0:T(8,128)S(1)}, u32[]{:S(2)}, u32[]{:S(2)}) %collective-permute-start.19) | collective-permute-done | bytes 16416 | tf_op jit(solution)/shard_map/ppermute | solution.py:33
  69.9 1.2 %collective-permute-done.21.rest_3_ = f32[8,512]{1,0:T(8,128)S(1)} collective-permute-done((f32[8,512]{1,0:T(8,128)S(1)}, f32[8,512]{1,0:T(8,128)S(1)}, u32[]{:S(2)}, u32[]{:S(2)}) %collective-permute-start.21) | collective-permute-done | bytes 16416 | tf_op jit(solution)/shard_map/ppermute | solution.py:462
  71.1 1.1 %scale.1 = (f32[5,5,40,50]{3,2,1,0:T(8,128)}, f32[1,50]{1,0:T(1,128)}) custom-call(f32[50,512]{1,0:T(8,128)S(1)} %get-tuple-element.46.own, f32[50,512]{1,0:T(8,128)S(1)} %collective-permute-done.17.beside, f32[8,512]{1,0:T(8,128)S(1)} %broadcast_add_fusion.rest_0_, f32[8,512]{1,0:T(8,128)S(1)} %collective-permute-done.19.rest_1_, ...), custom_call_target="tpu_custom_call" | custom-call | tf_op jit(solution)/shard_map/scale/pallas_call | solution.py:464
  (70 shorter events, 9.0 us)
Async XLA Ops:
  2.2 7.1 %collective-permute-start = (bf16[2,2,4,200]{3,2,1,0:T(4,128)(2,1)S(1)}, bf16[2,2,4,200]{3,2,1,0:T(4,128)(2,1)S(1)}, u32[]{:S(2)}, u32[]{:S(2)}) collective-permute-start(bf16[2,2,4,200]{3,2,1,0:T(4,128)(2,1)S(1)} %get-tuple-element.21), channel_id=1, source_target_pairs={{0,3},{1,2},{2,1},{3,0},{4,7},{5,6},{6,5},{7,4},{8,11},{9,10},{10,... | collective-permute-start | bytes 19208 | tf_op jit(solution)/shard_map/ppermute | solution.py:33
  4.6 4.7 %collective-permute-start.1 = (bf16[2,2,4,200]{3,2,1,0:T(4,128)(2,1)S(1)}, bf16[2,2,4,200]{3,2,1,0:T(4,128)(2,1)S(1)}, u32[]{:S(2)}, u32[]{:S(2)}) collective-permute-start(bf16[2,2,4,200]{3,2,1,0:T(4,128)(2,1)S(1)} %get-tuple-element.22), channel_id=1, source_target_pairs={{0,1},{1,0},{2,3},{3,2},{4,5},{5,4},{6,7},{7,6},{8,9},{9,8},{10,11... | collective-permute-start | bytes 19208 | tf_op jit(solution)/shard_map/ppermute | solution.py:33
  7.0 6.6 %collective-permute-start.4 = (bf16[528,128]{1,0:T(8,128)(2,1)S(1)}, bf16[528,128]{1,0:T(8,128)(2,1)S(1)}, u32[]{:S(2)}, u32[]{:S(2)}) collective-permute-start(bf16[528,128]{1,0:T(8,128)(2,1)S(1)} %pack.1.refs_0_), channel_id=1, source_target_pairs={{0,3},{1,2},{2,1},{3,0},{4,7},{5,6},{6,5},{7,4},{8,11},{9,10},{10,... | collective-permute-start | bytes 405512 | tf_op jit(solution)/shard_map/ppermute | solution.py:33
  7.2 14.1 %copy-start.2 = (bf16[2,16,64,200]{3,2,1,0:T(8,128)(2,1)S(1)}, bf16[2,16,64,200]{3,2,1,0:T(8,128)(2,1)}, u32[]{:S(2)}) copy-start(bf16[2,16,64,200]{3,2,1,0:T(8,128)(2,1)} %cot_far.1) | copy-start | bytes 2457604
  7.2 14.1 %copy-start.4 = (s32[2,8]{1,0:T(2,128)S(1)}, s32[2,8]{1,0:T(2,128)}, u32[]{:S(2)}) copy-start(s32[2,8]{1,0:T(2,128)} %near.1) | copy-start | bytes 196
  7.3 8.3 %collective-permute-start.5 = (bf16[2,2,64,200]{3,1,2,0:T(2,128)(2,1)S(1)}, bf16[2,2,64,200]{3,1,2,0:T(2,128)(2,1)S(1)}, u32[]{:S(2)}, u32[]{:S(2)}) collective-permute-start(bf16[2,2,64,200]{3,1,2,0:T(2,128)(2,1)S(1)} %copy.12), channel_id=1, source_target_pairs={{0,3},{1,2},{2,1},{3,0},{4,7},{5,6},{6,5},{7,4},{8,11},{9,10},{10,... | collective-permute-start | bytes 307208 | tf_op jit(solution)/shard_map/ppermute | solution.py:33
  9.2 6.4 %collective-permute-start.6 = (bf16[2,2,64,200]{3,1,2,0:T(2,128)(2,1)S(1)}, bf16[2,2,64,200]{3,1,2,0:T(2,128)(2,1)S(1)}, u32[]{:S(2)}, u32[]{:S(2)}) collective-permute-start(bf16[2,2,64,200]{3,1,2,0:T(2,128)(2,1)S(1)} %copy.13), channel_id=1, source_target_pairs={{0,1},{1,0},{2,3},{3,2},{4,5},{5,4},{6,7},{7,6},{8,9},{9,8},{10,11... | collective-permute-start | bytes 307208 | tf_op jit(solution)/shard_map/ppermute | solution.py:33
  9.5 4.1 %collective-permute-start.2 = (bf16[2,20,2,200]{3,2,1,0:T(2,128)(2,1)S(1)}, bf16[2,20,2,200]{3,2,1,0:T(2,128)(2,1)S(1)}, u32[]{:S(2)}, u32[]{:S(2)}) collective-permute-start(bf16[2,20,2,200]{3,2,1,0:T(2,128)(2,1)S(1)} %bitcast.68), channel_id=1, source_target_pairs={{0,8},{4,12},{8,0},{12,4},{16,24},{20,28},{24,16},{28,20},{1,9},{5... | collective-permute-start | bytes 96008 | tf_op jit(solution)/shard_map/ppermute | solution.py:33
  11.2 2.4 %collective-permute-start.3 = (bf16[2,20,2,200]{3,2,1,0:T(2,128)(2,1)S(1)}, bf16[2,20,2,200]{3,2,1,0:T(2,128)(2,1)S(1)}, u32[]{:S(2)}, u32[]{:S(2)}) collective-permute-start(bf16[2,20,2,200]{3,2,1,0:T(2,128)(2,1)S(1)} %get-tuple-element.47), channel_id=1, source_target_pairs={{8,16},{12,20},{16,8},{20,12},{9,17},{13,21},{17,9},{21,13},{10,18... | collective-permute-start | bytes 96008 | tf_op jit(solution)/shard_map/ppermute | solution.py:33
  13.6 4.8 %collective-permute-start.9 = (bf16[528,128]{1,0:T(8,128)(2,1)S(1)}, bf16[528,128]{1,0:T(8,128)(2,1)S(1)}, u32[]{:S(2)}, u32[]{:S(2)}) collective-permute-start(bf16[528,128]{1,0:T(8,128)(2,1)S(1)} %pack.1.refs_0_), channel_id=1, source_target_pairs={{0,1},{1,0},{2,3},{3,2},{4,5},{5,4},{6,7},{7,6},{8,9},{9,8},{10,11... | collective-permute-start | bytes 405512 | tf_op jit(solution)/shard_map/ppermute | solution.py:33
  13.6 4.8 %collective-permute-start.10 = (bf16[528,128]{1,0:T(8,128)(2,1)S(1)}, bf16[528,128]{1,0:T(8,128)(2,1)S(1)}, u32[]{:S(2)}, u32[]{:S(2)}) collective-permute-start(bf16[528,128]{1,0:T(8,128)(2,1)S(1)} %collective-permute-done.4.refs_1_), channel_id=1, source_target_pairs={{0,1},{1,0},{2,3},{3,2},{4,5},{5,4},{6,7},{7,6},{8,9},{9,8},{10,11... | collective-permute-start | bytes 405512 | tf_op jit(solution)/shard_map/ppermute | solution.py:33
  16.1 5.1 %collective-permute-start.7 = (bf16[106,2,200]{2,1,0:T(2,128)(2,1)S(1)}, bf16[106,2,200]{2,1,0:T(2,128)(2,1)S(1)}, u32[]{:S(2)}, u32[]{:S(2)}) collective-permute-start(bf16[106,2,200]{2,1,0:T(2,128)(2,1)S(1)} %get-tuple-element.53), channel_id=1, source_target_pairs={{0,4},{4,0},{8,12},{12,8},{16,20},{20,16},{24,28},{28,24},{1,5},{5... | collective-permute-start | bytes 254408 | tf_op jit(solution)/shard_map/ppermute | solution.py:33
  17.7 3.5 %collective-permute-start.8 = (bf16[106,2,200]{2,1,0:T(2,128)(2,1)S(1)}, bf16[106,2,200]{2,1,0:T(2,128)(2,1)S(1)}, u32[]{:S(2)}, u32[]{:S(2)}) collective-permute-start(bf16[106,2,200]{2,1,0:T(2,128)(2,1)S(1)} %get-tuple-element.52), channel_id=1, source_target_pairs={{4,8},{8,4},{12,16},{16,12},{20,24},{24,20},{5,9},{9,5},{13,17},{1... | collective-permute-start | bytes 254408 | tf_op jit(solution)/shard_map/ppermute | solution.py:33
  36.3 1.9 %collective-permute-start.11 = (f32[2,2,50,512]{3,2,1,0:T(8,128)S(1)}, f32[2,2,50,512]{3,2,1,0:T(8,128)S(1)}, u32[]{:S(2)}, u32[]{:S(2)}) collective-permute-start(f32[2,2,50,512]{3,2,1,0:T(8,128)S(1)} %get-tuple-element.36), channel_id=1, source_target_pairs={{0,1},{1,0},{2,3},{3,2},{4,5},{5,4},{6,7},{7,6},{8,9},{9,8},{10,11... | collective-permute-start | bytes 1228808 | tf_op jit(solution)/shard_map/ppermute | solution.py:33
  38.6 5.3 %collective-permute-start.12 = (bf16[1,2,50,512]{3,2,1,0:T(8,128)(2,1)S(1)}, bf16[1,2,50,512]{3,2,1,0:T(8,128)(2,1)S(1)}, u32[]{:S(2)}, u32[]{:S(2)}) collective-permute-start(bf16[1,2,50,512]{3,2,1,0:T(8,128)(2,1)S(1)} %select_convert_fusion), channel_id=1, source_target_pairs={{0,2},{1,3},{2,0},{3,1},{4,6},{5,7},{6,4},{7,5},{8,10},{9,11},{10,... | collective-permute-start | bytes 307208 | tf_op jit(solution)/shard_map/ppermute | solution.py:33
  44.2 8.1 %collective-permute-start.13 = (bf16[50,512]{1,0:T(8,128)(2,1)S(1)}, bf16[50,512]{1,0:T(8,128)(2,1)S(1)}, u32[]{:S(2)}, u32[]{:S(2)}) collective-permute-start(bf16[50,512]{1,0:T(8,128)(2,1)S(1)} %fusion.3), channel_id=1, source_target_pairs={{0,4},{4,0},{8,12},{12,8},{16,20},{20,16},{24,28},{28,24},{1,5},{5... | collective-permute-start | bytes 153608 | tf_op jit(solution)/shard_map/ppermute | solution.py:33
  52.6 6.2 %collective-permute-start.14 = (bf16[50,512]{1,0:T(8,128)(2,1)S(1)}, bf16[50,512]{1,0:T(8,128)(2,1)S(1)}, u32[]{:S(2)}, u32[]{:S(2)}) collective-permute-start(bf16[50,512]{1,0:T(8,128)(2,1)S(1)} %select_convert_fusion.1), channel_id=1, source_target_pairs={{0,8},{4,12},{8,0},{12,4},{16,24},{20,28},{24,16},{28,20},{1,9},{5... | collective-permute-start | bytes 153608 | tf_op jit(solution)/shard_map/ppermute | solution.py:33
  55.8 5.1 %collective-permute-start.15 = (bf16[50,512]{1,0:T(8,128)(2,1)S(1)}, bf16[50,512]{1,0:T(8,128)(2,1)S(1)}, u32[]{:S(2)}, u32[]{:S(2)}) collective-permute-start(bf16[50,512]{1,0:T(8,128)(2,1)S(1)} %select_convert_fusion.1), channel_id=1, source_target_pairs={{0,16},{4,20},{8,24},{12,28},{16,0},{20,4},{24,8},{28,12},{1,17},{... | collective-permute-start | bytes 153608 | tf_op jit(solution)/shard_map/ppermute | solution.py:33
  57.3 6.1 %collective-permute-start.16 = (bf16[50,512]{1,0:T(8,128)(2,1)S(1)}, bf16[50,512]{1,0:T(8,128)(2,1)S(1)}, u32[]{:S(2)}, u32[]{:S(2)}) collective-permute-start(bf16[50,512]{1,0:T(8,128)(2,1)S(1)} %select_convert_fusion.1), channel_id=1, source_target_pairs={{0,24},{4,28},{8,16},{12,20},{16,8},{20,12},{24,0},{28,4},{1,25},{... | collective-permute-start | bytes 153608 | tf_op jit(solution)/shard_map/ppermute | solution.py:33
  63.8 1.2 %collective-permute-start.18 = (f32[8,512]{1,0:T(8,128)S(1)}, f32[8,512]{1,0:T(8,128)S(1)}, u32[]{:S(2)}, u32[]{:S(2)}) collective-permute-start(f32[8,512]{1,0:T(8,128)S(1)} %broadcast_in_dim.87), channel_id=1, source_target_pairs={{0,1},{1,0},{2,3},{3,2},{4,5},{5,4},{6,7},{7,6},{8,9},{9,8},{10,11... | collective-permute-start | bytes 49160 | tf_op jit(solution)/shard_map/ppermute | solution.py:33
  63.8 7.3 %collective-permute-start.17 = (f32[50,512]{1,0:T(8,128)S(1)}, f32[50,512]{1,0:T(8,128)S(1)}, u32[]{:S(2)}, u32[]{:S(2)}) collective-permute-start(f32[50,512]{1,0:T(8,128)S(1)} %get-tuple-element.46.own), channel_id=1, source_target_pairs={{0,4},{4,0},{8,12},{12,8},{16,20},{20,16},{24,28},{28,24},{1,5},{5... | collective-permute-start | bytes 307208 | tf_op jit(solution)/shard_map/ppermute | solution.py:33
  65.0 4.9 %collective-permute-start.19 = (f32[8,512]{1,0:T(8,128)S(1)}, f32[8,512]{1,0:T(8,128)S(1)}, u32[]{:S(2)}, u32[]{:S(2)}) collective-permute-start(f32[8,512]{1,0:T(8,128)S(1)} %broadcast_add_fusion.rest_0_), channel_id=1, source_target_pairs={{0,4},{4,0},{8,12},{12,8},{16,20},{20,16},{24,28},{28,24},{1,5},{5... | collective-permute-start | bytes 49160 | tf_op jit(solution)/shard_map/ppermute | solution.py:33
  65.9 4.0 %collective-permute-start.20 = (f32[8,512]{1,0:T(8,128)S(1)}, f32[8,512]{1,0:T(8,128)S(1)}, u32[]{:S(2)}, u32[]{:S(2)}) collective-permute-start(f32[8,512]{1,0:T(8,128)S(1)} %broadcast_add_fusion.rest_0_), channel_id=1, source_target_pairs={{0,2},{1,3},{2,0},{3,1},{4,6},{5,7},{6,4},{7,5},{8,10},{9,11},{10,... | collective-permute-start | bytes 49160 | tf_op jit(solution)/shard_map/ppermute | solution.py:33
  66.5 4.6 %collective-permute-start.21 = (f32[8,512]{1,0:T(8,128)S(1)}, f32[8,512]{1,0:T(8,128)S(1)}, u32[]{:S(2)}, u32[]{:S(2)}) collective-permute-start(f32[8,512]{1,0:T(8,128)S(1)} %broadcast_add_fusion.rest_0_), channel_id=1, source_target_pairs={{0,6},{1,7},{2,4},{3,5},{4,2},{5,3},{6,0},{7,1},{8,14},{9,15},{10,... | collective-permute-start | bytes 49160 | tf_op jit(solution)/shard_map/ppermute | solution.py:462
  (4 other events, 16.9 us)
